TPU v7x, 32 devices: a whole 2x2x4 slice. The times are simulated.
32 devices in a mesh: dp: 4 (over z), ctx: 4 (over y, x), tensor: 2 (over core).
Axes of the slice: x: 2, y: 2, z: 4, core: 2. Of those that a mesh axis runs over, the one named last changes fastest.
Arguments:
- tokens: bfloat16 [32, 1024, 1024], P('dp', 'ctx'), may hold values from -6 to 6
- norm_gain: bfloat16 [1024], P(('dp', 'ctx')), may hold values from 0.5 to 1.5
- w_zx: bfloat16 [1024, 2, 2048], P(('dp', 'ctx'), None, 'tensor'), may hold values from -0.1875 to 0.1875
- w_dt: bfloat16 [1024, 32], P(('dp', 'ctx'), 'tensor'), may hold values from -0.1875 to 0.1875
- w_bc: bfloat16 [1024, 256], P(('dp', 'ctx')), may hold values from -0.1875 to 0.1875
- conv_x_w: float32 [4, 2048], P(None, 'tensor'), may hold values from -3 to 3
- conv_x_b: float32 [2048], P('tensor'), may hold values from -0.5 to 0.5
- conv_bc_w: float32 [4, 256], replicated, may hold values from -3 to 3
- conv_bc_b: float32 [256], replicated, may hold values from -0.5 to 0.5
- dt_bias: float32 [32], P('tensor'), may hold values from -4 to -1
- a_log: float32 [32], P('tensor'), may hold values from -6.9 to -0.7
- d_skip: float32 [32], P('tensor'), may hold values from 0.5 to 1.5
- norm_w: float32 [2048], P('tensor'), may hold values from 0.5 to 1.5
- w_out: bfloat16 [1024, 2048], P(('dp', 'ctx'), 'tensor'), may hold values from -0.125 to 0.125
- output_gradient: bfloat16 [32, 1024, 1024], P('dp', 'ctx'), may hold values from -6 to 6
Outputs:
- mixed_out: bfloat16 [32, 1024, 1024], P('dp', 'ctx')
- grad_tokens: float32 [32, 1024, 1024], P('dp', 'ctx')
- grad_norm_gain: float32 [1024], P(('dp', 'ctx'))
- grad_w_zx: float32 [1024, 2, 2048], P(('dp', 'ctx'), None, 'tensor')
- grad_w_dt: float32 [1024, 32], P(('dp', 'ctx'), 'tensor')
- grad_w_bc: float32 [1024, 256], P(('dp', 'ctx'))
- grad_conv_x_w: float32 [4, 2048], P(None, 'tensor')
- grad_conv_x_b: float32 [2048], P('tensor')
- grad_conv_bc_w: float32 [4, 256], replicated
- grad_conv_bc_b: float32 [256], replicated
- grad_dt_bias: float32 [32], P('tensor')
- grad_a_log: float32 [32], P('tensor')
- grad_d_skip: float32 [32], P('tensor')
- grad_norm_w: float32 [2048], P('tensor')
- grad_w_out: float32 [1024, 2048], P(('dp', 'ctx'), 'tensor')
All inputs are finite; a program needn't handle non-finite values.
Results may differ from a plain program's by a relative error of at most 0.012.
The roundings to bfloat16 on the way count: a program that leaves them out, or rounds other values in their place, can miss the bound.
Values may be sent and summed in bfloat16 or wider, within the bound.
No kernel may reach another device: no remote copies, remote signals or barrier semaphores. Data moves between devices by JAX's collectives and lax.ppermute only.
A program may use at most 256 MiB of HBM per device.

v0:
```python
from functools import partial

import jax
import jax.numpy as jnp
from jax import lax
from jax.sharding import PartitionSpec as P

SPAN = 256


EPS = 1e-05
HIGH = lax.Precision.HIGHEST


def shifted(block, axis, distance):
    devices = range(lax.axis_size(axis))
    route = [(i - distance, i) for i in devices if i - distance in devices]
    return lax.ppermute(block, axis, route)


def carried_in(part, axis, combine, identity, reverse):
    count = lax.axis_size(axis)
    place = lax.axis_index(axis)
    ahead = count - 1 - place if reverse else place
    gathered = jax.tree.map(lambda a: lax.all_gather(a, axis), part)
    state = jax.tree.map(lambda a, e: jnp.zeros_like(a) + jnp.asarray(e, a.dtype), part, identity)

    def one(hop, state):
        source = count - 1 - hop if reverse else hop
        return combine(
            state, jax.tree.map(lambda a: lax.dynamic_index_in_dim(a, source, 0, False), gathered)
        )

    return lax.fori_loop(0, ahead, one, state)


def block_step(memory, inputs, a_decay):
    values, step_size, input_map, output_map = inputs
    length = values.shape[0]
    decay_sum = jnp.cumsum(step_size * a_decay[None, :], axis=0)
    positions = jnp.arange(length)
    causal = (positions[:, None] >= positions[None, :])[:, :, None]
    spread = jnp.where(causal, decay_sum[:, None, :] - decay_sum[None, :, :], -jnp.inf)
    scores = jnp.dot(output_map, input_map.T, precision=HIGH)
    weights = jnp.exp(spread) * scores[:, :, None]
    scaled = values * step_size[:, :, None]
    inside = jnp.einsum("tsh,shp->thp", weights, scaled, precision=HIGH)
    from_memory = jnp.exp(decay_sum)[:, :, None] * jnp.einsum(
        "hpn,tn->thp", memory, output_map, precision=HIGH
    )
    closing = decay_sum[-1]
    remaining = jnp.exp(closing[None, :] - decay_sum)
    new_memory = jnp.exp(closing)[:, None, None] * memory + jnp.einsum(
        "shp,sn->hpn", remaining[:, :, None] * scaled, input_map, precision=HIGH
    )
    return (new_memory, inside + from_memory)


def part_scan(values, step_size, input_map, output_map, a_decay):
    blocks = values.shape[0] // SPAN

    def advance(memory, inputs):
        return jax.checkpoint(block_step)(memory, inputs, a_decay)

    def blocked(stacked):
        return stacked.reshape((blocks, SPAN) + stacked.shape[1:])

    initial = jnp.zeros((values.shape[1], values.shape[2], input_map.shape[1]), jnp.float32)
    final_memory, outputs = lax.scan(
        advance,
        initial,
        (blocked(values), blocked(step_size), blocked(input_map), blocked(output_map)),
    )
    decay_sum = jnp.cumsum(step_size * a_decay[None, :], axis=0)
    return (outputs.reshape(values.shape), final_memory, decay_sum)


def causal_edge(extended, weight, bias):
    conv_taps = weight.shape[0]
    length = extended.shape[1] - conv_taps + 1
    return bias + sum(
        (extended[:, offset : offset + length] * weight[offset] for offset in range(conv_taps))
    )


def local_core(inner_ext, bc_ext, unmixed_timestep, params, head_size):
    conv_x_w, conv_x_b, conv_bc_w, conv_bc_b, dt_bias, a_log, d_skip = params
    seqs_here, length, heads_here = unmixed_timestep.shape
    values = jax.nn.silu(causal_edge(inner_ext, conv_x_w, conv_x_b)).reshape(
        seqs_here, length, heads_here, head_size
    )
    mixed_bc = jax.nn.silu(causal_edge(bc_ext, conv_bc_w, conv_bc_b))
    half_width = mixed_bc.shape[-1] // 2
    input_map = mixed_bc[..., :half_width]
    output_map = mixed_bc[..., half_width:]
    step_size = jax.nn.softplus(unmixed_timestep + dt_bias)
    a_decay = -jnp.exp(a_log)
    outputs, final_memory, decay_sum = jax.vmap(partial(part_scan, a_decay=a_decay))(
        values, step_size, input_map, output_map
    )
    return (outputs + d_skip[:, None] * values, final_memory, decay_sum, output_map)


def read_carried(decay_sum, output_map, carried):
    return jnp.exp(decay_sum)[..., None] * jnp.einsum(
        "shpn,sln->slhp", carried, output_map, precision=HIGH
    )


def full_mix(inner_ext, bc_ext, unmixed_timestep, params, carried, head_size):
    y_zero, memory_zero, decay_sum, output_map = local_core(
        inner_ext, bc_ext, unmixed_timestep, params, head_size
    )
    y_full = y_zero + read_carried(decay_sum, output_map, carried)
    end_memory = jnp.exp(decay_sum[:, -1])[..., None, None] * carried + memory_zero
    return (y_full, end_memory)


def compose(earlier, later):
    return (earlier[0] + later[0], jnp.exp(later[0])[..., None, None] * earlier[1] + later[1])


def input_norm(residual, gain_values):
    return (
        residual
        * lax.rsqrt(jnp.mean(residual * residual, axis=-1, keepdims=True) + EPS)
        * gain_values
    )


def per_device(
    tokens,
    norm_gain,
    w_zx,
    w_dt,
    w_bc,
    conv_x_w,
    conv_x_b,
    conv_bc_w,
    conv_bc_b,
    dt_bias,
    a_log,
    d_skip,
    norm_w,
    w_out,
    output_gradient,
):
    complete_gate_inner, complete_timestep, complete_output, complete_bc_rows, full_gain = (
        lax.all_gather(w_zx, ("dp", "ctx"), axis=0, tiled=True),
        lax.all_gather(w_dt, ("dp", "ctx"), axis=0, tiled=True),
        lax.all_gather(w_out, ("dp", "ctx"), axis=0, tiled=True),
        lax.all_gather(w_bc, ("dp", "ctx"), axis=0, tiled=True),
        lax.all_gather(norm_gain, ("dp", "ctx"), axis=0, tiled=True),
    )
    seqs_here, length, width = tokens.shape
    heads_here = complete_timestep.shape[1]
    inner_here = complete_output.shape[1]
    head_size = inner_here // heads_here
    conv_taps = conv_x_w.shape[0]
    edge_rows = conv_taps - 1
    inner_total = inner_here * lax.axis_size("tensor")
    params = (conv_x_w, conv_x_b, conv_bc_w, conv_bc_b, dt_bias, a_log, d_skip)
    residual = tokens.astype(jnp.float32)
    gain_values = full_gain.astype(jnp.float32)
    normalized_rows = input_norm(residual, gain_values).astype(jnp.bfloat16)
    projected_rows = jnp.einsum(
        "cng,gom->cnom", normalized_rows, complete_gate_inner, preferred_element_type=jnp.float32
    )
    gate_raw = projected_rows[:, :, 0]
    inner_raw = projected_rows[:, :, 1].astype(jnp.bfloat16)
    unmixed_timestep = jnp.einsum(
        "cwt,tj->cwj", normalized_rows, complete_timestep, preferred_element_type=jnp.float32
    )
    unmixed_bc_values = jnp.einsum(
        "rvy,ym->rvm", normalized_rows, complete_bc_rows, preferred_element_type=jnp.float32
    ).astype(jnp.bfloat16)
    edge_inner, edge_bc = shifted(
        (inner_raw[:, length - edge_rows :], unmixed_bc_values[:, length - edge_rows :]), "ctx", 1
    )
    inner_ext = jnp.concatenate([edge_inner, inner_raw], 1).astype(jnp.float32)
    bc_ext = jnp.concatenate([edge_bc, unmixed_bc_values], 1).astype(jnp.float32)
    y_zero, memory_zero, decay_sum, output_map = local_core(
        inner_ext, bc_ext, unmixed_timestep, params, head_size
    )
    log_total = decay_sum[:, -1]
    identity = (jnp.zeros_like(log_total), jnp.zeros_like(memory_zero))
    carried = carried_in((log_total, memory_zero), "ctx", compose, identity, False)[1]
    y_ssd = y_zero + read_carried(decay_sum, output_map, carried)
    y_flat = y_ssd.reshape(seqs_here, length, inner_here)
    gate_act = jax.nn.silu(gate_raw)
    gated_rows = y_flat * gate_act
    squares = lax.psum(jnp.sum(gated_rows * gated_rows, axis=-1), "tensor")
    inv_rms = lax.rsqrt(squares / inner_total + EPS)[..., None]
    mixer_input_rows = (gated_rows * inv_rms * norm_w).astype(jnp.bfloat16)
    output_piece = jnp.einsum(
        "qau,zu->qaz", mixer_input_rows, complete_output, preferred_element_type=jnp.float32
    )
    total_out = lax.psum(output_piece, "tensor")
    mixed_out = (residual + total_out).astype(jnp.bfloat16)
    mixer_input_gradient = jnp.einsum(
        "rzv,vc->rzc", output_gradient, complete_output, preferred_element_type=jnp.float32
    )
    grad_w_out_part = jnp.einsum(
        "wxv,wxn->vn", output_gradient, mixer_input_rows, preferred_element_type=jnp.float32
    )
    weighted = mixer_input_gradient * norm_w
    gate_dots = lax.psum(jnp.sum(weighted * gated_rows, axis=-1), "tensor")
    grad_norm_w_part = jnp.sum(mixer_input_gradient * gated_rows * inv_rms, axis=(0, 1))
    grad_gated = (
        inv_rms * weighted
        - gated_rows * (inv_rms * inv_rms * inv_rms) * (gate_dots / inner_total)[..., None]
    )
    gate_sig = jax.nn.sigmoid(gate_raw)
    grad_gate = grad_gated * y_flat * gate_sig * (1.0 + gate_raw * (1.0 - gate_sig))
    grad_y = (grad_gated * gate_act).reshape(seqs_here, length, heads_here, head_size)
    pulled = jnp.einsum(
        "slhp,sln->shpn", grad_y * jnp.exp(decay_sum)[..., None], output_map, precision=HIGH
    )
    identity_back = (jnp.zeros_like(log_total), jnp.zeros_like(pulled))
    from_later = carried_in((log_total, pulled), "ctx", compose, identity_back, True)[1]
    mix_pieces = partial(full_mix, head_size=head_size)
    _, mix_pull = jax.vjp(mix_pieces, inner_ext, bc_ext, unmixed_timestep, params, carried)
    grad_inner_ext, grad_bc_ext, grad_dt_raw, grad_params, _ = mix_pull((grad_y, from_later))
    back_inner, back_bc = (
        shifted(grad_inner_ext[:, :edge_rows].astype(jnp.bfloat16), "ctx", -1).astype(jnp.float32),
        shifted(grad_bc_ext[:, :edge_rows].astype(jnp.bfloat16), "ctx", -1).astype(jnp.float32),
    )
    own_inner = grad_inner_ext[:, edge_rows:]
    own_bc = grad_bc_ext[:, edge_rows:]
    grad_inner = jnp.concatenate(
        [own_inner[:, : length - edge_rows], own_inner[:, length - edge_rows :] + back_inner], 1
    )
    grad_bc = jnp.concatenate(
        [own_bc[:, : length - edge_rows], own_bc[:, length - edge_rows :] + back_bc], 1
    )
    gradient_stack = jnp.stack(
        [grad_gate.astype(jnp.bfloat16), grad_inner.astype(jnp.bfloat16)], axis=2
    )
    reduced_timestep_gradient = grad_dt_raw.astype(jnp.bfloat16)
    reduced_bc_gradient = grad_bc.astype(jnp.bfloat16)
    grad_normed = jnp.einsum(
        "qwat,nat->qwn", gradient_stack, complete_gate_inner, preferred_element_type=jnp.float32
    )
    grad_normed = grad_normed + jnp.einsum(
        "wcn,kn->wck",
        reduced_timestep_gradient,
        complete_timestep,
        preferred_element_type=jnp.float32,
    )
    grad_normed = grad_normed + jnp.einsum(
        "hgz,qz->hgq", reduced_bc_gradient, complete_bc_rows, preferred_element_type=jnp.float32
    )
    grad_normed = lax.psum(grad_normed, "tensor")
    grad_zx_part = jnp.einsum(
        "ejp,ejnh->pnh", normalized_rows, gradient_stack, preferred_element_type=jnp.float32
    )
    grad_dt_part = jnp.einsum(
        "iwv,iwx->vx",
        normalized_rows,
        reduced_timestep_gradient,
        preferred_element_type=jnp.float32,
    )
    grad_bc_part = jnp.einsum(
        "tam,tag->mg", normalized_rows, reduced_bc_gradient, preferred_element_type=jnp.float32
    )
    _, norm_pull = jax.vjp(input_norm, residual, gain_values)
    grad_residual, grad_gain_part = norm_pull(grad_normed)
    grad_tokens = grad_residual + output_gradient.astype(jnp.float32)
    grad_zx, grad_dt, grad_w_out, grad_bc_rows, grad_gain = (
        lax.psum_scatter(grad_zx_part, ("dp", "ctx"), scatter_dimension=0, tiled=True),
        lax.psum_scatter(grad_dt_part, ("dp", "ctx"), scatter_dimension=0, tiled=True),
        lax.psum_scatter(grad_w_out_part, ("dp", "ctx"), scatter_dimension=0, tiled=True),
        lax.psum_scatter(grad_bc_part, ("dp", "ctx"), scatter_dimension=0, tiled=True),
        lax.psum_scatter(grad_gain_part, ("dp", "ctx"), scatter_dimension=0, tiled=True),
    )
    small_sums = lax.psum(
        (
            grad_params[0],
            grad_params[1],
            grad_params[2],
            grad_params[3],
            grad_params[4],
            grad_params[5],
            grad_params[6],
            grad_norm_w_part,
        ),
        ("dp", "ctx"),
    )
    grad_w_bc, grad_conv_bc_w, grad_conv_bc_b = lax.psum(
        (grad_bc_rows, small_sums[2], small_sums[3]), "tensor"
    )
    return (
        mixed_out,
        grad_tokens,
        grad_gain,
        grad_zx,
        grad_dt,
        grad_w_bc,
        small_sums[0],
        small_sums[1],
        grad_conv_bc_w,
        grad_conv_bc_b,
        small_sums[4],
        small_sums[5],
        small_sums[6],
        small_sums[7],
        grad_w_out,
    )


def solution(mesh):
    return jax.shard_map(
        per_device,
        mesh=mesh,
        in_specs=(
            P("dp", "ctx", None),
            P(("dp", "ctx")),
            P(("dp", "ctx"), None, "tensor"),
            P(("dp", "ctx"), "tensor"),
            P(("dp", "ctx"), None),
            P(None, "tensor"),
            P("tensor"),
            P(),
            P(),
            P("tensor"),
            P("tensor"),
            P("tensor"),
            P("tensor"),
            P(("dp", "ctx"), "tensor"),
            P("dp", "ctx", None),
        ),
        out_specs=(
            P("dp", "ctx", None),
            P("dp", "ctx", None),
            P(("dp", "ctx")),
            P(("dp", "ctx"), None, "tensor"),
            P(("dp", "ctx"), "tensor"),
            P(("dp", "ctx"), None),
            P(None, "tensor"),
            P("tensor"),
            P(),
            P(),
            P("tensor"),
            P("tensor"),
            P("tensor"),
            P("tensor"),
            P(("dp", "ctx"), "tensor"),
        ),
        check_vma=False,
    )
```

profile of v0, /device:TPU:9, one launch (start us, length us, event | category | flops | bytes accessed | tf_op | source)
XLA Modules:
  0.0 1442.7 jit_solution(14749879174814050983)
XLA Ops:
  11.9 28.9 %all-reduce.20 = bf16[1024]{0:T(1024)(128)(2,1)S(1)} all-reduce(bf16[1024]{0:T(1024)(128)(2,1)S(1)} %dynamic-update-slice), channel_id=1, replica_groups=mesh['dp'=4,'ctx'=4,'tensor'=2] {'dp','ctx'}, use_global_device_ids=true, to_apply=%add.20 | all-reduce | flops 1024 | bytes 4096
  43.9 37.7 %all_gather.34 = bf16[1024,256]{1,0:T(8,128)(2,1)S(1)} all-gather(bf16[64,256]{1,0:T(8,128)(2,1)} %param.23), channel_id=1, replica_groups=mesh['dp'=4,'ctx'=4,'tensor'=2] {'dp','ctx'}, dimensions={0}, use_global_device_ids=true | all-gather | bytes 557056 | tf_op jit(solution)/shard_map/all_gather | solution.py:152
  89.6 27.9 %all-gather.3 = bf16[16,64,16]{1,2,0:T(8,128)(2,1)S(1)} all-gather(bf16[1,64,16]{1,2,0:T(8,128)(2,1)S(1)} %bitcast.414), channel_id=1, replica_groups=mesh['dp'=4,'ctx'=4,'tensor'=2] {'dp','ctx'}, dimensions={0}, use_global_device_ids=true | all-gather | bytes 34816 | tf_op jit(solution)/shard_map/all_gather | solution.py:150
  130.7 15.1 %fusion.62 = f32[8,256,2,1024]{3,1,2,0:T(8,128)S(1)} fusion(bf16[1024,2,1024]{2,0,1:T(8,128)(2,1)} %all-gather.9.cloned.1.call-done, bf16[8,256,1024]{2,1,0:T(8,128)(2,1)} %param.19, f32[1024]{0:T(1024)S(1)} %convert_element_type.55, f32[8,256]{1,0:T(8,128)S(1)} %fusion.149), kind=kOutput, calls=%fused_computation.103 | convolution fusion | flops 8598323200 | bytes 25178112 | tf_op jit(solution)/shard_map/cng,gom->cnom/dot_general | solution.py:166
  160.7 19.5 %fusion.50 = (f32[8,256,1024]{2,1,0:T(8,128)}, f32[8,256,1024]{2,1,0:T(8,128)}) fusion(f32[1024]{0:T(1024)S(1)} %bitcast.393, f32[8,259,1024]{2,1,0:T(8,128)} %maximum_convert_fusion, f32[1024]{0:T(1024)S(1)} %bitcast.395, f32[1024]{0:T(1024)S(1)} %bitcast.391, f32[1024]{0:T(1024)S(1)} %bitcast.389, f32[1024]{0:T(1024)S(1)} %copy-done.56), kind=kLoop, calls=%fused_computation.88 | loop fusion | flops 25165824 | bytes 50352128 | tf_op jit(solution)/shard_map/jit(silu)/mul | solution.py:89
  180.1 9.3 copy.250
  189.4 11.3 fusion.82
  212.6 8.4 slice.205
  221.1 9.1 copy.263
  230.2 40.0 %fusion.5 = f32[8,16,64,256]{3,2,1,0:T(8,128)} fusion(f32[8,256,256]{2,1,0:T(8,128)} %fusion.158, f32[8,256,16]{1,2,0:T(8,128)} %copy.257, pred[256,256]{1,0:T(8,128)(4,1)S(1)} %iota_compare_fusion, f32[8,256,16,64]{1,3,2,0:T(8,128)} %bitcast.365, f32[8,256,16]{1,2,0:T(8,128)S(1)} %add_select_fusion), kind=kOutput, calls=%fused_computation.12 | convolution fusion | flops 6469713920 | bytes 19202048 | tf_op jit(solution)/shard_map/vmap()/while/body/eval_jaxpr/checkpoint/tsh,shp->thp/dot_general | solution.py:47
  270.3 113.3 %all-gather.13.cloned.1.call-done = f32[32,16,64,128]{3,2,1,0:T(8,128)} async-done(((f32[8,16,64,128]{3,2,1,0:T(8,128)}), f32[32,16,64,128]{3,2,1,0:T(8,128)}) %all-gather.13.cloned.1.call-update) | async-done | bytes 16777232 | tf_op jit(solution)/shard_map/all_gather | solution.py:25
  386.3 10.5 fusion.110
  396.8 18.1 %multiply_reduce_fusion.11 = (f32[8,256]{1,0:T(8,128)S(1)}, f32[8,256,16,64]{1,3,2,0:T(8,128)}) fusion(f32[8,256,16,64]{1,3,2,0:T(8,128)} %bitcast.382, f32[8,256,16,64]{1,3,2,0:T(8,128)} %fusion.110, f32[8,256,16,64]{1,3,2,0:T(8,128)} %bitcast.366, f32[16]{0:T(128)S(1)} %copy-done.64, f32[8,256,256]{2,1,0:T(8,128)S(1)} %copy-done.4, ...), kind=kOutput, calls=%fused_computation.84 | convolution fusion | flops 3248486400 | bytes 43131392 | tf_op jit(solution)/shard_map/vmap()/while/body/eval_jaxpr/checkpoint/hpn,tn->thp/dot_general | solution.py:48
  414.9 9.2 copy.262
  426.9 19.6 %all-gather.11.cloned.1.call-done = bf16[1024,1024]{1,0:T(8,128)(2,1)} async-done(((bf16[64,1024]{1,0:T(8,128)(2,1)}), bf16[1024,1024]{1,0:T(8,128)(2,1)}) %all-gather.11.cloned.1.call-update) | async-done | bytes 2097168 | tf_op jit(solution)/shard_map/all_gather | solution.py:151
  446.5 14.6 %multiply_reduce_fusion = (f32[1024]{0:T(1024)}, f32[8,256]{1,0:T(8,128)S(1)}, f32[8,256,1024]{2,1,0:T(8,128)}, f32[8,256,1024]{2,1,0:T(8,128)}) fusion(f32[8,256]{1,0:T(8,128)S(1)} %get-tuple-element.450, f32[1024]{0:T(1024)S(1)} %copy-done.57, f32[8,256,1024]{2,1,0:T(8,128)} %copy.262, f32[8,256,2,1024]{3,1,2,0:T(8,128)} %copy-done.6, ...), kind=kOutput, calls=%fused_computation.67 | convolution fusion | flops 4318032896 | bytes 39870464 | tf_op jit(solution)/shard_map/rzv,vc->rzc/dot_general | solution.py:200
  464.9 19.6 %multiply_reduce_fusion.1 = (f32[1024]{0:T(1024)}, f32[8,256,1024]{2,1,0:T(8,128)}, bf16[8,256,1,1024]{3,1,0,2:T(8,128)(2,1)}) fusion(f32[8,256,1024]{2,1,0:T(8,128)} %get-tuple-element.420, f32[8,256,2,1024]{3,1,2,0:T(8,128)} %copy-done.6, f32[8,256]{1,0:T(8,128)S(1)} %broadcast_multiply_fusion.9, f32[8,256,1024]{2,1,0:T(8,128)} %get-tuple-element.418, ...), kind=kLoop, calls=%fused_computation.68 | loop fusion | flops 48233472 | bytes 54558720 | tf_op jit(solution)/shard_map/transpose(jvp())/reduce_sum | solution.py:101
  484.5 9.1 copy.265
  493.7 11.1 fusion.53
  506.6 9.9 multiply_reduce_fusion.9
  517.7 19.1 %fusion.95 = f32[8,256,128]{2,1,0:T(8,128)} fusion(f32[8,16,64,128]{3,2,1,0:T(8,128)} %get-tuple-element.238, f32[8,256,16,64]{1,3,2,0:T(8,128)} %bitcast.357, f32[8,256,16]{1,2,0:T(8,128)S(1)} %copy.259), kind=kOutput, calls=%fused_computation.147 | convolution fusion | flops 3223322624 | bytes 13762560 | tf_op jit(solution)/shard_map/transpose(jvp(shpn,sln->slhp))/dot_general | solution.py:105
  536.8 123.8 %all-gather.15.cloned.1.call-done = f32[32,16,64,128]{3,2,1,0:T(8,128)} async-done(((f32[8,16,64,128]{3,2,1,0:T(8,128)}), f32[32,16,64,128]{3,2,1,0:T(8,128)}) %all-gather.15.cloned.1.call-update) | async-done | bytes 16777232 | tf_op jit(solution)/shard_map/all_gather | solution.py:25
  663.1 17.9 %while.17 = (s32[]{:T(128)}, f32[8,16,64,128]{3,2,1,0:T(8,128)}, s32[]{:T(128)}, f32[4,8,16]{2,1,0:T(8,128)S(1)}, f32[4,8,16,64,128]{4,3,2,1,0:T(8,128)}, /*index=5*/s32[]{:T(128)}, s32[]{:T(128)}, s32[]{:T(128)}, s32[]{:T(128)}) while((s32[]{:T(128)}, f32[8,16,64,128]{3,2,1,0:T(8,128)}, s32[]{:T(128)}, f32[4,8,16]{2,1,0:T(8,128)S(1)}, ...), condition=%wide.region_11.12_spmd, body=%wide.region_10.11_spmd.sunk | while | flops 2097158 | bytes 12584595 | solution.py:34
  663.2 5.9 bitcast_add_fusion.9
  675.0 5.9 bitcast_add_fusion.9
  701.5 8.4 multiply_reduce_fusion.6
  709.9 28.9 %fusion.3 = f32[8,16,64,256]{3,2,1,0:T(8,128)} fusion(f32[8,256,256]{2,1,0:T(8,128)S(1)} %fusion.182, f32[8,256,16]{1,2,0:T(8,128)S(1)} %copy-done.24, pred[256,256]{1,0:T(8,128)(4,1)S(1)} %iota_compare_fusion, f32[8,256,16,64]{1,3,2,0:T(8,128)S(1)} %bitcast.362), kind=kOutput, calls=%fused_computation.9 | convolution fusion | flops 6467616768 | bytes 19070976 | tf_op jit(solution)/shard_map/transpose(jvp(vmap()))/while/body/eval_jaxpr/checkpoint/tsh,shp->thp/dot_general | solution.py:47
  738.8 51.2 %fusion.11 = (f32[8,256,16]{1,2,0:T(8,128)}, f32[8,256,16]{1,2,0:T(8,128)}, f32[8,256,256]{2,1,0:T(8,128)}) fusion(f32[8,256,256]{2,1,0:T(8,128)S(1)} %fusion.182, f32[8,256,16]{1,2,0:T(8,128)S(1)} %copy-done.24, pred[256,256]{1,0:T(8,128)(4,1)S(1)} %iota_compare_fusion, f32[8,256,16,64]{1,3,2,0:T(8,128)} %bitcast.367, ...), kind=kOutput, calls=%fused_computation.18 | convolution fusion | flops 6519455744 | bytes 21561344 | tf_op jit(solution)/shard_map/transpose(jvp(vmap()))/while/body/eval_jaxpr/checkpoint/tsh,shp->thp/dot_general | solution.py:47
  790.1 16.7 %fusion.101 = f32[8,256,128]{2,1,0:T(8,128)} fusion(f32[8,16,64,128]{3,2,1,0:T(8,128)S(1)} %copy-done, f32[8,256,16,64]{1,3,2,0:T(8,128)} %bitcast.368, f32[8,256,16]{1,2,0:T(8,128)S(1)} %add_select_fusion, f32[8,256,16]{1,2,0:T(8,128)S(1)} %copy.271), kind=kOutput, calls=%fused_computation.149 | convolution fusion | flops 3225419776 | bytes 13893632 | tf_op jit(solution)/shard_map/transpose(jvp(vmap()))/while/body/eval_jaxpr/checkpoint/shp,sn->hpn/dot_general | solution.py:53
  806.8 14.6 %multiply_reduce_fusion.7 = (f32[8,256,16]{1,2,0:T(8,128)}, f32[8,256,16]{1,2,0:T(8,128)}, f32[8,256,16,64]{1,3,2,0:T(8,128)}) fusion(f32[8,256,16,64]{1,3,2,0:T(8,128)} %bitcast.369, f32[8,256,16]{1,2,0:T(8,128)S(1)} %add_select_fusion, f32[8,16,64,256]{3,2,1,0:T(8,128)S(1)} %copy-done.11, f32[8,256,16]{1,2,0:T(8,128)S(1)} %copy.271, ...), kind=kOutput, calls=%fused_computation.78 | convolution fusion | flops 3237937152 | bytes 30932992 | tf_op jit(solution)/shard_map/transpose(jvp(vmap()))/while/body/eval_jaxpr/checkpoint/shp,sn->hpn/dot_general | solution.py:53
  837.3 18.2 %fusion.98 = f32[8,256,128]{2,1,0:T(8,128)} fusion(f32[8,16,64,128]{3,2,1,0:T(8,128)} %copy-done.3, f32[8,256,16,64]{1,3,2,0:T(8,128)} %bitcast.358, f32[8,256,16]{1,2,0:T(8,128)S(1)} %copy.288), kind=kOutput, calls=%fused_computation.148 | convolution fusion | flops 3223322624 | bytes 13762560 | tf_op jit(solution)/shard_map/transpose(jvp(vmap()))/while/body/eval_jaxpr/checkpoint/hpn,tn->thp/dot_general | solution.py:48
  855.6 9.4 copy.274
  882.2 13.0 multiply_reduce_fusion.5
  895.2 14.6 %broadcast_multiply_fusion.1 = (f32[8,256,1024]{2,1,0:T(8,128)}, f32[8,256,1024]{2,1,0:T(8,128)}, f32[8,256,1024]{2,1,0:T(8,128)}, f32[8,256,1024]{2,1,0:T(8,128)}) fusion(f32[8,256,1024]{2,1,0:T(8,128)} %get-tuple-element.413, f32[1024]{0:T(1024)S(1)} %bitcast.394, f32[1024]{0:T(1024)S(1)} %bitcast.390, f32[1024]{0:T(1024)S(1)} %bitcast.392, ...), kind=kLoop, calls=%fused_computation.120 | loop fusion | flops 8388608 | bytes 41959424 | tf_op jit(solution)/shard_map/transpose(jvp())/mul | solution.py:82
  912.8 19.8 %reduce-window.36 = f32[8,16,2,128]{3,1,2,0:T(8,128)S(1)} reduce-window(f32[8,16,2,128]{3,1,2,0:T(8,128)S(1)} %copy.276, f32[]{:T(128)} %constant.151.clone.1), window={size=1x1x1x128 pad=0_0x0_0x0_0x0_127}, to_apply=%region_16.17 | reduce-window | flops 4161536 | bytes 262148 | tf_op jit(solution)/shard_map/reduce-window.6
  939.4 19.8 %reduce-window.48 = f32[8,16,2,128]{3,1,2,0:T(8,128)S(1)} reduce-window(f32[8,16,2,128]{3,1,2,0:T(8,128)S(1)} %copy.284, f32[]{:T(128)} %constant.151.clone.1), window={size=1x1x1x128 pad=0_0x0_0x0_0x0_127}, to_apply=%region_25.26 | reduce-window | flops 4161536 | bytes 262148 | tf_op jit(solution)/shard_map/reduce-window.8
  959.6 17.0 %fusion.175 = (bf16[8,259,1024]{2,1,0:T(8,128)(2,1)S(1)}, f32[8,259,1024]{2,1,0:T(8,128)}) fusion(f32[8,256,1024]{2,1,0:T(8,128)} %get-tuple-element.426, f32[8,256,1024]{2,1,0:T(8,128)} %get-tuple-element.427, f32[8,256,1024]{2,1,0:T(8,128)} %get-tuple-element.428, f32[8,256,1024]{2,1,0:T(8,128)} %get-tuple-element.425), kind=kLoop, calls=%fused_computation.266 | loop fusion | flops 8486912 | bytes 46284800 | tf_op jit(solution)/shard_map/convert.8
  986.3 15.1 %fusion.79 = f32[1024,2,1024]{2,0,1:T(8,128)} fusion(bf16[8,3,1,1024]{3,1,0,2:T(4,128)(2,1)S(1)} %fusion.134, bf16[8,253,1,1024]{3,1,0,2:T(8,128)(2,1)} %slice_bitcast_fusion, bf16[8,256,1,1024]{3,1,0,2:T(8,128)(2,1)} %get-tuple-element.423, bf16[8,256,1024]{2,1,0:T(8,128)(2,1)} %param.19, f32[1024]{0:T(1024)S(1)} %copy-done.31, f32[8,256]{1,0:T(8,128)S(1)} %copy-done.28), kind=kOutput, calls=%fused_computation.125 | convolution fusion | flops 8623489024 | bytes 20983808 | tf_op jit(solution)/shard_map/ejp,ejnh->pnh/dot_general | solution.py:254
  1002.1 12.0 fusion.89
  1023.1 16.9 %fusion.32 = f32[8,256,1024]{2,1,0:T(8,128)} fusion(f32[8,256,1024]{2,1,0:T(8,128)} %fusion.113, f32[8,256,1024]{2,1,0:T(8,128)} %fusion.139, bf16[1024,2,1024]{2,0,1:T(8,128)(2,1)} %all-gather.9.cloned.1.call-done, bf16[8,3,1,1024]{3,1,0,2:T(4,128)(2,1)S(1)} %fusion.134, bf16[8,253,1,1024]{3,1,0,2:T(8,128)(2,1)} %slice_bitcast_fusion, ...), kind=kOutput, calls=%fused_computation.50 | convolution fusion | flops 8619294720 | bytes 37748736 | tf_op jit(solution)/shard_map/qwat,nat->qwn/dot_general | solution.py:241
  1040.2 11.4 convolution_bitcast_fusion
  1058.0 17.4 %reduce-scatter.13.cloned.1.call-done = f32[64,16]{1,0:T(8,128)} async-done(((f32[1024,16]{1,0:T(8,128)}), f32[64,16]{1,0:T(8,128)}) %reduce-scatter.13.cloned.1.call-update) | async-done | bytes 4112
  1076.8 192.0 %reduce-scatter.9.cloned.1.call-done = f32[64,2,1024]{2,0,1:T(8,128)} async-done(((f32[1024,2,1024]{2,0,1:T(8,128)}), f32[64,2,1024]{2,0,1:T(8,128)}) %reduce-scatter.9.cloned.1.call-update) | async-done | bytes 524304 | tf_op jit(solution)/shard_map/reduce_scatter | solution.py:270
  1271.0 64.9 %all-reduce.27.cloned.1.call-done = (f32[8,256,1024]{2,1,0:T(8,128)}, f32[8,256,1024]{2,1,0:T(8,128)}, f32[64,256]{1,0:T(8,128)}) async-done(((f32[8,256,1024]{2,1,0:T(8,128)}, f32[8,256,1024]{2,1,0:T(8,128)}, f32[64,256]{1,0:T(8,128)}), (f32[8,256,1024]{2,1,0:T(8,128)}, f32[8,256,1024]{2,1,0:T(8,128)}, f32[64,256]{1,0:T(8,128)})) %all-reduce.27.cloned.1.call-update) | async-done | bytes 16842768 | tf_op jit(solution)/shard_map/psum | solution.py:198
  1336.0 6.1 fusion.25
  1342.1 60.0 %all-reduce.22 = (f32[1024]{0:T(1024)S(1)}, f32[4,1024]{1,0:T(4,128)}, f32[1024]{0:T(1024)}, f32[4,256]{1,0:T(4,128)S(1)}, f32[256]{0:T(256)S(1)}, /*index=5*/f3...) all-reduce(f32[1024]{0:T(1024)S(1)} %get-tuple-element.364, ...), channel_id=5, replica_groups=mesh['dp'=4,'ctx'=4,'tensor'=2] {'dp','ctx'}, use_global_device_ids=true, to_apply=%region_31.32.clone | all-reduce | flops 8496 | bytes 67968
  1402.7 14.7 %all-reduce.23 = (f32[4,256]{1,0:T(4,128)}, f32[256]{0:T(256)}) all-reduce(f32[4,256]{1,0:T(4,128)S(1)} %get-tuple-element.397, f32[256]{0:T(256)S(1)} %get-tuple-element.398), channel_id=1, replica_groups=mesh['dp'=4,'ctx'=4,'tensor'=2] {'tensor'}, use_global_device_ids=true, to_apply=%region_48.49 | all-reduce | flops 1280 | bytes 10240 | tf_op jit(solution)/shard_map/psum | solution.py:289
  1417.5 14.8 %fusion.28 = (f32[8,256,1024]{2,1,0:T(8,128)}, bf16[8,256,1024]{2,1,0:T(8,128)(2,1)}) fusion(bf16[8,256,1024]{2,1,0:T(8,128)(2,1)} %param.19, bf16[8,256,1024]{2,1,0:T(8,128)(2,1)} %param.33, f32[8,256,1024]{2,1,0:T(8,128)} %get-tuple-element.406, f32[8,256]{1,0:T(8,128)S(1)} %multiply_multiply_fusion.1, f32[1024]{0:T(1024)S(1)} %copy-done.31, ...), kind=kLoop, calls=%fused_computation.43 | loop fusion | flops 20971520 | bytes 37769216 | tf_op jit(solution)/shard_map/add | solution.py:268
  (301 shorter events, 171.6 us)
Async XLA Ops:
  7.2 82.4 %copy-start.60 = (bf16[64,16]{0,1:T(8,128)(2,1)S(1)}, bf16[64,16]{0,1:T(8,128)(2,1)}, u32[]{:S(2)}) copy-start(bf16[64,16]{0,1:T(8,128)(2,1)} %param.22) | copy-start | bytes 6148
  7.2 110.4 %copy-start.65 = (f32[16]{0:T(128)S(1)}, f32[16]{0:T(128)}, u32[]{:S(2)}) copy-start(f32[16]{0:T(128)} %param.29) | copy-start | bytes 196
  7.2 110.5 %copy-start.67 = (f32[16]{0:T(128)S(1)}, f32[16]{0:T(128)}, u32[]{:S(2)}) copy-start(f32[16]{0:T(128)} %param.28) | copy-start | bytes 196
  7.2 123.4 %all-gather.9.cloned.1.call-start = ((), (), s32[]{:S(2)}) async-start(), calls=%async_computation.4 | async-start | bytes 4456448 | tf_op jit(solution)/shard_map/all_gather | solution.py:149
  9.0 374.6 %all-gather.13.cloned.1.call-start = ((), (), s32[]{:S(2)}) async-start(), calls=%async_computation.8 | async-start | bytes 20971520 | tf_op jit(solution)/shard_map/all_gather | solution.py:25
  40.8 89.8 %copy-start.30 = (f32[1024]{0:T(1024)}, f32[1024]{0:T(1024)S(1)}, u32[]{:S(2)}) copy-start(f32[1024]{0:T(1024)S(1)} %convert_element_type.55) | copy-start | bytes 12292
  43.9 73.6 %copy-start.25 = (f32[8,256]{1,0:T(8,128)}, f32[8,256]{1,0:T(8,128)S(1)}, u32[]{:S(2)}) copy-start(f32[8,256]{1,0:T(8,128)S(1)} %fusion.29) | copy-start | bytes 24580
  43.9 86.7 %copy-start.27 = (f32[8,256]{1,0:T(8,128)}, f32[8,256]{1,0:T(8,128)S(1)}, u32[]{:S(2)}) copy-start(f32[8,256]{1,0:T(8,128)S(1)} %fusion.149) | copy-start | bytes 24580
  82.5 44.9 %copy-start.45 = (f32[4,1024]{1,0:T(4,128)S(1)}, f32[4,1024]{1,0:T(4,128)}, u32[]{:S(2)}) copy-start(f32[4,1024]{1,0:T(4,128)} %param.24) | copy-start | bytes 49156
  87.0 41.7 %copy-start.62 = (f32[4,256]{1,0:T(4,128)S(1)}, f32[4,256]{1,0:T(4,128)}, u32[]{:S(2)}) copy-start(f32[4,256]{1,0:T(4,128)} %param.26) | copy-start | bytes 12292
  87.0 42.1 %collective-permute-start.1 = (bf16[8,3,256]{2,1,0:T(4,128)(2,1)S(1)}, bf16[8,3,256]{2,1,0:T(4,128)(2,1)S(1)}, u32[]{:S(2)}, u32[]{:S(2)}) collective-permute-start(bf16[8,3,256]{2,1,0:T(4,128)(2,1)S(1)} %slice.197), channel_id=1, source_target_pairs={{0,2},{2,4},{4,6},{1,3},{3,5},{5,7},{8,10},{10,12},{12,14},{9,11},... | collective-permute-start | bytes 36872 | tf_op jit(solution)/shard_map/ppermute | solution.py:18
  127.3 33.3 %copy-start.32 = (f32[1,1024]{1,0:T(1,128)}, f32[1,1024]{1,0:T(1,128)S(1)}, u32[]{:S(2)}) copy-start(f32[1,1024]{1,0:T(1,128)S(1)} %get-tuple-element.445) | copy-start | bytes 12292
  127.3 33.3 %copy-start.34 = (f32[1,1024]{1,0:T(1,128)}, f32[1,1024]{1,0:T(1,128)S(1)}, u32[]{:S(2)}) copy-start(f32[1,1024]{1,0:T(1,128)S(1)} %get-tuple-element.446) | copy-start | bytes 12292
  127.4 33.3 %copy-start.36 = (f32[1,1024]{1,0:T(1,128)}, f32[1,1024]{1,0:T(1,128)S(1)}, u32[]{:S(2)}) copy-start(f32[1,1024]{1,0:T(1,128)S(1)} %get-tuple-element.447) | copy-start | bytes 12292
  127.4 33.3 %copy-start.38 = (f32[1,1024]{1,0:T(1,128)}, f32[1,1024]{1,0:T(1,128)S(1)}, u32[]{:S(2)}) copy-start(f32[1,1024]{1,0:T(1,128)S(1)} %get-tuple-element.448) | copy-start | bytes 12292
  128.7 23.9 %copy-start.46 = (f32[1,256]{1,0:T(1,128)}, f32[1,256]{1,0:T(1,128)S(1)}, u32[]{:S(2)}) copy-start(f32[1,256]{1,0:T(1,128)S(1)} %get-tuple-element.451) | copy-start | bytes 3076
  128.8 23.9 %copy-start.48 = (f32[1,256]{1,0:T(1,128)}, f32[1,256]{1,0:T(1,128)S(1)}, u32[]{:S(2)}) copy-start(f32[1,256]{1,0:T(1,128)S(1)} %get-tuple-element.452) | copy-start | bytes 3076
  128.8 23.9 %copy-start.50 = (f32[1,256]{1,0:T(1,128)}, f32[1,256]{1,0:T(1,128)S(1)}, u32[]{:S(2)}) copy-start(f32[1,256]{1,0:T(1,128)S(1)} %get-tuple-element.453) | copy-start | bytes 3076
  128.8 23.9 %copy-start.52 = (f32[1,256]{1,0:T(1,128)}, f32[1,256]{1,0:T(1,128)S(1)}, u32[]{:S(2)}) copy-start(f32[1,256]{1,0:T(1,128)S(1)} %get-tuple-element.454) | copy-start | bytes 3076
  130.6 22.1 %copy-start.1 = (f32[8,259,256]{2,1,0:T(8,128)}, f32[8,259,256]{2,1,0:T(8,128)S(1)}, u32[]{:S(2)}) copy-start(f32[8,259,256]{2,1,0:T(8,128)S(1)} %maximum_convert_fusion.1) | copy-start | bytes 6365188
  150.1 5.9 collective-permute-start
  200.8 245.7 %all-gather.11.cloned.1.call-start = ((), (), s32[]{:S(2)}) async-start(), calls=%async_computation.5 | async-start | bytes 2228224 | tf_op jit(solution)/shard_map/all_gather | solution.py:151
  201.5 459.1 %all-gather.15.cloned.1.call-start = ((), (), s32[]{:S(2)}) async-start(), calls=%async_computation.9 | async-start | bytes 20971520 | tf_op jit(solution)/shard_map/all_gather | solution.py:25
  414.9 31.6 %copy-start.57 = (f32[1024]{0:T(1024)S(1)}, f32[1024]{0:T(1024)}, u32[]{:S(2)}) copy-start(f32[1024]{0:T(1024)} %param.31) | copy-start | bytes 12292
  426.9 38.0 %copy-start.40 = (f32[8,256]{1,0:T(8,128)}, f32[8,256]{1,0:T(8,128)S(1)}, u32[]{:S(2)}) copy-start(f32[8,256]{1,0:T(8,128)S(1)} %get-tuple-element.450) | copy-start | bytes 24580
  504.8 535.1 %reduce-scatter.11.cloned.1.call-start = ((), (), s32[]{:S(2)}) async-start(), calls=%async_computation.7 | async-start | bytes 1114112 | tf_op jit(solution)/shard_map/reduce_scatter | solution.py:273
  694.8 15.1 %copy-start.3 = (f32[8,16,64,128]{3,2,1,0:T(8,128)}, f32[8,16,64,128]{3,2,1,0:T(8,128)S(1)}, u32[]{:S(2)}) copy-start(f32[8,16,64,128]{3,2,1,0:T(8,128)S(1)} %broadcast.159) | copy-start | bytes 12582916
  738.8 51.2 %copy-start = (f32[8,16,64,128]{3,2,1,0:T(8,128)S(1)}, f32[8,16,64,128]{3,2,1,0:T(8,128)}, u32[]{:S(2)}) copy-start(f32[8,16,64,128]{3,2,1,0:T(8,128)} %get-tuple-element.243) | copy-start | bytes 12582916
  790.0 16.7 %copy-start.11 = (f32[8,16,64,256]{3,2,1,0:T(8,128)S(1)}, f32[8,16,64,256]{3,2,1,0:T(8,128)}, u32[]{:S(2)}) copy-start(f32[8,16,64,256]{3,2,1,0:T(8,128)} %fusion.3) | copy-start | bytes 25165828
  879.7 15.4 %copy-start.33 = (f32[1,1024]{1,0:T(1,128)S(1)}, f32[1,1024]{1,0:T(1,128)}, u32[]{:S(2)}) copy-start(f32[1,1024]{1,0:T(1,128)} %copy-done.32) | copy-start | bytes 12292
  879.7 15.4 %copy-start.35 = (f32[1,1024]{1,0:T(1,128)S(1)}, f32[1,1024]{1,0:T(1,128)}, u32[]{:S(2)}) copy-start(f32[1,1024]{1,0:T(1,128)} %copy-done.34) | copy-start | bytes 12292
  879.7 15.4 %copy-start.37 = (f32[1,1024]{1,0:T(1,128)S(1)}, f32[1,1024]{1,0:T(1,128)}, u32[]{:S(2)}) copy-start(f32[1,1024]{1,0:T(1,128)} %copy-done.36) | copy-start | bytes 12292
  879.7 15.4 %copy-start.39 = (f32[1,1024]{1,0:T(1,128)S(1)}, f32[1,1024]{1,0:T(1,128)}, u32[]{:S(2)}) copy-start(f32[1,1024]{1,0:T(1,128)} %copy-done.38) | copy-start | bytes 12292
  879.8 53.0 %collective-permute-start.3 = (bf16[8,3,256]{2,1,0:T(4,128)(2,1)S(1)}, bf16[8,3,256]{2,1,0:T(4,128)(2,1)S(1)}, u32[]{:S(2)}, u32[]{:S(2)}) collective-permute-start(bf16[8,3,256]{2,1,0:T(4,128)(2,1)S(1)} %slice.218), channel_id=1, source_target_pairs={{2,0},{4,2},{6,4},{3,1},{5,3},{7,5},{10,8},{12,10},{14,12},{11,9},... | collective-permute-start | bytes 36872 | tf_op jit(solution)/shard_map/ppermute | solution.py:18
  895.2 38.5 %copy-start.28 = (f32[8,256]{1,0:T(8,128)S(1)}, f32[8,256]{1,0:T(8,128)}, u32[]{:S(2)}) copy-start(f32[8,256]{1,0:T(8,128)} %copy-done.27) | copy-start | bytes 24580
  895.2 38.5 %copy-start.31 = (f32[1024]{0:T(1024)S(1)}, f32[1024]{0:T(1024)}, u32[]{:S(2)}) copy-start(f32[1024]{0:T(1024)} %copy-done.30) | copy-start | bytes 12292
  938.9 136.5 %reduce-scatter.13.cloned.1.call-start = ((), (), s32[]{:S(2)}) async-start(), calls=%async_computation.10 | async-start | bytes 557056
  959.5 19.0 %copy-start.19 = (f32[8,256,16]{1,2,0:T(8,128)S(1)}, f32[8,256,16]{1,2,0:T(8,128)}, u32[]{:S(2)}) copy-start(f32[8,256,16]{1,2,0:T(8,128)} %copy-done.18) | copy-start | bytes 393220
  959.5 19.0 %copy-start.21 = (f32[8,256,16]{1,2,0:T(8,128)S(1)}, f32[8,256,16]{1,2,0:T(8,128)}, u32[]{:S(2)}) copy-start(f32[8,256,16]{1,2,0:T(8,128)} %get-tuple-element.363) | copy-start | bytes 393220
  959.6 19.0 %copy-start.43 = (u8[256,16]{0,1:T(8,128)(4,1)S(1)}, u8[256,16]{0,1:T(8,128)(4,1)}, u32[]{:S(2)}) copy-start(u8[256,16]{0,1:T(8,128)(4,1)} %copy-done.42) | copy-start | bytes 12292
  959.6 19.0 %copy-start.59 = (u8[256,16]{0,1:T(8,128)(4,1)S(1)}, u8[256,16]{0,1:T(8,128)(4,1)}, u32[]{:S(2)}) copy-start(u8[256,16]{0,1:T(8,128)(4,1)} %get-tuple-element.372) | copy-start | bytes 12292
  976.6 8.7 collective-permute-start.2
  985.3 283.5 %reduce-scatter.9.cloned.1.call-start = ((), (), s32[]{:S(2)}) async-start(), calls=%async_computation.6 | async-start | bytes 8912896 | tf_op jit(solution)/shard_map/reduce_scatter | solution.py:270
  1001.5 334.5 %all-reduce.27.cloned.1.call-start = ((), (), s32[]{:S(2)}) async-start(), calls=%async_computation.12 | async-start | bytes 33685504 | tf_op jit(solution)/shard_map/psum | solution.py:198
  1039.9 395.2 %reduce-scatter.15.cloned.1.call-start = ((), (), s32[]{:S(2)}) async-start(), calls=%async_computation.11 | async-start | bytes 4456448
  1057.0 285.1 %copy-start.61 = (f32[1024]{0:T(1024)S(1)}, f32[1024]{0:T(1024)}, u32[]{:S(2)}) copy-start(f32[1024]{0:T(1024)} %get-tuple-element.360) | copy-start | bytes 12292
  1057.0 360.4 %copy-start.26 = (f32[8,256]{1,0:T(8,128)S(1)}, f32[8,256]{1,0:T(8,128)}, u32[]{:S(2)}) copy-start(f32[8,256]{1,0:T(8,128)} %copy-done.25) | copy-start | bytes 24580
  1417.5 17.7 %copy-start.29 = (f32[64,256]{1,0:T(8,128)S(1)}, f32[64,256]{1,0:T(8,128)}, u32[]{:S(2)}) copy-start(f32[64,256]{1,0:T(8,128)} %get-tuple-element.587) | copy-start | bytes 196612
  (40 other events, 252.9 us)
Sparse Core Ops, SparseCore 0:
  11.4 82.8 all-gather.8
  200.9 182.6 all-gather.12
  386.3 60.1 all-gather.10
  504.9 155.6 all-gather.14
  939.0 60.9 reduce-scatter.10
  1002.2 73.1 reduce-scatter.12
  1077.7 191.0 reduce-scatter.8
  1272.1 63.8 all-reduce.26
  1338.9 96.1 reduce-scatter.14
where the time goes:
time: 1460 us; the launch traced here: 1440 us
  waiting for transfers between devices  535 us (37%)
  matrix products  373 us (26%)
  other arithmetic  219 us (15%)
  blocking collectives  181 us (12%)
  local copies, waits for them, and re-layouts  108 us (7%)
  between operations  16.8 us (1%)
    all_gather x2, waiting for transfers between devices, carried_in(): gathered = jax.tree.map(lambda a: lax.all_gather(a, axis), part)  237 us
    reduce_scatter x1, waiting for transfers between devices, per_device(): lax.psum_scatter(grad_zx_part, ('dp', 'ctx'), scatter_dimension=0, tiled=...  192 us
    dot_general x3, matrix products, block_step(): inside = jnp.einsum('tsh,shp->thp', weights, scaled, precision=HIGH)  120 us
    unnamed x2, blocking collectives  89 us
    another operation x15, other arithmetic  69.3 us
    psum x1, waiting for transfers between devices, per_device(): total_out = lax.psum(output_piece, 'tensor')  64.9 us
    dot_general x3, matrix products, block_step(): jnp.einsum('hpn,tn->thp', memory, output_map, precision=HIGH)  44.8 us
    dot_general x3, matrix products, block_step(): jnp.einsum('shp,sn->hpn', remaining[:, :, None] * scaled, input_map, prec...  42.7 us
  transfers between devices with their start and end apart: 13, of which 7 were waited for; matrix products, arithmetic and copies ran while one was open for 24% of the time, Pallas kernels for 0%

commit v1 on v0

v1 whole, which is shorter than its diff:
```python
from functools import partial

import jax
import jax.numpy as jnp
from jax import lax
from jax.experimental import pallas as pl
from jax.experimental.pallas import tpu as pltpu
from jax.sharding import PartitionSpec as P

EPS = 1e-05
LOG2E = 1.4426950408889634
LANES = 128
HIGH = lax.Precision.HIGHEST
BF = jnp.bfloat16
F32 = jnp.float32


def bits_of(axis):
    return [1 << i for i in reversed(range(lax.axis_size(axis).bit_length() - 1))]


def swap(block, axis, mask):
    return lax.ppermute(block, axis, [(i, i ^ mask) for i in range(lax.axis_size(axis))])


def side(axis, bit):
    return (lax.axis_index(axis) // bit) % 2


def row_bits():
    return [("dp", b) for b in bits_of("dp")] + [("ctx", b) for b in bits_of("ctx")]


def gather_rows(shard, order):
    places = row_bits()
    whole = shard.reshape((1,) * len(places) + shard.shape)
    for place in order:
        dim = places.index(place)
        other = swap(whole, *place)
        whole = jnp.where(
            side(*place) == 1,
            jnp.concatenate([other, whole], dim),
            jnp.concatenate([whole, other], dim),
        )
    return whole.reshape((-1,) + shard.shape[1:])


def halve(part, dim, place):
    up = side(*place)
    mine = lax.dynamic_index_in_dim(part, up, dim)
    theirs = lax.dynamic_index_in_dim(part, 1 - up, dim)
    return mine + swap(theirs.astype(BF), *place).astype(F32)


def scatter_rows(part, order):
    places = row_bits()
    left = part.reshape((2,) * len(places) + (part.shape[0] >> len(places),) + part.shape[1:])
    for place in order:
        left = halve(left, places.index(place), place)
    return left.reshape(left.shape[len(places) :])


def sum_over(part, places):
    for place in places:
        part = part + swap(part, *place)
    return part


def spread_out(blocks, length):
    parts = lax.axis_size("ctx")
    me = lax.axis_index("ctx")
    cuts = lax.axis_size("tensor")
    rows = length // cuts
    width = blocks.shape[-1]
    seqs = blocks.shape[0] // parts
    mine = lax.dynamic_slice_in_dim(blocks, lax.axis_index("tensor") * rows, rows, 1)
    mine = mine.reshape(parts, seqs, rows, width)
    slots = []
    for k in range(parts):
        piece = lax.dynamic_index_in_dim(mine, me ^ k, 0, False)
        slots.append(swap(piece, "ctx", k) if k else piece)
    return gather_cuts(jnp.stack(slots))


def gather_cuts(share):
    for bit in reversed(bits_of("tensor")):
        other = swap(share, "tensor", bit)
        share = jnp.where(
            side("tensor", bit) == 1,
            jnp.concatenate([other, share], 2),
            jnp.concatenate([share, other], 2),
        )
    return share


def cut_sum(part):
    bits = bits_of("tensor")
    slots, seqs, length, width = part.shape
    left = part.reshape((slots, seqs) + (2,) * len(bits) + (length >> len(bits), width))
    for dim, bit in enumerate(bits):
        left = halve(left, 2 + dim, ("tensor", bit))
    return left.reshape(slots, seqs, -1, width)


def send_home(share):
    parts = lax.axis_size("ctx")
    me = lax.axis_index("ctx")
    home = jnp.stack([swap(share[k], "ctx", k) if k else share[k] for k in range(parts)])
    home = gather_cuts(home)
    home = jnp.concatenate([lax.dynamic_index_in_dim(home, me ^ k, 0) for k in range(parts)])
    return home.reshape((-1,) + home.shape[2:])


def dot(a, b, dims):
    return lax.dot_general(a, b, (dims, ((), ())), preferred_element_type=F32)


NN = ((1,), (0,))
NT = ((1,), (1,))
TN = ((0,), (0,))


def tiled(lanes, width):
    return jnp.concatenate([lanes] * (width // lanes.shape[1]), 1)


def conv_rows(raw, before, weight):
    taps = len(weight) - 1
    width = raw.shape[1]
    ext = jnp.concatenate([before, raw], 1)
    total = tiled(weight[taps], width) + tiled(weight[taps - 1], width) * raw
    for k in range(1, taps):
        total += tiled(weight[taps - 1 - k], width) * pltpu.roll(ext, k, 1)[:, LANES:]
    return total


def fold(rows):
    return sum(rows[:, i : i + LANES] for i in range(0, rows.shape[1], LANES))


def conv_back(grad, after, raw, weight, totals):
    taps = len(weight) - 1
    width = grad.shape[1]
    ext = jnp.concatenate([grad, after], 1)
    out = tiled(weight[taps - 1], width) * grad
    totals[taps][...] += fold(grad)
    totals[taps - 1][...] += fold(grad * raw)
    for k in range(1, taps):
        moved = pltpu.roll(ext, width + LANES - k, 1)[:, :width]
        out += tiled(weight[taps - 1 - k], width) * moved
        totals[taps - 1 - k][...] += fold(moved * raw)
    return out


def order_mask(width, keep):
    row = lax.broadcasted_iota(jnp.int32, (width, width), 0)
    col = lax.broadcasted_iota(jnp.int32, (width, width), 1)
    return keep(row, col)


def head_rows(dt_raw, dt_bias, a_log):
    biased = dt_raw + dt_bias
    step = jnp.maximum(biased, 0.0) + jnp.log1p(jnp.exp(-jnp.abs(biased)))
    a_decay = -jnp.exp(a_log)
    return biased, step, a_decay


def fill_heads(cs, heads, cs_ref, col_ref, ecs_ref, rem_ref, end_ref):
    width = cs.shape[1]
    cs2 = cs * LOG2E
    cs_ref[...] = cs2
    last = jnp.broadcast_to(cs2[:, width - 1 :], cs2.shape)
    ecs_ref[...] = jnp.exp2(cs2)
    rem_ref[...] = jnp.exp2(last - cs2)
    end_ref[...] = jnp.exp2(last[:, :LANES])
    columns = jnp.transpose(cs2)
    for h in range(heads):
        col_ref[h] = jnp.broadcast_to(columns[:, h : h + 1], (width, LANES))


def decay_blocks(cs_row, column):
    count = cs_row.shape[1] // LANES
    out = {}
    for i in range(count):
        for j in range(i, count):
            gap = cs_row[:, j * LANES : (j + 1) * LANES] - column[i * LANES : (i + 1) * LANES]
            out[i, j] = jnp.exp2(jnp.minimum(gap, 0.0) if i == j else gap)
    return out


def block(ref, i, j):
    return ref[i * LANES : (i + 1) * LANES, j * LANES : (j + 1) * LANES]


def mixing(decay, score_ref):
    count = score_ref.shape[0] // LANES
    none = jnp.zeros((LANES, LANES), BF)
    return jnp.concatenate(
        [
            jnp.concatenate(
                [
                    (decay[i, j] * block(score_ref, i, j)).astype(BF) if j >= i else none
                    for j in range(count)
                ],
                1,
            )
            for i in range(count)
        ],
        0,
    )


def forward_kernel(
    heads, me, raw, bc_raw, dt_raw, cw, cbw, hp,
    z_out, zbc_out, y_out, cs_out, mem_out,
    mem, before, before_bc, step_s, cs_s, col_s, ecs_s, rem_s, end_s, score_s, maps_s,
):
    head_size = raw.shape[2] // heads
    half = bc_raw.shape[2] // 2
    width = raw.shape[3]
    taps = cw.shape[0]

    @pl.when(pl.program_id(1) == 0)
    def _():
        mem[...] = jnp.zeros_like(mem)
        before[...] = jnp.zeros_like(before)
        before_bc[...] = jnp.zeros_like(before_bc)

    bc = bc_raw[0, 0].astype(F32)
    zbc = conv_rows(bc, before_bc[...], [cbw[j] for j in range(taps)])
    before_bc[...] = bc[:, width - LANES :]
    zbc_out[0, 0] = zbc
    maps_s[...] = (zbc * jax.nn.sigmoid(zbc)).astype(BF)
    causal = order_mask(width, lambda s, t: s <= t)
    score_s[...] = jnp.where(causal, dot(maps_s[:half], maps_s[half:], TN), 0.0)

    _, step, a_decay = head_rows(dt_raw[0, 0], hp[0], hp[1])
    cs = jnp.dot(step * a_decay, causal.astype(F32), precision=HIGH, preferred_element_type=F32)
    cs_out[0, 0] = cs
    step_s[...] = step
    fill_heads(cs, heads, cs_s, col_s, ecs_s, rem_s, end_s)

    def one(h, carry):
        rows = pl.ds(pl.multiple_of(h * head_size, head_size), head_size)
        row = pl.ds(h, 1)
        own = raw[0, 0, rows, :].astype(F32)
        z = conv_rows(own, before[rows, :], [cw[j, rows, :] for j in range(taps)])
        before[rows, :] = own[:, width - LANES :]
        z_out[0, 0, rows, :] = z
        x = z * jax.nn.sigmoid(z)
        scaled = x * step_s[row, :]
        decay = decay_blocks(cs_s[row, :], col_s[h])
        inside = dot(scaled.astype(BF), mixing(decay, score_s), NN)
        memory = mem[rows, :]
        memory_low = memory.astype(BF)
        mem_out[0, 0, rows, :] = memory_low
        held = dot(memory_low, maps_s[half:], NN) * ecs_s[row, :]
        y_out[0, 0, rows, :] = inside + held + hp[2, row, :] * x
        gained = dot((scaled * rem_s[row, :]).astype(BF), maps_s[:half], NT)
        mem[rows, :] = memory * end_s[row, :] + gained
        return carry

    lax.fori_loop(0, heads, one, 0)


def backward_kernel(
    heads, me, z_in, raw, y_in, g_in, zbc_in, bc_raw, dt_raw, cs_in, mem_in, cw, cbw, hp,
    gin_out, gbc_out, gdt_out, sum_x, sum_bc, sum_h,
    gmem, gmem_low, after, after_bc, step_s, cs_s, col_s, ecs_s, rem_s, end_s, score_s, maps_s,
    gscore_s, eg_s, rx_s, pq_s, e_s, r_s, d_s, k_s,
):
    head_size = raw.shape[2] // heads
    half = bc_raw.shape[2] // 2
    width = raw.shape[3]
    taps = cw.shape[0]
    count = width // LANES

    @pl.when((pl.program_id(0) == 0) & (pl.program_id(1) == 0))
    def _():
        sum_x[...] = jnp.zeros_like(sum_x)
        sum_bc[...] = jnp.zeros_like(sum_bc)
        sum_h[...] = jnp.zeros_like(sum_h)
        pq_s[...] = jnp.zeros_like(pq_s)
        e_s[...] = jnp.zeros_like(e_s)
        r_s[...] = jnp.zeros_like(r_s)
        d_s[...] = jnp.zeros_like(d_s)
        k_s[...] = jnp.zeros_like(k_s)

    @pl.when(pl.program_id(1) == 0)
    def _():
        gmem[...] = jnp.zeros_like(gmem)
        after[...] = jnp.zeros_like(after)
        after_bc[...] = jnp.zeros_like(after_bc)

    zbc = zbc_in[0, 0]
    sig_bc = jax.nn.sigmoid(zbc)
    maps_s[...] = (zbc * sig_bc).astype(BF)
    causal = order_mask(width, lambda s, t: s <= t)
    score_s[...] = jnp.where(causal, dot(maps_s[:half], maps_s[half:], TN), 0.0)
    gscore_s[...] = jnp.zeros_like(gscore_s)

    biased, step, a_decay = head_rows(dt_raw[0, 0], hp[0], hp[1])
    step_s[...] = step
    fill_heads(cs_in[0, 0], heads, cs_s, col_s, ecs_s, rem_s, end_s)

    def one(h, carry):
        rows = pl.ds(pl.multiple_of(h * head_size, head_size), head_size)
        row = pl.ds(h, 1)
        z = z_in[0, 0, rows, :]
        sig = jax.nn.sigmoid(z)
        x = z * sig
        step_row = step_s[row, :]
        skip = hp[2, row, :]
        scaled = x * step_row
        scaled_low = scaled.astype(BF)
        scaled_back = scaled_low.astype(F32)
        g_low = g_in[0, 0, rows, :]
        g = g_low.astype(F32)
        decay = decay_blocks(cs_s[row, :], col_s[h])
        inside = dot(g_low, mixing(decay, score_s), NT)
        gweights = dot(scaled_low, g_low, TN)
        for (i, j), weight in decay.items():
            place = (slice(i * LANES, (i + 1) * LANES), slice(j * LANES, (j + 1) * LANES))
            gscore_s[place] += weight * gweights[place]
        later = gmem[rows, :]
        later_low = later.astype(BF)
        gmem_low[rows, :] = later_low
        outside = dot(later_low, maps_s[:half], NN) * rem_s[row, :]
        gscaled = inside + outside
        both = g * (y_in[0, 0, rows, :] - skip * x) - scaled_back * inside
        pq_s[row, :] = jnp.sum(both, 0, keepdims=True)
        e_s[row, :] = jnp.sum(scaled_back * outside, 0, keepdims=True)
        r_s[row, :] = jnp.sum(x * gscaled, 0, keepdims=True)
        d_s[row, :] += jnp.sum(g * x, 0, keepdims=True)
        k_s[row, :] = jnp.sum(later * mem_in[0, 0, rows, :].astype(F32), 0, keepdims=True)
        eg = (g * ecs_s[row, :]).astype(BF)
        eg_s[rows, :] = eg
        rx_s[rows, :] = (scaled * rem_s[row, :]).astype(BF)
        gmem[rows, :] = later * end_s[row, :] + dot(eg, maps_s[half:], NT)
        gz = (step_row * gscaled + skip * g) * (sig * (1.0 + z * (1.0 - sig)))
        own = raw[0, 0, rows, :].astype(F32)
        grad = conv_back(
            gz, after[rows, :], own, [cw[j, rows, :] for j in range(taps)],
            [sum_x.at[j, rows, :] for j in range(taps)],
        )
        after[rows, :] = gz[:, :LANES]
        gin_out[0, 0, rows, :] = grad.astype(BF)
        return carry

    lax.fori_loop(0, heads, one, 0)

    gscore = jnp.where(causal, gscore_s[...], 0.0).astype(BF)
    gout_map = dot(maps_s[:half], gscore, NN) + dot(mem_in[0, 0], eg_s[...], TN)
    gin_map = dot(maps_s[half:], gscore, NT) + dot(gmem_low[...], rx_s[...], TN)
    gmaps = jnp.concatenate([gin_map, gout_map], 0) * (sig_bc * (1.0 + zbc * (1.0 - sig_bc)))
    gbc = conv_back(
        gmaps, after_bc[...], bc_raw[0, 0].astype(F32), [cbw[j] for j in range(taps)],
        [sum_bc.at[j] for j in range(taps)],
    )
    after_bc[...] = gmaps[:, :LANES]
    gbc_out[0, 0] = gbc.astype(BF)

    from_here = order_mask(width, lambda t, u: t >= u).astype(F32)
    strictly = order_mask(width, lambda s, u: s < u).astype(F32)
    carried = jnp.sum(k_s[...], 1, keepdims=True) * end_s[:, :1]
    gdecay = (
        jnp.dot(pq_s[...], from_here, precision=HIGH, preferred_element_type=F32)
        + jnp.dot(e_s[...], strictly, precision=HIGH, preferred_element_type=F32)
        + carried
    )
    gdt = (a_decay * gdecay + r_s[...]) * jax.nn.sigmoid(biased)
    gdt_out[0, 0] = gdt
    sum_h[0] += fold(gdt)
    sum_h[1] += fold(gdecay * step * a_decay)

    @pl.when((pl.program_id(0) == pl.num_programs(0) - 1) & (pl.program_id(1) == pl.num_programs(1) - 1))
    def _():
        sum_h[2] = fold(d_s[...])


def run_forward(inner, bc, dt, cw, cbw, hp, heads):
    parts, seqs, rows, width = inner.shape
    maps, head_pad, states = bc.shape[2], dt.shape[2], bc.shape[2] // 2

    def part(count, last=width):
        return pl.BlockSpec((1, 1, count, last), lambda s, c, me: (c ^ me[0], s, 0, 0))

    def fixed(shape):
        return pl.BlockSpec(shape, lambda s, c, me: (0,) * len(shape))

    def shape(count, last=width, kind=F32):
        return jax.ShapeDtypeStruct((parts, seqs, count, last), kind)

    return pl.pallas_call(
        partial(forward_kernel, heads),
        grid_spec=pltpu.PrefetchScalarGridSpec(
            num_scalar_prefetch=1,
            grid=(seqs, parts),
            in_specs=[part(rows), part(maps), part(head_pad), fixed(cw.shape), fixed(cbw.shape), fixed(hp.shape)],
            out_specs=[part(rows), part(maps), part(rows), part(head_pad), part(rows, states)],
            scratch_shapes=[
                pltpu.VMEM((rows, states), F32),
                pltpu.VMEM((rows, LANES), F32),
                pltpu.VMEM((maps, LANES), F32),
                pltpu.VMEM((head_pad, width), F32),
                pltpu.VMEM((head_pad, width), F32),
                pltpu.VMEM((heads, width, LANES), F32),
                pltpu.VMEM((head_pad, width), F32),
                pltpu.VMEM((head_pad, width), F32),
                pltpu.VMEM((head_pad, LANES), F32),
                pltpu.VMEM((width, width), F32),
                pltpu.VMEM((maps, width), BF),
            ],
        ),
        out_shape=[
            shape(rows),
            shape(maps),
            shape(rows),
            shape(head_pad),
            shape(rows, states, BF),
        ],
        compiler_params=pltpu.CompilerParams(
            dimension_semantics=("arbitrary", "arbitrary"), vmem_limit_bytes=48 << 20
        ),
        cost_estimate=pl.CostEstimate(flops=4 << 30, bytes_accessed=32 << 20, transcendentals=0),
        name="scan_forward",
    )(lax.axis_index("ctx").reshape(1), inner, bc, dt, cw, cbw, hp)


def run_backward(z, inner, y, g, zbc, bc, dt, cs, mem, cw, cbw, hp, heads):
    parts, seqs, rows, width = inner.shape
    maps, head_pad, states = bc.shape[2], dt.shape[2], bc.shape[2] // 2

    def part(count, last=width):
        return pl.BlockSpec(
            (1, 1, count, last), lambda s, c, me: ((parts - 1 - c) ^ me[0], s, 0, 0)
        )

    def fixed(shape):
        return pl.BlockSpec(shape, lambda s, c, me: (0,) * len(shape))

    def shape(count, kind=F32):
        return jax.ShapeDtypeStruct((parts, seqs, count, width), kind)

    return pl.pallas_call(
        partial(backward_kernel, heads),
        grid_spec=pltpu.PrefetchScalarGridSpec(
            num_scalar_prefetch=1,
            grid=(seqs, parts),
            in_specs=[
                part(rows), part(rows), part(rows), part(rows), part(maps), part(maps),
                part(head_pad), part(head_pad), part(rows, states),
                fixed(cw.shape), fixed(cbw.shape), fixed(hp.shape),
            ],
            out_specs=[
                part(rows), part(maps), part(head_pad),
                fixed(cw.shape), fixed(cbw.shape), fixed((3, head_pad, LANES)),
            ],
            scratch_shapes=[
                pltpu.VMEM((rows, states), F32),
                pltpu.VMEM((rows, states), BF),
                pltpu.VMEM((rows, LANES), F32),
                pltpu.VMEM((maps, LANES), F32),
                pltpu.VMEM((head_pad, width), F32),
                pltpu.VMEM((head_pad, width), F32),
                pltpu.VMEM((heads, width, LANES), F32),
                pltpu.VMEM((head_pad, width), F32),
                pltpu.VMEM((head_pad, width), F32),
                pltpu.VMEM((head_pad, LANES), F32),
                pltpu.VMEM((width, width), F32),
                pltpu.VMEM((maps, width), BF),
                pltpu.VMEM((width, width), F32),
                pltpu.VMEM((rows, width), BF),
                pltpu.VMEM((rows, width), BF),
                pltpu.VMEM((head_pad, width), F32),
                pltpu.VMEM((head_pad, width), F32),
                pltpu.VMEM((head_pad, width), F32),
                pltpu.VMEM((head_pad, width), F32),
                pltpu.VMEM((head_pad, LANES), F32),
            ],
        ),
        out_shape=[
            shape(rows, BF),
            shape(maps, BF),
            shape(head_pad),
            jax.ShapeDtypeStruct(cw.shape, F32),
            jax.ShapeDtypeStruct(cbw.shape, F32),
            jax.ShapeDtypeStruct((3, head_pad, LANES), F32),
        ],
        compiler_params=pltpu.CompilerParams(
            dimension_semantics=("arbitrary", "arbitrary"), vmem_limit_bytes=48 << 20
        ),
        cost_estimate=pl.CostEstimate(flops=8 << 30, bytes_accessed=48 << 20, transcendentals=0),
        name="scan_backward",
    )(lax.axis_index("ctx").reshape(1), z, inner, y, g, zbc, bc, dt, cs, mem, cw, cbw, hp)


def project(rows, weight):
    return jnp.einsum("ksld,di->ksil", rows, weight, preferred_element_type=F32)


def project_back(grad, weight):
    return jnp.einsum("ksil,di->ksld", grad, weight, preferred_element_type=F32)


def weight_grad(rows, grad):
    return jnp.einsum("ksld,ksil->di", rows, grad, preferred_element_type=F32)


def per_device(
    tokens, norm_gain, w_zx, w_dt, w_bc, conv_x_w, conv_x_b, conv_bc_w, conv_bc_b,
    dt_bias, a_log, d_skip, norm_w, w_out, output_gradient,
):
    seqs_here, length, width = tokens.shape
    heads = w_dt.shape[1]
    head_pad = -(-heads // 8) * 8
    inner_here = w_out.shape[1]
    inner_total = inner_here * lax.axis_size("tensor")
    maps = w_bc.shape[1]
    dp_bits = [("dp", b) for b in bits_of("dp")]
    ctx_bits = [("ctx", b) for b in bits_of("ctx")]
    tensor_bits = [("tensor", b) for b in bits_of("tensor")]

    small = jnp.concatenate(
        [
            w_bc,
            jnp.pad(w_dt, ((0, 0), (0, head_pad - heads))),
            norm_gain[:, None],
            jnp.zeros((w_bc.shape[0], LANES - head_pad - 1), BF),
        ],
        1,
    )
    small = gather_rows(small, dp_bits + ctx_bits)
    full_bc = small[:, :maps]
    full_dt = small[:, maps : maps + head_pad]
    gain = small[:, maps + head_pad].astype(F32)
    full_inner = gather_rows(w_zx[:, 1], dp_bits + ctx_bits)
    rows = spread_out(tokens, length)
    full_out = gather_rows(w_out, dp_bits + ctx_bits[::-1])
    cots = spread_out(output_gradient, length)
    full_gate = gather_rows(w_zx[:, 0], dp_bits + ctx_bits)

    residual = rows.astype(F32)
    normed = (
        residual * lax.rsqrt(jnp.mean(residual * residual, axis=-1, keepdims=True) + EPS) * gain
    ).astype(BF)
    bc_raw = project(normed, full_bc).astype(BF)
    dt_raw = project(normed, full_dt)
    inner_raw = project(normed, full_inner).astype(BF)

    def lanes(column):
        return jnp.broadcast_to(column[..., None], column.shape + (LANES,))

    cw = lanes(jnp.concatenate([conv_x_w, conv_x_b[None]], 0))
    cbw = lanes(jnp.concatenate([conv_bc_w, conv_bc_b[None]], 0))
    hp = jnp.pad(jnp.stack([dt_bias, a_log, d_skip]), ((0, 0), (0, head_pad - heads)))
    hp = jnp.broadcast_to(hp[..., None], hp.shape + (length,))

    z, zbc, y, cs, mem = run_forward(inner_raw, bc_raw, dt_raw, cw, cbw, hp, heads)

    gate_raw = project(normed, full_gate)
    grad_mixed = project(cots, full_out)
    gate_sig = jax.nn.sigmoid(gate_raw)
    gate_act = gate_raw * gate_sig
    gated = y * gate_act
    norm_column = norm_w[:, None]
    weighted = grad_mixed * norm_column
    sums = jnp.stack([jnp.sum(gated * gated, axis=2), jnp.sum(weighted * gated, axis=2)])
    sums = sum_over(sums, tensor_bits)[:, :, :, None]
    inv_rms = lax.rsqrt(sums[0] / inner_total + EPS)
    mixed_in = (gated * inv_rms * norm_column).astype(BF)
    grad_norm_w = jnp.sum(grad_mixed * gated * inv_rms, axis=(0, 1, 3))
    grad_gated = inv_rms * weighted - gated * (inv_rms * inv_rms * inv_rms) * (
        sums[1] / inner_total
    )
    grad_gate = (grad_gated * y * gate_sig * (1.0 + gate_raw * (1.0 - gate_sig))).astype(BF)
    grad_y = (grad_gated * gate_act).astype(BF)

    grad_inner, grad_bc, grad_dt, sum_x, sum_bc, sum_h = run_backward(
        z, inner_raw, y, grad_y, zbc, bc_raw, dt_raw, cs, mem, cw, cbw, hp, heads
    )

    grad_w_out = scatter_rows(weight_grad(cots, mixed_in), ctx_bits + dp_bits[::-1])
    mixed = cut_sum(project_back(mixed_in, full_out))
    cuts = lax.axis_size("tensor")
    share = lax.dynamic_slice_in_dim(
        rows, lax.axis_index("tensor") * (length // cuts), length // cuts, 2
    )
    mixed_out = send_home((share.astype(F32) + mixed).astype(BF))
    grad_w_gate = scatter_rows(weight_grad(normed, grad_gate), ctx_bits[::-1] + dp_bits[::-1])

    grad_dt_low = grad_dt.astype(BF)
    grad_normed = (
        project_back(grad_gate, full_gate)
        + project_back(grad_inner, full_inner)
        + project_back(grad_dt_low, full_dt)
        + project_back(grad_bc, full_bc)
    )
    grad_home = send_home(cut_sum(grad_normed).astype(BF)).astype(F32)

    grad_w_inner = scatter_rows(weight_grad(normed, grad_inner), ctx_bits + dp_bits[::-1])
    grad_small = jnp.concatenate(
        [weight_grad(normed, grad_bc), weight_grad(normed, grad_dt_low)[:, :heads]], 1
    )
    grad_small = scatter_rows(grad_small, ctx_bits[::-1] + dp_bits[::-1])
    grad_w_bc = sum_over(grad_small[:, :maps], tensor_bits)
    grad_w_dt = grad_small[:, maps:]

    here = tokens.astype(F32)
    r = lax.rsqrt(jnp.mean(here * here, axis=-1, keepdims=True) + EPS)
    scaled = gain * grad_home
    grad_tokens = (
        output_gradient.astype(F32)
        + r * scaled
        - here * (r * r * r) * jnp.mean(here * scaled, axis=-1, keepdims=True)
    )
    grad_gain = jnp.sum(here * r * grad_home, axis=(0, 1))

    sum_x = jnp.sum(sum_x, -1)
    sum_bc = jnp.sum(sum_bc, -1)
    sum_h = jnp.sum(sum_h, -1)[:, :heads]
    pieces = [sum_x, grad_norm_w, sum_h, grad_gain]
    flat = jnp.concatenate([p.reshape(-1) for p in pieces] + [sum_bc.reshape(-1)])
    size = flat.shape[0]
    flat = jnp.pad(flat, (0, -size % 1024)).reshape(-1, LANES)
    flat = sum_over(flat, ctx_bits + dp_bits).reshape(-1)[:size]
    out = []
    for p in pieces + [sum_bc]:
        out.append(flat[: p.size].reshape(p.shape))
        flat = flat[p.size :]
    sum_x, grad_norm_w, sum_h, grad_gain, sum_bc = out
    sum_bc = sum_over(sum_bc, tensor_bits)
    taps = conv_x_w.shape[0]
    row = lax.axis_index("dp") * lax.axis_size("ctx") + lax.axis_index("ctx")
    grad_gain = lax.dynamic_slice_in_dim(
        grad_gain, row * norm_gain.shape[0], norm_gain.shape[0], 0
    )
    return (
        mixed_out,
        grad_tokens,
        grad_gain,
        jnp.stack([grad_w_gate, grad_w_inner], 1),
        grad_w_dt,
        grad_w_bc,
        sum_x[:taps],
        sum_x[taps],
        sum_bc[:taps],
        sum_bc[taps],
        sum_h[0],
        sum_h[1],
        sum_h[2],
        grad_norm_w,
        grad_w_out,
    )


def solution(mesh):
    rows = P(("dp", "ctx"), "tensor")
    tokens = P("dp", "ctx", None)
    heads = P("tensor")
    return jax.shard_map(
        per_device,
        mesh=mesh,
        in_specs=(
            tokens, P(("dp", "ctx")), P(("dp", "ctx"), None, "tensor"), rows, P(("dp", "ctx"), None),
            P(None, "tensor"), heads, P(), P(), heads, heads, heads, heads, rows, tokens,
        ),
        out_specs=(
            tokens, tokens, P(("dp", "ctx")), P(("dp", "ctx"), None, "tensor"), rows,
            P(("dp", "ctx"), None), P(None, "tensor"), heads, P(), P(), heads, heads, heads, heads, rows,
        ),
        check_vma=False,
    )
```

time: 1460 us -> 587 us (0.40)
  waiting for transfers between devices: 535 us -> 159 us
  matrix products: 373 us -> 91.7 us
  blocking collectives: 181 us -> 0 us
  other arithmetic: 219 us -> 76.1 us
  Pallas kernels: 0 us -> 116 us
  starting transfers between devices: 9.23 us -> 78.5 us
  local copies, waits for them, and re-layouts: 108 us -> 54 us
    dot_general x28 -> x15, matrix products: 373 us -> 91.7 us  [the longest x5 33.5 us: project(): return jnp.einsum('ksld,di->ksil', rows, weight, preferred_element_type=F32)]
    all_gather x4 -> x0, waiting for transfers between devices: 257 us -> none  [the longest x2 237 us: carried_in(): gathered = jax.tree.map(lambda a: lax.all_gather(a, axis), part)]
    reduce_scatter x2 -> x0, waiting for transfers between devices: 192 us -> none  [the longest x1 192 us: per_device(): lax.psum_scatter(grad_zx_part, ('dp', 'ctx'), scatter_dimension=0, tiled=...]
    ppermute x4 -> x57, waiting for transfers between devices: 0.01 us -> 159 us  [swap(): lax.ppermute(block, axis, [(i, i ^ mask) for i in range(lax.axis_size(axi...]
    pallas_call x0 -> x2, Pallas kernels: none -> 116 us  [the longest x1 68.3 us: run_backward(): pl.pallas_call(partial(backward_kernel, heads), grid_spec=pltpu.PrefetchS...]
    unnamed x2 -> x0, blocking collectives: 89 us -> none
    all_gather x3 -> x0, blocking collectives: 70.9 us -> none  [the longest x1 37.7 us: per_device(): lax.all_gather(w_bc, ('dp', 'ctx'), axis=0, tiled=True)]
    ppermute x4 -> x57, starting transfers between devices: 8.41 us -> 78.5 us  [swap(): lax.ppermute(block, axis, [(i, i ^ mask) for i in range(lax.axis_size(axi...]
  transfers between devices with their start and end apart: 13 -> 57, of which waited for: 7 -> 25; matrix products, arithmetic and copies ran while one was open for 24% -> 24% of each run, Pallas kernels for 0% -> 8%
where the time goes in v1:
time: 587 us; the launch traced here: 577 us
  waiting for transfers between devices  159 us (27%)
  Pallas kernels  116 us (20%)
  matrix products  91.7 us (16%)
  starting transfers between devices  78.5 us (13%)
  other arithmetic  76.1 us (13%)
  local copies, waits for them, and re-layouts  54 us (9%)
    ppermute x57, waiting for transfers between devices, swap(): lax.ppermute(block, axis, [(i, i ^ mask) for i in range(lax.axis_size(axi...  159 us
    ppermute x57, starting transfers between devices, swap(): lax.ppermute(block, axis, [(i, i ^ mask) for i in range(lax.axis_size(axi...  78.5 us
    pallas_call x1, Pallas kernels, run_backward(): pl.pallas_call(partial(backward_kernel, heads), grid_spec=pltpu.PrefetchS...  68.3 us
    pallas_call x1, Pallas kernels, run_forward(): pl.pallas_call(partial(forward_kernel, heads), grid_spec=pltpu.PrefetchSc...  48 us
    dot_general x5, matrix products, project(): return jnp.einsum('ksld,di->ksil', rows, weight, preferred_element_type=F32)  33.5 us
    dot_general x5, matrix products, project_back(): return jnp.einsum('ksil,di->ksld', grad, weight, preferred_element_type=F32)  33.2 us
    dot_general x5, matrix products, weight_grad(): return jnp.einsum('ksld,ksil->di', rows, grad, preferred_element_type=F32)  25.1 us
    convert_element_type x1, other arithmetic, per_device(): (grad_gated * y * gate_sig * (1.0 + gate_raw * (1.0 - gate_sig))).astype(BF)  16.9 us
  transfers between devices with their start and end apart: 57, of which 25 were waited for; matrix products, arithmetic and copies ran while one was open for 24% of the time, Pallas kernels for 8%

profile of v1, /device:TPU:9, one launch (start us, length us, event | category | flops | bytes accessed | tf_op | source)
XLA Modules:
  0.0 577.4 jit_solution(7597047501360828669)
XLA Ops:
  12.0 3.1 fusion.7
  22.0 6.2 %collective-permute-done.12 = bf16[1,1,1,1,64,1024]{5,4,0,1,3,2:T(8,128)(2,1)S(1)} collective-permute-done((bf16[1,1,1,1,64,1024]{5,4,0,1,3,2:T(8,128)(2,1)S(1)}, bf16[1,1,1,1,64,1024]{5,4,0,1,3,2:T(8,128)(2,1)S(1)}, u32[]{:S(2)}, u32[]{:S(2)}) %collective-permute-start.12) | collective-permute-done | bytes 131104 | tf_op jit(solution)/shard_map/ppermute | solution.py:23
  33.7 3.7 collective-permute-done.10
  37.4 3.3 collective-permute-start.13
  41.0 4.8 collective-permute-done.13
  45.9 5.5 collective-permute-done.17
  54.5 3.8 collective-permute-start.3
  62.9 4.2 collective-permute-done.18
  67.2 16.3 %collective-permute-done.6 = bf16[2,2,1,1,64,1024]{5,4,3,2,1,0:T(8,128)(2,1)S(1)} collective-permute-done((bf16[2,2,1,1,64,1024]{5,4,3,2,1,0:T(8,128)(2,1)S(1)}, bf16[2,2,1,1,64,1024]{5,4,3,2,1,0:T(8,128)(2,1)S(1)}, u32[]{:S(2)}, u32[]{:S(2)}) %collective-permute-start.6) | collective-permute-done | bytes 524320 | tf_op jit(solution)/shard_map/ppermute | solution.py:23
  83.7 12.6 %collective-permute-done.21 = bf16[2,128,1024]{2,1,0:T(8,128)(2,1)S(1)} collective-permute-done((bf16[2,128,1024]{2,1,0:T(8,128)(2,1)S(1)}, bf16[2,128,1024]{2,1,0:T(8,128)(2,1)S(1)}, u32[]{:S(2)}, u32[]{:S(2)}) %collective-permute-start.21) | collective-permute-done | bytes 524320 | tf_op jit(solution)/shard_map/ppermute | solution.py:23
  99.5 9.7 %collective-permute-done.11 = bf16[2,2,2,1,64,384]{5,4,3,2,1,0:T(8,128)(2,1)S(1)} collective-permute-done((bf16[2,2,2,1,64,384]{5,4,3,2,1,0:T(8,128)(2,1)S(1)}, bf16[2,2,2,1,64,384]{5,4,3,2,1,0:T(8,128)(2,1)S(1)}, u32[]{:S(2)}, u32[]{:S(2)}) %collective-permute-start.11) | collective-permute-done | bytes 393248 | tf_op jit(solution)/shard_map/ppermute | solution.py:23
  109.2 8.3 %collective-permute-start.23 = (bf16[4,2,128,1024]{3,2,1,0:T(8,128)(2,1)}, bf16[4,2,128,1024]{3,2,1,0:T(8,128)(2,1)}, u32[]{:S(2)}, u32[]{:S(2)}) collective-permute-start(bf16[4,2,128,1024]{3,2,1,0:T(8,128)(2,1)} %pad_maximum_fusion.3), channel_id=1, source_target_pairs={{0,1},{1,0},{2,3},{3,2},{4,5},{5,4},{6,7},{7,6},{8,9},{9,8},{10,11... | collective-permute-start | bytes 6291464 | tf_op jit(solution)/shard_map/ppermute | solution.py:23
  121.8 9.9 %collective-permute-done.7 = bf16[2,2,2,1,64,1024]{5,4,3,2,1,0:T(8,128)(2,1)S(1)} collective-permute-done((bf16[2,2,2,1,64,1024]{5,4,3,2,1,0:T(8,128)(2,1)S(1)}, bf16[2,2,2,1,64,1024]{5,4,3,2,1,0:T(8,128)(2,1)S(1)}, u32[]{:S(2)}, u32[]{:S(2)}) %collective-permute-start.7) | collective-permute-done | bytes 1048608 | tf_op jit(solution)/shard_map/ppermute | solution.py:23
  131.9 4.3 fusion.3
  138.1 6.5 %convert_bitcast_fusion.raw = bf16[4,2,1024,256]{3,2,1,0:T(8,128)(2,1)} fusion(bf16[1024,1024,1,1]{1,0,3,2:T(8,128)(2,1)S(1)} %bitcast.357, bf16[4,2,256,1024]{3,2,1,0:T(8,128)(2,1)S(1)} %get-tuple-element.88, f32[1024]{0:T(1024)S(1)} %convert_reduce_fusion, f32[4,2,256]{2,1,0:T(2,128)S(1)} %add_rsqrt_fusion.1), kind=kOutput, calls=%fused_computation.49 | convolution fusion | flops 4305453056 | bytes 10498048 | tf_op jit(solution)/shard_map/ksld,di->ksil/dot_general | solution.py:499
  148.1 48.0 %scan_forward.1 = (f32[4,2,1024,256]{3,2,1,0:T(8,128)}, f32[4,2,256,256]{3,2,1,0:T(8,128)S(1)}, f32[4,2,1024,256]{3,2,1,0:T(8,128)}, f32[4,2,16,256]{3,2,1,0:T(8,128)S(1)}, bf16[4,2,1024,128]{3,2,1,0:T(8,128)(2,1)S(1)}) custom-call(s32[1]{0:T(128)} %bitcast.7.me, bf16[4,2,1024,256]{3,2,1,0:T(8,128)(2,1)} %convert_bitcast_fusion.raw, ...), custom_call_target="tpu_custom_call" | custom-call | flops 4294967296 | bytes 33554432 | tf_op jit(solution)/shard_map/scan_forward/pallas_call | solution.py:394
  196.1 7.2 %fusion.62 = f32[1024,4,2,256]{3,0,2,1:T(8,128)} fusion(bf16[1024,1024,1,1]{1,0,3,2:T(8,128)(2,1)S(1)} %bitcast.380, bf16[4,2,256,1024]{3,2,1,0:T(8,128)(2,1)S(1)} %get-tuple-element.88, f32[1024]{0:T(1024)S(1)} %convert_reduce_fusion, f32[4,2,256]{2,1,0:T(2,128)S(1)} %add_rsqrt_fusion.1), kind=kOutput, calls=%fused_computation.212 | convolution fusion | flops 4303355904 | bytes 14692352 | tf_op jit(solution)/shard_map/ksld,di->ksil/dot_general | solution.py:499
  203.4 16.7 %multiply_reduce_fusion.1 = (f32[4,2,256]{2,1,0:T(2,128)S(1)}, f32[4,2,256]{2,1,0:T(2,128)S(1)}, f32[4,2,1024,256]{3,2,1,0:T(8,128)}, f32[1024,4,2,256]{3,0,2,1:T(8,128)}) fusion(f32[1024]{0:T(1024)S(1)} %copy-done.46, f32[4,2,1024,256]{3,2,1,0:T(8,128)} %get-tuple-element.26.y_in, f32[1024,4,2,256]{3,0,2,1:T(8,128)} %fusion.62, ...), kind=kOutput, calls=%fused_computation.36 | convolution fusion | flops 4359974912 | bytes 39866368 | tf_op jit(solution)/shard_map/ksld,di->ksil/dot_general | solution.py:499
  220.1 4.4 collective-permute-start.24
  225.4 16.9 %fusion.17 = (bf16[4,2,1024,256]{3,2,1,0:T(8,128)(2,1)}, bf16[4,2,1024,256]{3,2,1,0:T(8,128)(2,1)}, f32[1024]{0:T(1024)S(1)}, bf16[4,2,256,1024]{2,3,1,0:T(8,128)(2,1)}) fusion(f32[1024,4,2,256]{3,0,2,1:T(8,128)} %fusion.62, f32[4,2,1024,256]{3,2,1,0:T(8,128)} %get-tuple-element.26.y_in, f32[4,2,256]{2,1,0:T(2,128)S(1)} %get-tuple-element.141, ...), kind=kLoop, calls=%fused_computation.30 | loop fusion | flops 50330624 | bytes 46170112 | tf_op jit(solution)/shard_map/convert_element_type | solution.py:576
  242.3 68.3 %scan_backward.1 = (bf16[4,2,1024,256]{3,2,1,0:T(8,128)(2,1)}, bf16[4,2,256,256]{3,2,1,0:T(8,128)(2,1)S(1)}, f32[4,2,16,256]{3,2,1,0:T(8,128)S(1)}, f32[5,1024,1...) custom-call(s32[1]{0:T(128)} %bitcast.7.me, f32[4,2,1024,256]{3,2,1,0:T(8,128)} %get-tuple-element.27.z_in, ...), custom_call_target="tpu_custom_call" | custom-call | flops 8589934592 | bytes 50331648 | tf_op jit(solution)/shard_map/scan_backward/pallas_call | solution.py:445
  315.3 4.7 fusion.31
  322.8 6.9 %fusion.72 = f32[4,2,256,1024]{3,2,1,0:T(8,128)} fusion(bf16[4,2,1024,256]{3,2,1,0:T(8,128)(2,1)S(1)} %copy-done.22, bf16[1024,1024,1,1]{1,0,3,2:T(8,128)(2,1)S(1)} %bitcast.381), kind=kOutput, calls=%fused_computation.217 | convolution fusion | flops 4294967296 | bytes 14680064 | tf_op jit(solution)/shard_map/ksil,di->ksld/dot_general | solution.py:503
  329.8 7.3 %fusion.60 = f32[1024,1024,1,1]{1,0,3,2:T(8,128)} fusion(bf16[4,2,1024,256]{3,2,1,0:T(8,128)(2,1)S(1)} %copy-done.22, bf16[4,2,256,1024]{3,2,1,0:T(8,128)(2,1)S(1)} %copy-done.12, f32[1024]{0:T(1024)S(1)} %convert_reduce_fusion, f32[4,2,256]{2,1,0:T(2,128)S(1)} %copy-done.45), kind=kOutput, calls=%fused_computation.211 | convolution fusion | flops 4303355904 | bytes 12595200 | tf_op jit(solution)/shard_map/ksld,ksil->di/dot_general | solution.py:507
  337.1 9.2 %fusion.54 = f32[1024,1024,1,1]{1,0,3,2:T(8,128)} fusion(f32[4,2,1024,256]{3,2,1,0:T(8,128)S(1)} %bitcast.356, f32[4,2,256]{2,1,0:T(2,128)S(1)} %get-tuple-element.142, f32[1024]{0:T(1024)S(1)} %copy-done.46, bf16[1,2,128,1024]{3,2,1,0:T(8,128)(2,1)} %bitcast.424, bf16[1,2,128,1024]{3,2,1,0:T(8,128)(2,1)} %bitcast.421, ...), kind=kOutput, calls=%fused_computation.208 | convolution fusion | flops 4345298944 | bytes 16789504 | tf_op jit(solution)/shard_map/ksld,ksil->di/dot_general | solution.py:507
  349.4 12.7 %add_add_fusion = f32[4,2,256,1024]{3,2,1,0:T(8,128)} fusion(f32[4,2,256,1024]{3,2,1,0:T(8,128)S(1)} %fusion.25, f32[4,2,256,1024]{3,2,1,0:T(8,128)} %fusion.31, f32[4,2,256,1024]{3,2,1,0:T(8,128)} %fusion.72, bf16[4,2,1024,256]{3,2,1,0:T(8,128)(2,1)} %get-tuple-element.31, bf16[1024,1024,1,1]{1,0,3,2:T(8,128)(2,1)S(1)} %bitcast.358), kind=kOutput, calls=%fused_computation.31 | convolution fusion | flops 4301258752 | bytes 39845888 | tf_op jit(solution)/shard_map/ksil,di->ksld/dot_general | solution.py:503
  362.1 3.9 bitcast_convert_fusion
  373.3 6.2 %copy.206 = bf16[4,2,256,1024]{3,2,1,0:T(8,128)(2,1)} copy(bf16[4,2,256,1024]{2,3,1,0:T(8,128)(2,1)} %get-tuple-element.92) | data formatting | bytes 8388608 | tf_op jit(solution)/shard_map/ksil,di->ksld/dot_general | solution.py:503
  379.5 7.6 %fusion.71 = f32[4,2,2,128,1024]{4,3,2,1,0:T(8,128)S(1)} fusion(bf16[4,2,2,128,1024]{4,3,2,1,0:T(8,128)(2,1)} %bitcast.371, bf16[1024,1024,1,1,1]{1,0,4,3,2:T(8,128)(2,1)} %bitcast.379), kind=kOutput, calls=%fused_computation.216 | convolution fusion | flops 4294967296 | bytes 14680064 | tf_op jit(solution)/shard_map/ksil,di->ksld/dot_general | solution.py:503
  387.1 5.1 fusion.58
  394.6 4.8 collective-permute-done.48
  407.7 3.6 collective-permute-start.51
  415.4 3.3 copy.228
  425.7 3.5 copy_add_fusion.1
  430.7 12.9 %collective-permute-done.43 = bf16[2,2,1,2,64,1024]{5,0,4,3,2,1:T(2,128)(2,1)S(1)} collective-permute-done((bf16[2,2,1,2,64,1024]{5,0,4,3,2,1:T(2,128)(2,1)}, bf16[2,2,1,2,64,1024]{5,0,4,3,2,1:T(2,128)(2,1)S(1)}, u32[]{:S(2)}, u32[]{:S(2)}) %collective-permute-start.43) | collective-permute-done | bytes 1048608 | tf_op jit(solution)/shard_map/ppermute | solution.py:23
  449.6 5.3 collective-permute-done.40
  455.5 3.2 collective-permute-done.44
  467.0 6.4 %collective-permute-done.31 = bf16[2,128,1024]{2,1,0:T(8,128)(2,1)S(1)} collective-permute-done((bf16[2,128,1024]{2,1,0:T(8,128)(2,1)S(1)}, bf16[2,128,1024]{2,1,0:T(8,128)(2,1)S(1)}, u32[]{:S(2)}, u32[]{:S(2)}) %collective-permute-start.31) | collective-permute-done | bytes 524320 | tf_op jit(solution)/shard_map/ppermute | solution.py:23
  476.6 8.9 %collective-permute-done.33 = bf16[2,128,1024]{2,1,0:T(8,128)(2,1)S(1)} collective-permute-done((bf16[2,128,1024]{2,1,0:T(8,128)(2,1)S(1)}, bf16[2,128,1024]{2,1,0:T(8,128)(2,1)S(1)}, u32[]{:S(2)}, u32[]{:S(2)}) %collective-permute-start.33) | collective-permute-done | bytes 524320 | tf_op jit(solution)/shard_map/ppermute | solution.py:23
  485.8 5.4 collective-permute-start.34
  494.8 15.1 %collective-permute-done.42 = bf16[1,1,1,1,64,1024]{5,0,4,3,2,1:T(2,128)(2,1)S(1)} collective-permute-done((bf16[1,1,1,1,64,1024]{5,0,4,3,2,1:T(2,128)(2,1)S(1)}, bf16[1,1,1,1,64,1024]{5,0,4,3,2,1:T(2,128)(2,1)S(1)}, u32[]{:S(2)}, u32[]{:S(2)}) %collective-permute-start.42) | collective-permute-done | bytes 131104 | tf_op jit(solution)/shard_map/ppermute | solution.py:23
  518.2 17.6 %collective-permute-done.27 = bf16[2,128,1024]{2,1,0:T(8,128)(2,1)S(1)} collective-permute-done((bf16[2,128,1024]{2,1,0:T(8,128)(2,1)S(1)}, bf16[2,128,1024]{2,1,0:T(8,128)(2,1)S(1)}, u32[]{:S(2)}, u32[]{:S(2)}) %collective-permute-start.27) | collective-permute-done | bytes 524320 | tf_op jit(solution)/shard_map/ppermute | solution.py:23
  536.1 2.9 collective-permute-start.29
  542.4 3.1 copy-done.7
  545.5 4.5 fusion.6
  550.4 5.0 maximum_select_fusion.2
  556.3 6.3 %fusion.2 = f32[8,256,1024]{2,1,0:T(8,128)} fusion(bf16[8,256,1024]{2,1,0:T(8,128)(2,1)S(1)} %copy-done.8, bf16[8,256,1024]{2,1,0:T(8,128)(2,1)} %param.29, bf16[4,2,256,1024]{3,2,1,0:T(8,128)(2,1)S(1)} %copy-done.10, f32[8,256]{1,0:T(8,128)S(1)} %broadcast_multiply_fusion, f32[8,256]{1,0:T(8,128)S(1)} %get-tuple-element.143, ...), kind=kLoop, calls=%fused_computation.10 | loop fusion | flops 18874368 | bytes 21000192 | tf_op jit(solution)/shard_map/sub | solution.py:613
  562.6 3.2 collective-permute-start.37
  (349 shorter events, 132.8 us)
Async XLA Ops:
  4.8 46.7 %collective-permute-start = (bf16[2,128,1024]{2,1,0:T(8,128)(2,1)}, bf16[2,128,1024]{2,1,0:T(8,128)(2,1)S(1)}, u32[]{:S(2)}, u32[]{:S(2)}) collective-permute-start(bf16[2,128,1024]{2,1,0:T(8,128)(2,1)} %get-tuple-element.112), channel_id=1, source_target_pairs={{0,2},{2,0},{4,6},{6,4},{1,3},{3,1},{5,7},{7,5},{8,10},{10,8},{12,... | collective-permute-start | bytes 1572872 | tf_op jit(solution)/shard_map/ppermute | solution.py:23
  6.0 47.1 %collective-permute-start.1 = (bf16[2,128,1024]{2,1,0:T(8,128)(2,1)}, bf16[2,128,1024]{2,1,0:T(8,128)(2,1)}, u32[]{:S(2)}, u32[]{:S(2)}) collective-permute-start(bf16[2,128,1024]{2,1,0:T(8,128)(2,1)} %get-tuple-element.111), channel_id=1, source_target_pairs={{0,4},{2,6},{4,0},{6,2},{1,5},{3,7},{5,1},{7,3},{8,12},{10,14},{12... | collective-permute-start | bytes 1572872 | tf_op jit(solution)/shard_map/ppermute | solution.py:23
  7.2 45.8 %collective-permute-start.2 = (bf16[2,128,1024]{2,1,0:T(8,128)(2,1)}, bf16[2,128,1024]{2,1,0:T(8,128)(2,1)}, u32[]{:S(2)}, u32[]{:S(2)}) collective-permute-start(bf16[2,128,1024]{2,1,0:T(8,128)(2,1)} %get-tuple-element.110), channel_id=1, source_target_pairs={{0,6},{2,4},{4,2},{6,0},{1,7},{3,5},{5,3},{7,1},{8,14},{10,12},{12... | collective-permute-start | bytes 1572872 | tf_op jit(solution)/shard_map/ppermute | solution.py:23
  8.5 9.1 %collective-permute-start.8 = (bf16[1,1,1,1,64,384]{5,4,0,3,2,1:T(8,128)(2,1)}, bf16[1,1,1,1,64,384]{5,4,0,3,2,1:T(8,128)(2,1)}, u32[]{:S(2)}, u32[]{:S(2)}) collective-permute-start(bf16[1,1,1,1,64,384]{5,4,0,3,2,1:T(8,128)(2,1)} %get-tuple-element.135), channel_id=1, source_target_pairs={{0,16},{8,24},{16,0},{24,8},{1,17},{9,25},{17,1},{25,9},{2,18},{10... | collective-permute-start | bytes 147464 | tf_op jit(solution)/shard_map/ppermute | solution.py:23
  11.9 9.9 %collective-permute-start.4 = (bf16[1,1,1,1,64,1024]{5,4,0,3,2,1:T(8,128)(2,1)S(1)}, bf16[1,1,1,1,64,1024]{5,4,0,3,2,1:T(8,128)(2,1)S(1)}, u32[]{:S(2)}, u32[]{:S(2)}) collective-permute-start(bf16[1,1,1,1,64,1024]{5,4,0,3,2,1:T(8,128)(2,1)S(1)} %bitcast.382), channel_id=1, source_target_pairs={{0,16},{8,24},{16,0},{24,8},{1,17},{9,25},{17,1},{25,9},{2,18},{10... | collective-permute-start | bytes 393224 | tf_op jit(solution)/shard_map/ppermute | solution.py:23
  17.6 10.6 %collective-permute-start.12 = (bf16[1,1,1,1,64,1024]{5,4,0,1,3,2:T(8,128)(2,1)S(1)}, bf16[1,1,1,1,64,1024]{5,4,0,1,3,2:T(8,128)(2,1)S(1)}, u32[]{:S(2)}, u32[]{:S(2)}) collective-permute-start(bf16[1,1,1,1,64,1024]{5,4,0,1,3,2:T(8,128)(2,1)S(1)} %bitcast.386), channel_id=1, source_target_pairs={{0,16},{8,24},{16,0},{24,8},{1,17},{9,25},{17,1},{25,9},{2,18},{10... | collective-permute-start | bytes 393224 | tf_op jit(solution)/shard_map/ppermute | solution.py:23
  21.8 9.2 %collective-permute-start.16 = (bf16[1,1,1,1,64,1024]{5,4,3,2,1,0:T(8,128)(2,1)S(1)}, bf16[1,1,1,1,64,1024]{5,4,3,2,1,0:T(8,128)(2,1)S(1)}, u32[]{:S(2)}, u32[]{:S(2)}) collective-permute-start(bf16[1,1,1,1,64,1024]{5,4,3,2,1,0:T(8,128)(2,1)S(1)} %bitcast.412), channel_id=1, source_target_pairs={{0,16},{8,24},{16,0},{24,8},{1,17},{9,25},{17,1},{25,9},{2,18},{10... | collective-permute-start | bytes 393224 | tf_op jit(solution)/shard_map/ppermute | solution.py:23
  31.0 9.7 %collective-permute-start.5 = (bf16[2,1,1,1,64,1024]{5,4,0,3,2,1:T(8,128)(2,1)S(1)}, bf16[2,1,1,1,64,1024]{5,4,0,3,2,1:T(8,128)(2,1)S(1)}, u32[]{:S(2)}, u32[]{:S(2)}) collective-permute-start(bf16[2,1,1,1,64,1024]{5,4,0,3,2,1:T(8,128)(2,1)S(1)} %fusion.26), channel_id=1, source_target_pairs={{0,8},{8,0},{16,24},{24,16},{1,9},{9,1},{17,25},{25,17},{2,10},{10... | collective-permute-start | bytes 786440 | tf_op jit(solution)/shard_map/ppermute | solution.py:23
  37.4 8.4 %collective-permute-start.13 = (bf16[2,1,1,1,64,1024]{5,4,0,1,3,2:T(8,128)(2,1)S(1)}, bf16[2,1,1,1,64,1024]{5,4,0,1,3,2:T(8,128)(2,1)S(1)}, u32[]{:S(2)}, u32[]{:S(2)}) collective-permute-start(bf16[2,1,1,1,64,1024]{5,4,0,1,3,2:T(8,128)(2,1)S(1)} %fusion.28), channel_id=1, source_target_pairs={{0,8},{8,0},{16,24},{24,16},{1,9},{9,1},{17,25},{25,17},{2,10},{10... | collective-permute-start | bytes 786440 | tf_op jit(solution)/shard_map/ppermute | solution.py:23
  40.7 10.7 %collective-permute-start.17 = (bf16[2,1,1,1,64,1024]{5,4,0,3,2,1:T(8,128)(2,1)S(1)}, bf16[2,1,1,1,64,1024]{5,4,0,3,2,1:T(8,128)(2,1)S(1)}, u32[]{:S(2)}, u32[]{:S(2)}) collective-permute-start(bf16[2,1,1,1,64,1024]{5,4,0,3,2,1:T(8,128)(2,1)S(1)} %fusion.30), channel_id=1, source_target_pairs={{0,8},{8,0},{16,24},{24,16},{1,9},{9,1},{17,25},{25,17},{2,10},{10... | collective-permute-start | bytes 786440 | tf_op jit(solution)/shard_map/ppermute | solution.py:23
  45.8 12.8 %collective-permute-start.20 = (bf16[2,128,1024]{2,1,0:T(8,128)(2,1)S(1)}, bf16[2,128,1024]{2,1,0:T(8,128)(2,1)S(1)}, u32[]{:S(2)}, u32[]{:S(2)}) collective-permute-start(bf16[2,128,1024]{2,1,0:T(8,128)(2,1)S(1)} %copy-done.39), channel_id=1, source_target_pairs={{0,2},{2,0},{4,6},{6,4},{1,3},{3,1},{5,7},{7,5},{8,10},{10,8},{12,... | collective-permute-start | bytes 1572872 | tf_op jit(solution)/shard_map/ppermute | solution.py:23
  51.4 11.3 %collective-permute-start.14 = (bf16[2,2,1,1,64,1024]{5,4,0,1,3,2:T(8,128)(2,1)S(1)}, bf16[2,2,1,1,64,1024]{5,4,0,1,3,2:T(8,128)(2,1)S(1)}, u32[]{:S(2)}, u32[]{:S(2)}) collective-permute-start(bf16[2,2,1,1,64,1024]{5,4,0,1,3,2:T(8,128)(2,1)S(1)} %maximum_select_fusion.12), channel_id=1, source_target_pairs={{0,4},{2,6},{4,0},{6,2},{1,5},{3,7},{5,1},{7,3},{8,12},{10,14},{12... | collective-permute-start | bytes 1572872 | tf_op jit(solution)/shard_map/ppermute | solution.py:23
  51.5 32.1 %collective-permute-start.6 = (bf16[2,2,1,1,64,1024]{5,4,3,2,1,0:T(8,128)(2,1)S(1)}, bf16[2,2,1,1,64,1024]{5,4,3,2,1,0:T(8,128)(2,1)S(1)}, u32[]{:S(2)}, u32[]{:S(2)}) collective-permute-start(bf16[2,2,1,1,64,1024]{5,4,3,2,1,0:T(8,128)(2,1)S(1)} %copy.136), channel_id=1, source_target_pairs={{0,4},{2,6},{4,0},{6,2},{1,5},{3,7},{5,1},{7,3},{8,12},{10,14},{12... | collective-permute-start | bytes 1572872 | tf_op jit(solution)/shard_map/ppermute | solution.py:23
  53.0 14.0 %collective-permute-start.18 = (bf16[2,2,1,1,64,1024]{5,4,0,1,3,2:T(8,128)(2,1)S(1)}, bf16[2,2,1,1,64,1024]{5,4,0,1,3,2:T(8,128)(2,1)S(1)}, u32[]{:S(2)}, u32[]{:S(2)}) collective-permute-start(bf16[2,2,1,1,64,1024]{5,4,0,1,3,2:T(8,128)(2,1)S(1)} %maximum_select_fusion.14), channel_id=1, source_target_pairs={{0,2},{2,0},{4,6},{6,4},{1,3},{3,1},{5,7},{7,5},{8,10},{10,8},{12,... | collective-permute-start | bytes 1572872 | tf_op jit(solution)/shard_map/ppermute | solution.py:23
  54.5 77.4 %collective-permute-start.3 = (bf16[4,2,128,1024]{3,2,1,0:T(8,128)(2,1)S(1)}, bf16[4,2,128,1024]{3,2,1,0:T(8,128)(2,1)S(1)}, u32[]{:S(2)}, u32[]{:S(2)}) collective-permute-start(bf16[4,2,128,1024]{3,2,1,0:T(8,128)(2,1)S(1)} %pad_maximum_fusion.2), channel_id=1, source_target_pairs={{0,1},{1,0},{2,3},{3,2},{4,5},{5,4},{6,7},{7,6},{8,9},{9,8},{10,11... | collective-permute-start | bytes 6291464 | tf_op jit(solution)/shard_map/ppermute | solution.py:23
  58.6 37.8 %collective-permute-start.21 = (bf16[2,128,1024]{2,1,0:T(8,128)(2,1)S(1)}, bf16[2,128,1024]{2,1,0:T(8,128)(2,1)S(1)}, u32[]{:S(2)}, u32[]{:S(2)}) collective-permute-start(bf16[2,128,1024]{2,1,0:T(8,128)(2,1)S(1)} %copy-done.36), channel_id=1, source_target_pairs={{0,4},{2,6},{4,0},{6,2},{1,5},{3,7},{5,1},{7,3},{8,12},{10,14},{12... | collective-permute-start | bytes 1572872 | tf_op jit(solution)/shard_map/ppermute | solution.py:23
  62.7 33.7 %collective-permute-start.22 = (bf16[2,128,1024]{2,1,0:T(8,128)(2,1)S(1)}, bf16[2,128,1024]{2,1,0:T(8,128)(2,1)S(1)}, u32[]{:S(2)}, u32[]{:S(2)}) collective-permute-start(bf16[2,128,1024]{2,1,0:T(8,128)(2,1)S(1)} %copy-done.35), channel_id=1, source_target_pairs={{0,6},{2,4},{4,2},{6,0},{1,7},{3,5},{5,3},{7,1},{8,14},{10,12},{12... | collective-permute-start | bytes 1572872 | tf_op jit(solution)/shard_map/ppermute | solution.py:23
  67.0 50.8 %collective-permute-start.15 = (bf16[2,2,2,1,64,1024]{5,4,0,1,3,2:T(8,128)(2,1)S(1)}, bf16[2,2,2,1,64,1024]{5,4,0,1,3,2:T(8,128)(2,1)S(1)}, u32[]{:S(2)}, u32[]{:S(2)}) collective-permute-start(bf16[2,2,2,1,64,1024]{5,4,0,1,3,2:T(8,128)(2,1)S(1)} %maximum_select_fusion.8), channel_id=1, source_target_pairs={{0,2},{2,0},{4,6},{6,4},{1,3},{3,1},{5,7},{7,5},{8,10},{10,8},{12,... | collective-permute-start | bytes 3145736 | tf_op jit(solution)/shard_map/ppermute | solution.py:23
  83.6 36.3 %collective-permute-start.19 = (bf16[2,2,1,2,64,1024]{5,4,0,1,3,2:T(8,128)(2,1)S(1)}, bf16[2,2,1,2,64,1024]{5,4,0,1,3,2:T(8,128)(2,1)S(1)}, u32[]{:S(2)}, u32[]{:S(2)}) collective-permute-start(bf16[2,2,1,2,64,1024]{5,4,0,1,3,2:T(8,128)(2,1)S(1)} %maximum_select_fusion.9), channel_id=1, source_target_pairs={{0,4},{2,6},{4,0},{6,2},{1,5},{3,7},{5,1},{7,3},{8,12},{10,14},{12... | collective-permute-start | bytes 3145736 | tf_op jit(solution)/shard_map/ppermute | solution.py:23
  96.4 12.8 %collective-permute-start.11 = (bf16[2,2,2,1,64,384]{5,4,3,2,1,0:T(8,128)(2,1)S(1)}, bf16[2,2,2,1,64,384]{5,4,3,2,1,0:T(8,128)(2,1)S(1)}, u32[]{:S(2)}, u32[]{:S(2)}) collective-permute-start(bf16[2,2,2,1,64,384]{5,4,3,2,1,0:T(8,128)(2,1)S(1)} %maximum_select_fusion.16), channel_id=1, source_target_pairs={{0,2},{2,0},{4,6},{6,4},{1,3},{3,1},{5,7},{7,5},{8,10},{10,8},{12,... | collective-permute-start | bytes 1179656 | tf_op jit(solution)/shard_map/ppermute | solution.py:23
  96.4 35.3 %collective-permute-start.7 = (bf16[2,2,2,1,64,1024]{5,4,3,2,1,0:T(8,128)(2,1)S(1)}, bf16[2,2,2,1,64,1024]{5,4,3,2,1,0:T(8,128)(2,1)S(1)}, u32[]{:S(2)}, u32[]{:S(2)}) collective-permute-start(bf16[2,2,2,1,64,1024]{5,4,3,2,1,0:T(8,128)(2,1)S(1)} %maximum_select_fusion.7), channel_id=1, source_target_pairs={{0,2},{2,0},{4,6},{6,4},{1,3},{3,1},{5,7},{7,5},{8,10},{10,8},{12,... | collective-permute-start | bytes 3145736 | tf_op jit(solution)/shard_map/ppermute | solution.py:23
  109.2 94.1 %collective-permute-start.23 = (bf16[4,2,128,1024]{3,2,1,0:T(8,128)(2,1)}, bf16[4,2,128,1024]{3,2,1,0:T(8,128)(2,1)}, u32[]{:S(2)}, u32[]{:S(2)}) collective-permute-start(bf16[4,2,128,1024]{3,2,1,0:T(8,128)(2,1)} %pad_maximum_fusion.3), channel_id=1, source_target_pairs={{0,1},{1,0},{2,3},{3,2},{4,5},{5,4},{6,7},{7,6},{8,9},{9,8},{10,11... | collective-permute-start | bytes 6291464 | tf_op jit(solution)/shard_map/ppermute | solution.py:23
  349.0 73.9 %collective-permute-start.53 = (bf16[2,2,1,2,64,1024]{5,4,3,2,1,0:T(8,128)(2,1)}, bf16[2,2,1,2,64,1024]{5,4,3,2,1,0:T(8,128)(2,1)}, u32[]{:S(2)}, u32[]{:S(2)}) collective-permute-start(bf16[2,2,1,2,64,1024]{5,4,3,2,1,0:T(8,128)(2,1)} %dynamic-slice_convert_fusion.1), channel_id=1, source_target_pairs={{0,4},{2,6},{4,0},{6,2},{1,5},{3,7},{5,1},{7,3},{8,12},{10,14},{12... | collective-permute-start | bytes 3145736 | tf_op jit(solution)/shard_map/ppermute | solution.py:23
  366.0 93.2 %collective-permute-start.30 = (bf16[4,2,1,128,1024]{4,3,1,2,0:T(8,128)(2,1)}, bf16[4,2,1,128,1024]{4,3,1,2,0:T(8,128)(2,1)}, u32[]{:S(2)}, u32[]{:S(2)}) collective-permute-start(bf16[4,2,1,128,1024]{4,3,1,2,0:T(8,128)(2,1)} %bitcast_convert_fusion), channel_id=1, source_target_pairs={{0,1},{1,0},{2,3},{3,2},{4,5},{5,4},{6,7},{7,6},{8,9},{9,8},{10,11... | collective-permute-start | bytes 6291464 | tf_op jit(solution)/shard_map/ppermute | solution.py:23
  368.0 24.2 %collective-permute-start.47 = (bf16[2,2,2,1,64,272]{5,4,3,2,1,0:T(8,128)(2,1)}, bf16[2,2,2,1,64,272]{5,4,3,2,1,0:T(8,128)(2,1)}, u32[]{:S(2)}, u32[]{:S(2)}) collective-permute-start(bf16[2,2,2,1,64,272]{5,4,3,2,1,0:T(8,128)(2,1)} %dynamic-slice_convert_fusion.5), channel_id=1, source_target_pairs={{0,2},{2,0},{4,6},{6,4},{1,3},{3,1},{5,7},{7,5},{8,10},{10,8},{12,... | collective-permute-start | bytes 835592 | tf_op jit(solution)/shard_map/ppermute | solution.py:23
  373.1 52.6 %collective-permute-start.39 = (bf16[2,2,2,1,64,1024]{5,0,4,3,2,1:T(2,128)(2,1)}, bf16[2,2,2,1,64,1024]{5,0,4,3,2,1:T(2,128)(2,1)}, u32[]{:S(2)}, u32[]{:S(2)}) collective-permute-start(bf16[2,2,2,1,64,1024]{5,0,4,3,2,1:T(2,128)(2,1)} %copy.229), channel_id=1, source_target_pairs={{0,2},{2,0},{4,6},{6,4},{1,3},{3,1},{5,7},{7,5},{8,10},{10,8},{12,... | collective-permute-start | bytes 3145736 | tf_op jit(solution)/shard_map/ppermute | solution.py:23
  393.3 6.1 %collective-permute-start.48 = (bf16[2,2,1,1,64,272]{5,4,3,2,1,0:T(8,128)(2,1)S(1)}, bf16[2,2,1,1,64,272]{5,4,3,2,1,0:T(8,128)(2,1)S(1)}, u32[]{:S(2)}, u32[]{:S(2)}) collective-permute-start(bf16[2,2,1,1,64,272]{5,4,3,2,1,0:T(8,128)(2,1)S(1)} %dynamic-slice_convert_fusion.9), channel_id=1, source_target_pairs={{0,4},{2,6},{4,0},{6,2},{1,5},{3,7},{5,1},{7,3},{8,12},{10,14},{12... | collective-permute-start | bytes 417800 | tf_op jit(solution)/shard_map/ppermute | solution.py:23
  407.7 13.5 %collective-permute-start.51 = (f32[64,256]{1,0:T(8,128)}, f32[64,256]{1,0:T(8,128)}, u32[]{:S(2)}, u32[]{:S(2)}) collective-permute-start(f32[64,256]{1,0:T(8,128)} %slice.172), channel_id=1, source_target_pairs={{0,1},{1,0},{2,3},{3,2},{4,5},{5,4},{6,7},{7,6},{8,9},{9,8},{10,11... | collective-permute-start | bytes 196616 | tf_op jit(solution)/shard_map/ppermute | solution.py:23
  418.7 25.0 %collective-permute-start.43 = (bf16[2,2,1,2,64,1024]{5,0,4,3,2,1:T(2,128)(2,1)}, bf16[2,2,1,2,64,1024]{5,0,4,3,2,1:T(2,128)(2,1)S(1)}, u32[]{:S(2)}, u32[]{:S(2)}) collective-permute-start(bf16[2,2,1,2,64,1024]{5,0,4,3,2,1:T(2,128)(2,1)} %copy.228), channel_id=1, source_target_pairs={{0,4},{2,6},{4,0},{6,2},{1,5},{3,7},{5,1},{7,3},{8,12},{10,14},{12... | collective-permute-start | bytes 3145736 | tf_op jit(solution)/shard_map/ppermute | solution.py:23
  421.1 89.2 %collective-permute-start.25 = (bf16[4,2,1,128,1024]{4,3,2,1,0:T(8,128)(2,1)}, bf16[4,2,1,128,1024]{4,3,2,1,0:T(8,128)(2,1)S(1)}, u32[]{:S(2)}, u32[]{:S(2)}) collective-permute-start(bf16[4,2,1,128,1024]{4,3,2,1,0:T(8,128)(2,1)} %dynamic-slice_convert_fusion), channel_id=1, source_target_pairs={{0,1},{1,0},{2,3},{3,2},{4,5},{5,4},{6,7},{7,6},{8,9},{9,8},{10,11... | collective-permute-start | bytes 6291464 | tf_op jit(solution)/shard_map/ppermute | solution.py:23
  425.3 22.4 %collective-permute-start.54 = (bf16[2,2,1,1,64,1024]{5,4,3,2,1,0:T(8,128)(2,1)S(1)}, bf16[2,2,1,1,64,1024]{5,4,3,2,1,0:T(8,128)(2,1)S(1)}, u32[]{:S(2)}, u32[]{:S(2)}) collective-permute-start(bf16[2,2,1,1,64,1024]{5,4,3,2,1,0:T(8,128)(2,1)S(1)} %dynamic-slice_convert_fusion.2), channel_id=1, source_target_pairs={{0,2},{2,0},{4,6},{6,4},{1,3},{3,1},{5,7},{7,5},{8,10},{10,8},{12,... | collective-permute-start | bytes 1572872 | tf_op jit(solution)/shard_map/ppermute | solution.py:23
  429.5 25.4 %collective-permute-start.40 = (bf16[2,2,1,1,64,1024]{5,0,4,3,2,1:T(2,128)(2,1)S(1)}, bf16[2,2,1,1,64,1024]{5,0,4,3,2,1:T(2,128)(2,1)S(1)}, u32[]{:S(2)}, u32[]{:S(2)}) collective-permute-start(bf16[2,2,1,1,64,1024]{5,0,4,3,2,1:T(2,128)(2,1)S(1)} %dynamic-slice_convert_fusion.4), channel_id=1, source_target_pairs={{0,4},{2,6},{4,0},{6,2},{1,5},{3,7},{5,1},{7,3},{8,12},{10,14},{12... | collective-permute-start | bytes 1572872 | tf_op jit(solution)/shard_map/ppermute | solution.py:23
  446.4 12.3 %collective-permute-start.44 = (bf16[2,2,1,1,64,1024]{5,0,4,3,2,1:T(2,128)(2,1)S(1)}, bf16[2,2,1,1,64,1024]{5,0,4,3,2,1:T(2,128)(2,1)S(1)}, u32[]{:S(2)}, u32[]{:S(2)}) collective-permute-start(bf16[2,2,1,1,64,1024]{5,0,4,3,2,1:T(2,128)(2,1)S(1)} %dynamic-slice_convert_fusion.3), channel_id=1, source_target_pairs={{0,2},{2,0},{4,6},{6,4},{1,3},{3,1},{5,7},{7,5},{8,10},{10,8},{12,... | collective-permute-start | bytes 1572872 | tf_op jit(solution)/shard_map/ppermute | solution.py:23
  447.8 17.3 %collective-permute-start.55 = (bf16[2,1,1,1,64,1024]{5,4,3,2,1,0:T(8,128)(2,1)S(1)}, bf16[2,1,1,1,64,1024]{5,4,3,2,1,0:T(8,128)(2,1)S(1)}, u32[]{:S(2)}, u32[]{:S(2)}) collective-permute-start(bf16[2,1,1,1,64,1024]{5,4,3,2,1,0:T(8,128)(2,1)S(1)} %dynamic-slice_convert_fusion.6), channel_id=1, source_target_pairs={{0,8},{8,0},{16,24},{24,16},{1,9},{9,1},{17,25},{25,17},{2,10},{10... | collective-permute-start | bytes 786440 | tf_op jit(solution)/shard_map/ppermute | solution.py:23
  462.1 11.4 %collective-permute-start.31 = (bf16[2,128,1024]{2,1,0:T(8,128)(2,1)S(1)}, bf16[2,128,1024]{2,1,0:T(8,128)(2,1)S(1)}, u32[]{:S(2)}, u32[]{:S(2)}) collective-permute-start(bf16[2,128,1024]{2,1,0:T(8,128)(2,1)S(1)} %get-tuple-element.104), channel_id=1, source_target_pairs={{0,2},{2,0},{4,6},{6,4},{1,3},{3,1},{5,7},{7,5},{8,10},{10,8},{12,... | collective-permute-start | bytes 1572872 | tf_op jit(solution)/shard_map/ppermute | solution.py:23
  463.3 11.8 %collective-permute-start.32 = (bf16[2,128,1024]{2,1,0:T(8,128)(2,1)S(1)}, bf16[2,128,1024]{2,1,0:T(8,128)(2,1)S(1)}, u32[]{:S(2)}, u32[]{:S(2)}) collective-permute-start(bf16[2,128,1024]{2,1,0:T(8,128)(2,1)S(1)} %get-tuple-element.103), channel_id=1, source_target_pairs={{0,4},{2,6},{4,0},{6,2},{1,5},{3,7},{5,1},{7,3},{8,12},{10,14},{12... | collective-permute-start | bytes 1572872 | tf_op jit(solution)/shard_map/ppermute | solution.py:23
  463.6 22.0 %collective-permute-start.33 = (bf16[2,128,1024]{2,1,0:T(8,128)(2,1)S(1)}, bf16[2,128,1024]{2,1,0:T(8,128)(2,1)S(1)}, u32[]{:S(2)}, u32[]{:S(2)}) collective-permute-start(bf16[2,128,1024]{2,1,0:T(8,128)(2,1)S(1)} %get-tuple-element.102), channel_id=1, source_target_pairs={{0,6},{2,4},{4,2},{6,0},{1,7},{3,5},{5,3},{7,1},{8,14},{10,12},{12... | collective-permute-start | bytes 1572872 | tf_op jit(solution)/shard_map/ppermute | solution.py:23
  465.2 26.0 %collective-permute-start.41 = (bf16[2,1,1,1,64,1024]{5,0,4,3,2,1:T(2,128)(2,1)S(1)}, bf16[2,1,1,1,64,1024]{5,0,4,3,2,1:T(2,128)(2,1)S(1)}, u32[]{:S(2)}, u32[]{:S(2)}) collective-permute-start(bf16[2,1,1,1,64,1024]{5,0,4,3,2,1:T(2,128)(2,1)S(1)} %dynamic-slice_convert_fusion.8), channel_id=1, source_target_pairs={{0,8},{8,0},{16,24},{24,16},{1,9},{9,1},{17,25},{25,17},{2,10},{10... | collective-permute-start | bytes 786440 | tf_op jit(solution)/shard_map/ppermute | solution.py:23
  473.5 19.0 %collective-permute-start.45 = (bf16[2,1,1,1,64,1024]{5,0,4,3,2,1:T(2,128)(2,1)S(1)}, bf16[2,1,1,1,64,1024]{5,0,4,3,2,1:T(2,128)(2,1)S(1)}, u32[]{:S(2)}, u32[]{:S(2)}) collective-permute-start(bf16[2,1,1,1,64,1024]{5,0,4,3,2,1:T(2,128)(2,1)S(1)} %dynamic-slice_convert_fusion.7), channel_id=1, source_target_pairs={{0,8},{8,0},{16,24},{24,16},{1,9},{9,1},{17,25},{25,17},{2,10},{10... | collective-permute-start | bytes 786440 | tf_op jit(solution)/shard_map/ppermute | solution.py:23
  475.2 42.3 %collective-permute-start.56 = (bf16[1,1,1,1,64,1024]{5,4,3,2,1,0:T(8,128)(2,1)S(1)}, bf16[1,1,1,1,64,1024]{5,4,3,2,1,0:T(8,128)(2,1)S(1)}, u32[]{:S(2)}, u32[]{:S(2)}) collective-permute-start(bf16[1,1,1,1,64,1024]{5,4,3,2,1,0:T(8,128)(2,1)S(1)} %dynamic-slice_convert_fusion.10), channel_id=1, source_target_pairs={{0,16},{8,24},{16,0},{24,8},{1,17},{9,25},{17,1},{25,9},{2,18},{10... | collective-permute-start | bytes 393224 | tf_op jit(solution)/shard_map/ppermute | solution.py:23
  485.8 53.3 %collective-permute-start.34 = (bf16[4,2,128,1024]{3,2,1,0:T(8,128)(2,1)S(1)}, bf16[4,2,128,1024]{3,2,1,0:T(8,128)(2,1)S(1)}, u32[]{:S(2)}, u32[]{:S(2)}) collective-permute-start(bf16[4,2,128,1024]{3,2,1,0:T(8,128)(2,1)S(1)} %pad_maximum_fusion.5), channel_id=1, source_target_pairs={{0,1},{1,0},{2,3},{3,2},{4,5},{5,4},{6,7},{7,6},{8,9},{9,8},{10,11... | collective-permute-start | bytes 6291464 | tf_op jit(solution)/shard_map/ppermute | solution.py:23
  491.8 18.2 %collective-permute-start.42 = (bf16[1,1,1,1,64,1024]{5,0,4,3,2,1:T(2,128)(2,1)S(1)}, bf16[1,1,1,1,64,1024]{5,0,4,3,2,1:T(2,128)(2,1)S(1)}, u32[]{:S(2)}, u32[]{:S(2)}) collective-permute-start(bf16[1,1,1,1,64,1024]{5,0,4,3,2,1:T(2,128)(2,1)S(1)} %dynamic-slice_convert_fusion.12), channel_id=1, source_target_pairs={{0,16},{8,24},{16,0},{24,8},{1,17},{9,25},{17,1},{25,9},{2,18},{10... | collective-permute-start | bytes 393224 | tf_op jit(solution)/shard_map/ppermute | solution.py:23
  493.1 22.5 %collective-permute-start.46 = (bf16[1,1,1,1,64,1024]{5,0,4,3,2,1:T(2,128)(2,1)S(1)}, bf16[1,1,1,1,64,1024]{5,0,4,3,2,1:T(2,128)(2,1)S(1)}, u32[]{:S(2)}, u32[]{:S(2)}) collective-permute-start(bf16[1,1,1,1,64,1024]{5,0,4,3,2,1:T(2,128)(2,1)S(1)} %dynamic-slice_convert_fusion.11), channel_id=1, source_target_pairs={{0,16},{8,24},{16,0},{24,8},{1,17},{9,25},{17,1},{25,9},{2,18},{10... | collective-permute-start | bytes 393224 | tf_op jit(solution)/shard_map/ppermute | solution.py:23
  511.8 24.0 %collective-permute-start.27 = (bf16[2,128,1024]{2,1,0:T(8,128)(2,1)S(1)}, bf16[2,128,1024]{2,1,0:T(8,128)(2,1)S(1)}, u32[]{:S(2)}, u32[]{:S(2)}) collective-permute-start(bf16[2,128,1024]{2,1,0:T(8,128)(2,1)S(1)} %get-tuple-element.107), channel_id=1, source_target_pairs={{0,4},{2,6},{4,0},{6,2},{1,5},{3,7},{5,1},{7,3},{8,12},{10,14},{12... | collective-permute-start | bytes 1572872 | tf_op jit(solution)/shard_map/ppermute | solution.py:23
  512.1 23.7 %collective-permute-start.28 = (bf16[2,128,1024]{2,1,0:T(8,128)(2,1)S(1)}, bf16[2,128,1024]{2,1,0:T(8,128)(2,1)S(1)}, u32[]{:S(2)}, u32[]{:S(2)}) collective-permute-start(bf16[2,128,1024]{2,1,0:T(8,128)(2,1)S(1)} %get-tuple-element.106), channel_id=1, source_target_pairs={{0,6},{2,4},{4,2},{6,0},{1,7},{3,5},{5,3},{7,1},{8,14},{10,12},{12... | collective-permute-start | bytes 1572872 | tf_op jit(solution)/shard_map/ppermute | solution.py:23
  515.5 20.3 %collective-permute-start.26 = (bf16[2,128,1024]{2,1,0:T(8,128)(2,1)S(1)}, bf16[2,128,1024]{2,1,0:T(8,128)(2,1)S(1)}, u32[]{:S(2)}, u32[]{:S(2)}) collective-permute-start(bf16[2,128,1024]{2,1,0:T(8,128)(2,1)S(1)} %get-tuple-element.108), channel_id=1, source_target_pairs={{0,2},{2,0},{4,6},{6,4},{1,3},{3,1},{5,7},{7,5},{8,10},{10,8},{12,... | collective-permute-start | bytes 1572872 | tf_op jit(solution)/shard_map/ppermute | solution.py:23
  536.1 14.3 %collective-permute-start.29 = (bf16[4,2,128,1024]{3,2,1,0:T(8,128)(2,1)S(1)}, bf16[4,2,128,1024]{3,2,1,0:T(8,128)(2,1)}, u32[]{:S(2)}, u32[]{:S(2)}) collective-permute-start(bf16[4,2,128,1024]{3,2,1,0:T(8,128)(2,1)S(1)} %pad_maximum_fusion.4), channel_id=1, source_target_pairs={{0,1},{1,0},{2,3},{3,2},{4,5},{5,4},{6,7},{7,6},{8,9},{9,8},{10,11... | collective-permute-start | bytes 6291464 | tf_op jit(solution)/shard_map/ppermute | solution.py:23
  555.5 7.1 %collective-permute-start.36 = (f32[72,128]{1,0:T(8,128)S(1)}, f32[72,128]{1,0:T(8,128)S(1)}, u32[]{:S(2)}, u32[]{:S(2)}) collective-permute-start(f32[72,128]{1,0:T(8,128)S(1)} %fusion.49), channel_id=1, source_target_pairs={{0,2},{2,0},{4,6},{6,4},{1,3},{3,1},{5,7},{7,5},{8,10},{10,8},{12,... | collective-permute-start | bytes 110600 | tf_op jit(solution)/shard_map/ppermute | solution.py:23
  (70 other events, 1192.5 us)

commit v2 on v1

v2 whole, which is shorter than its diff:
```python
from functools import partial

import jax
import jax.numpy as jnp
from jax import lax
from jax.experimental import pallas as pl
from jax.experimental.pallas import tpu as pltpu
from jax.sharding import PartitionSpec as P

EPS = 1e-05
LOG2E = 1.4426950408889634
LANES = 128
GROUP = 2
HIGH = lax.Precision.HIGHEST
BF = jnp.bfloat16
F32 = jnp.float32


def bits_of(axis):
    return [1 << i for i in reversed(range(lax.axis_size(axis).bit_length() - 1))]


def swap(block, axis, mask):
    return lax.ppermute(block, axis, [(i, i ^ mask) for i in range(lax.axis_size(axis))])


def side(axis, bit):
    return (lax.axis_index(axis) // bit) % 2


def row_bits():
    return [("dp", b) for b in bits_of("dp")] + [("ctx", b) for b in bits_of("ctx")]


def open_gather(shard):
    return shard.reshape((1,) * len(row_bits()) + shard.shape)


def double(whole, place):
    dim = row_bits().index(place)
    other = swap(whole, *place)
    return jnp.where(
        side(*place) == 1,
        jnp.concatenate([other, whole], dim),
        jnp.concatenate([whole, other], dim),
    )


def close_gather(whole):
    return whole.reshape((-1,) + whole.shape[len(row_bits()) + 1 :])


def gather_rows(shard, order):
    whole = open_gather(shard)
    for place in order:
        whole = double(whole, place)
    return close_gather(whole)


def both_ways(array, cut):
    return [array[:, :cut], array[:, cut:]]


def tie(*trees):
    leaves, shape = jax.tree.flatten(trees)
    return jax.tree.unflatten(shape, lax.optimization_barrier(tuple(leaves)))


def offer(part, dim, axis):
    me = lax.axis_index(axis)
    pieces = [
        lax.dynamic_index_in_dim(part, me ^ k, dim, False) for k in range(lax.axis_size(axis))
    ]
    return [swap(x, axis, k) if k else x for k, x in enumerate(pieces)]


def add_up(pieces):
    return sum(x.astype(F32) for x in pieces)


def open_scatter(part):
    return part.reshape((lax.axis_size("dp"), lax.axis_size("ctx"), -1) + part.shape[1:])


def sum_over(part, places):
    for place in places:
        part = part + swap(part, *place)
    return part


def spread_out(blocks, length):
    parts = lax.axis_size("ctx")
    me = lax.axis_index("ctx")
    cuts = lax.axis_size("tensor")
    rows = length // cuts
    width = blocks.shape[-1]
    seqs = blocks.shape[0] // parts
    mine = lax.dynamic_slice_in_dim(blocks, lax.axis_index("tensor") * rows, rows, 1)
    mine = mine.reshape(parts, seqs, rows, width)
    slots = []
    for k in range(parts):
        piece = lax.dynamic_index_in_dim(mine, me ^ k, 0, False)
        slots.append(swap(piece, "ctx", k) if k else piece)
    return slots


def gather_cuts(share):
    for bit in reversed(bits_of("tensor")):
        other = swap(share, "tensor", bit)
        share = jnp.where(
            side("tensor", bit) == 1,
            jnp.concatenate([other, share], 2),
            jnp.concatenate([share, other], 2),
        )
    return share


def shares(grad, weight):
    cuts = lax.axis_size("tensor")
    rows = grad.shape[3] // cuts
    me = lax.axis_index("tensor")
    return [
        project_back(lax.dynamic_slice_in_dim(grad, (me ^ k) * rows, rows, 3), weight)
        for k in range(cuts)
    ]


def own_share(parts):
    mine, *others = parts
    return mine + add_up([swap(x.astype(BF), "tensor", k + 1) for k, x in enumerate(others)])


def send_home(share):
    return [swap(share[k], "ctx", k) if k else share[k] for k in range(lax.axis_size("ctx"))]


def arrange(slots):
    me = lax.axis_index("ctx")
    home = gather_cuts(jnp.stack(slots))
    home = jnp.concatenate([lax.dynamic_index_in_dim(home, me ^ k, 0) for k in range(len(slots))])
    return home.reshape((-1,) + home.shape[2:])


def dot(a, b, dims):
    return lax.dot_general(a, b, (dims, ((), ())), preferred_element_type=F32)


NN = ((1,), (0,))
NT = ((1,), (1,))
TN = ((0,), (0,))


def tiled(lanes, width):
    return jnp.concatenate([lanes] * (width // lanes.shape[1]), 1)


def conv_rows(raw, before, weight):
    taps = len(weight) - 1
    width = raw.shape[1]
    ext = jnp.concatenate([before, raw], 1)
    total = tiled(weight[taps], width) + tiled(weight[taps - 1], width) * raw
    for k in range(1, taps):
        total += tiled(weight[taps - 1 - k], width) * pltpu.roll(ext, k, 1)[:, LANES:]
    return total


def fold(rows):
    return sum(rows[:, i : i + LANES] for i in range(0, rows.shape[1], LANES))


def conv_back(grad, after, raw, weight):
    taps = len(weight) - 1
    width = grad.shape[1]
    ext = jnp.concatenate([grad, after], 1)
    out = tiled(weight[taps - 1], width) * grad
    terms = [None] * (taps - 1) + [fold(grad * raw), fold(grad)]
    for k in range(1, taps):
        moved = pltpu.roll(ext, width + LANES - k, 1)[:, :width]
        out += tiled(weight[taps - 1 - k], width) * moved
        terms[taps - 1 - k] = fold(moved * raw)
    return out, terms


def order_mask(width, keep):
    row = lax.broadcasted_iota(jnp.int32, (width, width), 0)
    col = lax.broadcasted_iota(jnp.int32, (width, width), 1)
    return keep(row, col)


def head_rows(dt_raw, dt_bias, a_log):
    biased = dt_raw + dt_bias
    step = jnp.maximum(biased, 0.0) + jnp.log1p(jnp.exp(-jnp.abs(biased)))
    a_decay = -jnp.exp(a_log)
    return biased, step, a_decay


def fill_heads(cs, heads, cs_ref, col_ref, ecs_ref, rem_ref, end_ref):
    width = cs.shape[1]
    cs2 = cs * LOG2E
    cs_ref[...] = cs2
    last = jnp.broadcast_to(cs2[:, width - 1 :], cs2.shape)
    ecs_ref[...] = jnp.exp2(cs2)
    rem_ref[...] = jnp.exp2(last - cs2)
    end_ref[...] = jnp.exp2(last[:, :LANES])
    columns = jnp.transpose(cs2)
    for h in range(heads):
        col_ref[h] = jnp.broadcast_to(columns[:, h : h + 1], (width, LANES))


def decay_blocks(cs_row, column):
    count = cs_row.shape[1] // LANES
    out = {}
    for i in range(count):
        for j in range(i, count):
            gap = cs_row[:, j * LANES : (j + 1) * LANES] - column[i * LANES : (i + 1) * LANES]
            out[i, j] = jnp.exp2(jnp.minimum(gap, 0.0) if i == j else gap)
    return out


def block(ref, i, j):
    return ref[i * LANES : (i + 1) * LANES, j * LANES : (j + 1) * LANES]


def mixing(decay, score_ref):
    count = score_ref.shape[0] // LANES
    none = jnp.zeros((LANES, LANES), BF)
    return jnp.concatenate(
        [
            jnp.concatenate(
                [
                    (decay[i, j] * block(score_ref, i, j)).astype(BF) if j >= i else none
                    for j in range(count)
                ],
                1,
            )
            for i in range(count)
        ],
        0,
    )


def loop_heads(heads, compute, store):
    group = GROUP if heads % GROUP == 0 else 1

    def some(i, carry):
        done = [compute(i * group + u) for u in range(group)]
        store(done)
        return carry

    lax.fori_loop(0, heads // group, some, 0)


def forward_kernel(
    heads, me, raw, bc_raw, dt_raw, cw, cbw, hp,
    z_out, y_out, cs_out, mem_out, zbc_out,
    mem, before, before_bc, step_s, cs_s, col_s, ecs_s, rem_s, end_s, score_s, maps_s,
):
    head_size = raw.shape[2] // heads
    half = bc_raw.shape[2] // 2
    width = raw.shape[3]
    taps = cw.shape[0]

    @pl.when(pl.program_id(1) == 0)
    def _():
        mem[...] = jnp.zeros_like(mem)
        before[...] = jnp.zeros_like(before)
        before_bc[...] = jnp.zeros_like(before_bc)

    bc = bc_raw[0, 0].astype(F32)
    zbc = conv_rows(bc, before_bc[...], [cbw[j] for j in range(taps)])
    before_bc[...] = bc[:, width - LANES :]
    zbc_out[0, 0] = zbc
    maps_s[...] = (zbc * jax.nn.sigmoid(zbc)).astype(BF)
    causal = order_mask(width, lambda s, t: s <= t)
    score_s[...] = jnp.where(causal, dot(maps_s[:half], maps_s[half:], TN), 0.0)

    _, step, a_decay = head_rows(dt_raw[0, 0], hp[0], hp[1])
    cs = jnp.dot(step * a_decay, causal.astype(F32), precision=HIGH, preferred_element_type=F32)
    cs_out[0, 0] = cs
    step_s[...] = step
    fill_heads(cs, heads, cs_s, col_s, ecs_s, rem_s, end_s)

    def compute(h):
        rows = pl.ds(pl.multiple_of(h * head_size, head_size), head_size)
        row = pl.ds(h, 1)
        own = raw[0, 0, rows, :].astype(F32)
        z = conv_rows(own, before[rows, :], [cw[j, rows, :] for j in range(taps)])
        x = z * jax.nn.sigmoid(z)
        scaled = x * step_s[row, :]
        decay = decay_blocks(cs_s[row, :], col_s[h])
        inside = dot(scaled.astype(BF), mixing(decay, score_s), NN)
        memory = mem[rows, :]
        memory_low = memory.astype(BF)
        held = dot(memory_low, maps_s[half:], NN) * ecs_s[row, :]
        y = inside + held + hp[2, row, :] * x
        gained = dot((scaled * rem_s[row, :]).astype(BF), maps_s[:half], NT)
        return rows, own[:, width - LANES :], z, y, memory_low, memory * end_s[row, :] + gained

    def store(done):
        for rows, edge, z, y, memory_low, memory in done:
            before[rows, :] = edge
            z_out[0, 0, rows, :] = z
            y_out[0, 0, rows, :] = y
            mem_out[0, 0, rows, :] = memory_low
            mem[rows, :] = memory

    loop_heads(heads, compute, store)


def backward_kernel(
    heads, me, z_in, raw, y_in, g_in, zbc_in, bc_raw, dt_raw, cs_in, mem_in, cw, cbw, hp,
    grad_out, sum_x, sum_bc, sum_h,
    gmem, gmem_low, after, after_bc, step_s, cs_s, col_s, ecs_s, rem_s, end_s, score_s, maps_s,
    gscore_s, eg_s, rx_s, pq_s, e_s, r_s, d_s, k_s,
):
    inner = raw.shape[2]
    head_size = inner // heads
    half = zbc_in.shape[2] // 2
    width = raw.shape[3]
    taps = cw.shape[0]

    @pl.when((pl.program_id(0) == 0) & (pl.program_id(1) == 0))
    def _():
        sum_x[...] = jnp.zeros_like(sum_x)
        sum_h[...] = jnp.zeros_like(sum_h)
        pq_s[...] = jnp.zeros_like(pq_s)
        e_s[...] = jnp.zeros_like(e_s)
        r_s[...] = jnp.zeros_like(r_s)
        d_s[...] = jnp.zeros_like(d_s)
        k_s[...] = jnp.zeros_like(k_s)
        sum_bc[...] = jnp.zeros_like(sum_bc)

    @pl.when(pl.program_id(1) == 0)
    def _():
        gmem[...] = jnp.zeros_like(gmem)
        after[...] = jnp.zeros_like(after)
        after_bc[...] = jnp.zeros_like(after_bc)

    zbc = zbc_in[0, 0]
    sig_bc = jax.nn.sigmoid(zbc)
    maps_s[...] = (zbc * sig_bc).astype(BF)
    causal = order_mask(width, lambda s, t: s <= t)
    score_s[...] = jnp.where(causal, dot(maps_s[:half], maps_s[half:], TN), 0.0)
    gscore_s[...] = jnp.zeros_like(gscore_s)

    biased, step, a_decay = head_rows(dt_raw[0, 0], hp[0], hp[1])
    step_s[...] = step
    fill_heads(cs_in[0, 0], heads, cs_s, col_s, ecs_s, rem_s, end_s)

    def compute(h):
        rows = pl.ds(pl.multiple_of(h * head_size, head_size), head_size)
        row = pl.ds(h, 1)
        z = z_in[0, 0, rows, :]
        sig = jax.nn.sigmoid(z)
        x = z * sig
        step_row = step_s[row, :]
        skip = hp[2, row, :]
        scaled = x * step_row
        scaled_low = scaled.astype(BF)
        scaled_back = scaled_low.astype(F32)
        g_low = g_in[0, 0, rows, :]
        g = g_low.astype(F32)
        decay = decay_blocks(cs_s[row, :], col_s[h])
        inside = dot(g_low, mixing(decay, score_s), NT)
        gweights = dot(scaled_low, g_low, TN)
        gscore = {
            (i, j): weight * gweights[i * LANES : (i + 1) * LANES, j * LANES : (j + 1) * LANES]
            for (i, j), weight in decay.items()
        }
        later = gmem[rows, :]
        later_low = later.astype(BF)
        outside = dot(later_low, maps_s[:half], NN) * rem_s[row, :]
        gscaled = inside + outside
        both = g * (y_in[0, 0, rows, :] - skip * x) - scaled_back * inside
        sums = (
            jnp.sum(both, 0, keepdims=True),
            jnp.sum(scaled_back * outside, 0, keepdims=True),
            jnp.sum(x * gscaled, 0, keepdims=True),
            d_s[row, :] + jnp.sum(g * x, 0, keepdims=True),
            jnp.sum(later * mem_in[0, 0, rows, :].astype(F32), 0, keepdims=True),
        )
        eg = (g * ecs_s[row, :]).astype(BF)
        rx = (scaled * rem_s[row, :]).astype(BF)
        earlier = later * end_s[row, :] + dot(eg, maps_s[half:], NT)
        gz = (step_row * gscaled + skip * g) * (sig * (1.0 + z * (1.0 - sig)))
        grad, terms = conv_back(
            gz, after[rows, :], raw[0, 0, rows, :].astype(F32),
            [cw[j, rows, :] for j in range(taps)],
        )
        terms = [sum_x[j, rows, :] + term for j, term in enumerate(terms)]
        return rows, row, gscore, sums, later_low, eg, rx, earlier, gz[:, :LANES], grad, terms

    def store(done):
        for i, j in done[0][2]:
            place = (slice(i * LANES, (i + 1) * LANES), slice(j * LANES, (j + 1) * LANES))
            gscore_s[place] += sum(one[2][i, j] for one in done)
        for rows, row, _, sums, later_low, eg, rx, earlier, edge, grad, terms in done:
            for ref, value in zip((pq_s, e_s, r_s, d_s, k_s), sums):
                ref[row, :] = value
            gmem_low[rows, :] = later_low
            eg_s[rows, :] = eg
            rx_s[rows, :] = rx
            gmem[rows, :] = earlier
            after[rows, :] = edge
            grad_out[0, 0, rows, :] = grad.astype(BF)
            for j, term in enumerate(terms):
                sum_x[j, rows, :] = term

    loop_heads(heads, compute, store)

    gscore = jnp.where(causal, gscore_s[...], 0.0).astype(BF)
    gout_map = dot(maps_s[:half], gscore, NN) + dot(mem_in[0, 0], eg_s[...], TN)
    gin_map = dot(maps_s[half:], gscore, NT) + dot(gmem_low[...], rx_s[...], TN)
    gmaps = jnp.concatenate([gin_map, gout_map], 0) * (sig_bc * (1.0 + zbc * (1.0 - sig_bc)))
    gbc, terms = conv_back(
        gmaps, after_bc[...], bc_raw[0, 0].astype(F32), [cbw[j] for j in range(taps)]
    )
    for j, term in enumerate(terms):
        sum_bc[j] += term
    after_bc[...] = gmaps[:, :LANES]
    grad_out[0, 0, inner : inner + 2 * half, :] = gbc.astype(BF)

    from_here = order_mask(width, lambda t, u: t >= u).astype(F32)
    strictly = order_mask(width, lambda s, u: s < u).astype(F32)
    carried = jnp.sum(k_s[...], 1, keepdims=True) * end_s[:, :1]
    gdecay = (
        jnp.dot(pq_s[...], from_here, precision=HIGH, preferred_element_type=F32)
        + jnp.dot(e_s[...], strictly, precision=HIGH, preferred_element_type=F32)
        + carried
    )
    gdt = (a_decay * gdecay + r_s[...]) * jax.nn.sigmoid(biased)
    grad_out[0, 0, inner + 2 * half :, :] = gdt.astype(BF)
    sum_h[0] += fold(gdt)
    sum_h[1] += fold(gdecay * step * a_decay)

    @pl.when((pl.program_id(0) == pl.num_programs(0) - 1) & (pl.program_id(1) == pl.num_programs(1) - 1))
    def _():
        sum_h[2] = fold(d_s[...])


def head_scratch(head_pad, heads, width, maps):
    return [
        pltpu.VMEM((head_pad, width), F32),
        pltpu.VMEM((head_pad, width), F32),
        pltpu.VMEM((heads, width, LANES), F32),
        pltpu.VMEM((head_pad, width), F32),
        pltpu.VMEM((head_pad, width), F32),
        pltpu.VMEM((head_pad, LANES), F32),
        pltpu.VMEM((width, width), F32),
        pltpu.VMEM((maps, width), BF),
    ]


def fixed(array):
    return pl.BlockSpec(array.shape, lambda s, c, me: (0,) * len(array.shape))


def kernel_call(body, name, flops, reverse, inputs, kinds, outs, scratch):
    parts, seqs = inputs[0].shape[:2]

    def part(array):
        def place(s, c, me):
            return ((parts - 1 - c if reverse else c) ^ me[0], s, 0, 0)

        return pl.BlockSpec((1, 1) + array.shape[2:], place)

    def spec(array, kind):
        return part(array) if kind == "p" else fixed(array)

    return pl.pallas_call(
        body,
        grid_spec=pltpu.PrefetchScalarGridSpec(
            num_scalar_prefetch=1,
            grid=(seqs, parts),
            in_specs=[spec(x, k) for x, k in zip(inputs, kinds)],
            out_specs=[spec(x, k) for x, k in outs],
            scratch_shapes=scratch,
        ),
        out_shape=[x for x, _ in outs],
        compiler_params=pltpu.CompilerParams(
            dimension_semantics=("arbitrary", "arbitrary"), vmem_limit_bytes=48 << 20
        ),
        cost_estimate=pl.CostEstimate(flops=flops, bytes_accessed=16 << 20, transcendentals=0),
        name=name,
    )(lax.axis_index("ctx").reshape(1), *inputs)


def run_forward(inner, bc, dt, cw, cbw, hp, heads):
    parts, seqs, rows, width = inner.shape
    maps, head_pad, states = bc.shape[2], dt.shape[2], bc.shape[2] // 2

    def out(count, last=width, kind=F32):
        return jax.ShapeDtypeStruct((parts, seqs, count, last), kind), "p"

    scratch = [
        pltpu.VMEM((rows, states), F32), pltpu.VMEM((rows, LANES), F32), pltpu.VMEM((maps, LANES), F32),
    ]
    return kernel_call(
        partial(forward_kernel, heads), "scan_forward", 45 << 30, False,
        [inner, bc, dt, cw, cbw, hp], "pppfff",
        [out(rows), out(rows), out(head_pad), out(rows, states, BF), out(maps)],
        scratch + head_scratch(head_pad, heads, width, maps),
    )


def run_backward(z, inner, y, g, zbc, bc, dt, cs, mem, cw, cbw, hp, heads):
    parts, seqs, rows, width = inner.shape
    maps, head_pad, states = zbc.shape[2], dt.shape[2], zbc.shape[2] // 2
    grads = jax.ShapeDtypeStruct((parts, seqs, rows + maps + head_pad, width), BF)
    sums = [cw.shape, cbw.shape, (3, head_pad, LANES)]
    scratch = [
        pltpu.VMEM((rows, states), F32), pltpu.VMEM((rows, states), BF),
        pltpu.VMEM((rows, LANES), F32), pltpu.VMEM((maps, LANES), F32),
    ]
    scratch += head_scratch(head_pad, heads, width, maps)
    scratch += [
        pltpu.VMEM((width, width), F32), pltpu.VMEM((rows, width), BF), pltpu.VMEM((rows, width), BF),
    ]
    scratch += [pltpu.VMEM((head_pad, width), F32)] * 4 + [pltpu.VMEM((head_pad, LANES), F32)]
    return kernel_call(
        partial(backward_kernel, heads), "scan_backward", 60 << 30, True,
        [z, inner, y, g, zbc, bc, dt, cs, mem, cw, cbw, hp], "pppppppppfff",
        [(grads, "p")] + [(jax.ShapeDtypeStruct(x, F32), "f") for x in sums], scratch,
    )


def project(rows, weight):
    return jnp.einsum("ksld,di->ksil", rows, weight, preferred_element_type=F32)


def project_back(grad, weight):
    return jnp.einsum("ksil,di->ksld", grad, weight, preferred_element_type=F32)


def weight_grad(rows, grad):
    return jnp.einsum("ksld,ksil->di", rows, grad, preferred_element_type=F32)


def per_device(
    tokens, norm_gain, w_zx, w_dt, w_bc, conv_x_w, conv_x_b, conv_bc_w, conv_bc_b,
    dt_bias, a_log, d_skip, norm_w, w_out, output_gradient,
):
    seqs_here, length, width = tokens.shape
    heads = w_dt.shape[1]
    head_pad = -(-heads // 16) * 16
    inner_here = w_out.shape[1]
    inner_total = inner_here * lax.axis_size("tensor")
    maps = w_bc.shape[1]
    rest = inner_here + maps
    dp_bits = [("dp", b) for b in bits_of("dp")]
    ctx_bits = [("ctx", b) for b in bits_of("ctx")]
    ways = [ctx_bits, ctx_bits[::-1]]
    tensor_bits = [("tensor", b) for b in bits_of("tensor")]

    rows = spread_out(tokens, length)
    scan_weights = jnp.concatenate(
        [w_zx[:, 1], w_bc, jnp.pad(w_dt, ((0, 0), (0, head_pad - heads)))], 1
    )
    scan_weights = both_ways(scan_weights, inner_here // 2 + LANES)
    full_scan = jnp.concatenate(
        [gather_rows(x, dp_bits + way) for x, way in zip(scan_weights, ways)], 1
    )
    gain = gather_rows(norm_gain[None], dp_bits + ctx_bits).reshape(-1).astype(F32)
    rows = gather_cuts(jnp.stack(rows))
    rows, gain, outer, cot_ready = tie(
        rows, gain, jnp.concatenate([w_out, w_zx[:, 0]], 1), output_gradient
    )
    outer = lax.all_gather(outer, ("dp", "ctx"), axis=0, tiled=True)
    cots = spread_out(cot_ready, length)

    def lanes(column):
        return jnp.broadcast_to(column[..., None], column.shape + (LANES,))

    cw = lanes(jnp.concatenate([conv_x_w, conv_x_b[None]], 0))
    cbw = lanes(jnp.concatenate([conv_bc_w, conv_bc_b[None]], 0))
    hp = jnp.pad(jnp.stack([dt_bias, a_log, d_skip]), ((0, 0), (0, head_pad - heads)))
    hp = jnp.broadcast_to(hp[..., None], hp.shape + (length,))

    residual = rows.astype(F32)
    normed = (
        residual * lax.rsqrt(jnp.mean(residual * residual, axis=-1, keepdims=True) + EPS) * gain
    ).astype(BF)
    inner_raw = project(normed, full_scan[:, :inner_here]).astype(BF)
    bc_raw = project(normed, full_scan[:, inner_here:rest]).astype(BF)
    dt_raw = project(normed, full_scan[:, rest:])
    z, y, cs, mem, zbc = run_forward(inner_raw, bc_raw, dt_raw, cw, cbw, hp, heads)

    y, outer, cots = tie(y, outer, cots)
    cots = gather_cuts(jnp.stack(cots))
    full_out, full_gate = outer[:, :inner_here], outer[:, inner_here:]
    norm_column = norm_w[:, None]
    gate_raw = project(normed, full_gate)
    grad_mixed = project(cots, full_out)
    gate_sig = jax.nn.sigmoid(gate_raw)
    gate_act = gate_raw * gate_sig
    gated = y * gate_act
    weighted = grad_mixed * norm_column
    sums = jnp.stack([jnp.sum(gated * gated, axis=2), jnp.sum(weighted * gated, axis=2)])
    sums = sum_over(sums, tensor_bits)[:, :, :, None]
    inv_rms = lax.rsqrt(sums[0] / inner_total + EPS)
    mixed_in = (gated * inv_rms * norm_column).astype(BF)
    grad_norm_w = jnp.sum(grad_mixed * gated * inv_rms, axis=(0, 1, 3))
    grad_gated = inv_rms * weighted - gated * (inv_rms * inv_rms * inv_rms) * (
        sums[1] / inner_total
    )
    grad_gate = (grad_gated * y * gate_sig * (1.0 + gate_raw * (1.0 - gate_sig))).astype(BF)
    grad_y = (grad_gated * gate_act).astype(BF)

    outer_grad = jnp.concatenate(
        [weight_grad(cots, mixed_in).astype(BF), weight_grad(normed, grad_gate).astype(BF)], 1
    )
    mixed_in, grad_gate, outer_grad = tie(mixed_in, grad_gate, outer_grad)
    outer_grad = offer(open_scatter(outer_grad), 1, "ctx")
    cuts = lax.axis_size("tensor")
    share = lax.dynamic_slice_in_dim(
        rows, lax.axis_index("tensor") * (length // cuts), length // cuts, 2
    ).astype(F32)
    mixed = (share + own_share(shares(mixed_in, full_out))).astype(BF)
    normed_gate = [x.astype(BF) for x in shares(grad_gate, full_gate)]
    grad_y, mixed, normed_gate = tie(grad_y, mixed, normed_gate)
    mixed = send_home(mixed)

    grad_scan, sum_x, sum_bc, sum_h = run_backward(
        z, inner_raw, y, grad_y, zbc, bc_raw, dt_raw, cs, mem, cw, cbw, hp, heads
    )
    grad_scan, mixed, outer_grad = tie(grad_scan, mixed, outer_grad)

    scan_grad = weight_grad(normed, grad_scan).astype(BF)
    grad_scan, scan_grad = tie(grad_scan, scan_grad)
    scan_grad = offer(open_scatter(scan_grad), 1, "ctx")
    grad_share = [
        x.astype(F32) + part for x, part in zip(normed_gate, shares(grad_scan, full_scan))
    ]
    grad_share = own_share(grad_share).astype(BF)
    grad_share, scan_grad, outer_grad = tie(grad_share, scan_grad, outer_grad)
    grad_home = send_home(grad_share)
    weight_grads = jnp.concatenate([add_up(outer_grad), add_up(scan_grad)], -1).astype(BF)
    weight_grads = add_up(offer(weight_grads, 0, "dp"))
    grad_w_out, grad_w_gate = weight_grads[:, :inner_here], weight_grads[:, inner_here : 2 * inner_here]
    scan_grad = weight_grads[:, 2 * inner_here :]
    grad_w_inner = scan_grad[:, :inner_here]
    grad_w_bc = sum_over(scan_grad[:, inner_here:rest], tensor_bits)
    grad_w_dt = scan_grad[:, rest : rest + heads]
    r = lax.rsqrt(jnp.mean(share * share, axis=-1, keepdims=True) + EPS)
    grad_gain = jnp.sum(share * r * grad_share.astype(F32), axis=(0, 1, 2))

    sum_x = jnp.sum(sum_x, -1)
    sum_bc = jnp.sum(sum_bc, -1)
    sum_h = jnp.sum(sum_h, -1)[:, :heads]
    pieces = [sum_x, grad_norm_w, sum_h, grad_gain, sum_bc]
    flat = jnp.concatenate([p.reshape(-1) for p in pieces])
    size = flat.shape[0]
    flat = jnp.pad(flat, (0, -size % 1024)).reshape(-1, LANES)
    flat = sum_over(flat, ctx_bits + dp_bits).reshape(-1)[:size]
    out = []
    for p in pieces:
        out.append(flat[: p.size].reshape(p.shape))
        flat = flat[p.size :]
    sum_x, grad_norm_w, sum_h, grad_gain, sum_bc = out
    sum_bc, grad_gain = jax.tree.map(lambda x: sum_over(x, tensor_bits), (sum_bc, grad_gain))
    taps = conv_x_w.shape[0]
    row = lax.axis_index("dp") * lax.axis_size("ctx") + lax.axis_index("ctx")
    grad_gain = lax.dynamic_slice_in_dim(
        grad_gain, row * norm_gain.shape[0], norm_gain.shape[0], 0
    )

    mixed_out = arrange(mixed)
    grad_home = arrange(grad_home).astype(F32)
    here = tokens.astype(F32)
    r = lax.rsqrt(jnp.mean(here * here, axis=-1, keepdims=True) + EPS)
    scaled = gain * grad_home
    grad_tokens = (
        output_gradient.astype(F32)
        + r * scaled
        - here * (r * r * r) * jnp.mean(here * scaled, axis=-1, keepdims=True)
    )
    return (
        mixed_out,
        grad_tokens,
        grad_gain,
        jnp.stack([grad_w_gate, grad_w_inner], 1),
        grad_w_dt,
        grad_w_bc,
        sum_x[:taps],
        sum_x[taps],
        sum_bc[:taps],
        sum_bc[taps],
        sum_h[0],
        sum_h[1],
        sum_h[2],
        grad_norm_w,
        grad_w_out,
    )


def solution(mesh):
    rows = P(("dp", "ctx"), "tensor")
    tokens = P("dp", "ctx", None)
    heads = P("tensor")
    return jax.shard_map(
        per_device,
        mesh=mesh,
        in_specs=(
            tokens, P(("dp", "ctx")), P(("dp", "ctx"), None, "tensor"), rows, P(("dp", "ctx"), None),
            P(None, "tensor"), heads, P(), P(), heads, heads, heads, heads, rows, tokens,
        ),
        out_specs=(
            tokens, tokens, P(("dp", "ctx")), P(("dp", "ctx"), None, "tensor"), rows,
            P(("dp", "ctx"), None), P(None, "tensor"), heads, P(), P(), heads, heads, heads, heads, rows,
        ),
        check_vma=False,
    )
```

time: 587 us -> 501 us (0.85)
  Pallas kernels: 116 us -> 86.4 us
  starting transfers between devices: 78.5 us -> 51.3 us
  waiting for transfers between devices: 159 us -> 132 us
  between operations: 2.34 us -> 15.7 us
  other arithmetic: 76.1 us -> 68.8 us
  local copies, waits for them, and re-layouts: 54 us -> 47.5 us
    ppermute x57 -> x47, waiting for transfers between devices: 159 us -> 112 us  [swap(): lax.ppermute(block, axis, [(i, i ^ mask) for i in range(lax.axis_size(axi...]
    pallas_call x2, Pallas kernels: 116 us -> 86.4 us  [kernel_call(): pl.pallas_call(body, grid_spec=pltpu.PrefetchScalarGridSpec(num_scalar_pr...]
    ppermute x57 -> x47, starting transfers between devices: 78.5 us -> 51.3 us  [swap(): lax.ppermute(block, axis, [(i, i ^ mask) for i in range(lax.axis_size(axi...]
    all_gather x0 -> x1, waiting for transfers between devices: none -> 20.6 us  [per_device(): outer = lax.all_gather(outer, ('dp', 'ctx'), axis=0, tiled=True)]
    optimization_barrier x0 -> x3, local copies, waits for them, and re-layouts: none -> 16.5 us  [tie(): return jax.tree.unflatten(shape, lax.optimization_barrier(tuple(leaves)))]
    convert_element_type x16 -> x1, local copies, waits for them, and re-layouts: 10.9 us -> 0.08 us  [per_device(): gather_rows(norm_gain[None], dp_bits + ctx_bits).reshape(-1).astype(F32)]
    add x12 -> x1, other arithmetic: 11 us -> 1.48 us  [add_up(): return sum((x.astype(F32) for x in pieces))]
    another operation x4 -> x6, other arithmetic: 3.56 us -> 12.2 us  [the longest x2 3.03 us: spread_out(): return gather_cuts(jnp.stack(slots))]
  transfers between devices with their start and end apart: 57 -> 48, of which waited for: 25 -> 22; matrix products, arithmetic and copies ran while one was open for 24% -> 23% of each run, Pallas kernels for 8% -> 17%
where the time goes in v2:
time: 501 us; the launch traced here: 497 us
  waiting for transfers between devices  132 us (26%)
  matrix products  94.6 us (19%)
  Pallas kernels  86.4 us (17%)
  other arithmetic  68.8 us (14%)
  starting transfers between devices  51.3 us (10%)
  local copies, waits for them, and re-layouts  47.5 us (9%)
  between operations  15.7 us (3%)
    ppermute x47, waiting for transfers between devices, swap(): lax.ppermute(block, axis, [(i, i ^ mask) for i in range(lax.axis_size(axi...  112 us
    pallas_call x2, Pallas kernels, kernel_call(): pl.pallas_call(body, grid_spec=pltpu.PrefetchScalarGridSpec(num_scalar_pr...  86.4 us
    ppermute x47, starting transfers between devices, swap(): lax.ppermute(block, axis, [(i, i ^ mask) for i in range(lax.axis_size(axi...  51.3 us
    dot_general x5, matrix products, project(): return jnp.einsum('ksld,di->ksil', rows, weight, preferred_element_type=F32)  35.2 us
    dot_general x3, matrix products, weight_grad(): return jnp.einsum('ksld,ksil->di', rows, grad, preferred_element_type=F32)  33 us
    dot_general x6, matrix products, project_back(): return jnp.einsum('ksil,di->ksld', grad, weight, preferred_element_type=F32)  26.4 us
    all_gather x1, waiting for transfers between devices, per_device(): outer = lax.all_gather(outer, ('dp', 'ctx'), axis=0, tiled=True)  20.6 us
    optimization_barrier x3, local copies, waits for them, and re-layouts, tie(): return jax.tree.unflatten(shape, lax.optimization_barrier(tuple(leaves)))  16.5 us
  transfers between devices with their start and end apart: 48, of which 22 were waited for; matrix products, arithmetic and copies ran while one was open for 23% of the time, Pallas kernels for 17%

profile of v2, /device:TPU:9, one launch (start us, length us, event | category | flops | bytes accessed | tf_op | source)
XLA Modules:
  0.0 496.7 jit_solution(17529438273026574102)
XLA Ops:
  12.9 2.3 collective-permute-start.12
  16.0 7.3 %collective-permute-done.8 = bf16[2,128,1024]{2,1,0:T(8,128)(2,1)S(1)} collective-permute-done((bf16[2,128,1024]{2,1,0:T(8,128)(2,1)}, bf16[2,128,1024]{2,1,0:T(8,128)(2,1)S(1)}, u32[]{:S(2)}, u32[]{:S(2)}) %collective-permute-start.8) | collective-permute-done | bytes 524320 | tf_op jit(solution)/shard_map/ppermute | solution.py:24
  23.3 2.3 collective-permute-start
  25.6 9.9 %collective-permute-done.10 = bf16[2,128,1024]{2,1,0:T(8,128)(2,1)S(1)} collective-permute-done((bf16[2,128,1024]{2,1,0:T(8,128)(2,1)}, bf16[2,128,1024]{2,1,0:T(8,128)(2,1)S(1)}, u32[]{:S(2)}, u32[]{:S(2)}) %collective-permute-start.10) | collective-permute-done | bytes 524320 | tf_op jit(solution)/shard_map/ppermute | solution.py:24
  39.2 2.2 collective-permute-done.13
  48.3 2.5 collective-permute-done.1
  54.2 3.0 collective-permute-done.2
  61.5 6.0 %maximum_select_fusion = bf16[4,2,256,1024]{3,2,1,0:T(8,128)(2,1)} fusion(bf16[1,2,128,1024]{3,2,1,0:T(8,128)(2,1)} %bitcast.275, bf16[1,2,128,1024]{3,2,1,0:T(8,128)(2,1)S(1)} %bitcast.273, bf16[1,2,128,1024]{3,2,1,0:T(8,128)(2,1)S(1)} %bitcast.271, bf16[1,2,128,1024]{3,2,1,0:T(8,128)(2,1)S(1)} %get-tuple-element.189, ...), kind=kLoop, calls=%fused_computation.41 | loop fusion | flops 44040192 | bytes 8388609 | tf_op jit(solution)/shard_map/jit(_where)/select_n | solution.py:110
  67.7 5.7 %collective-permute-done.3 = bf16[2,2,2,1,64,640]{5,4,0,1,3,2:T(8,128)(2,1)} collective-permute-done((bf16[2,2,2,1,64,640]{5,4,0,1,3,2:T(8,128)(2,1)S(1)}, bf16[2,2,2,1,64,640]{5,4,0,1,3,2:T(8,128)(2,1)}, u32[]{:S(2)}, u32[]{:S(2)}) %collective-permute-start.3) | collective-permute-done | bytes 655392 | tf_op jit(solution)/shard_map/ppermute | solution.py:24
  80.0 1.9 constant_dynamic-slice_fusion.8
  88.5 6.3 %convert_bitcast_fusion.raw = bf16[4,2,1024,256]{3,2,1,0:T(8,128)(2,1)} fusion(bf16[1024,656]{0,1:T(8,128)(2,1)S(1)} %copy-done.38, bf16[1024,640]{0,1:T(8,128)(2,1)S(1)} %copy-done.41, bf16[4,2,256,1024]{3,2,1,0:T(8,128)(2,1)S(1)} %copy-done.3, f32[1024]{0:T(1024)S(1)} %reshape.1669, f32[4,2,256]{2,1,0:T(2,128)S(1)} %add_rsqrt_fusion.1), kind=kOutput, calls=%fused_computation.52 | convolution fusion | flops 4309647360 | bytes 11055104 | tf_op jit(solution)/shard_map/ksld,di->ksil/dot_general | solution.py:528
  97.0 35.2 %scan_forward.1 = (f32[4,2,1024,256]{3,2,1,0:T(8,128)}, f32[4,2,1024,256]{3,2,1,0:T(8,128)}, f32[4,2,16,256]{3,2,1,0:T(8,128)S(1)}, bf16[4,2,1024,128]{3,2,1,0:T(8,128)(2,1)S(1)}, f32[4,2,256,256]{3,2,1,0:T(8,128)S(1)}) custom-call(s32[1]{0:T(128)} %bitcast.me, bf16[4,2,1024,256]{3,2,1,0:T(8,128)(2,1)} %convert_bitcast_fusion.raw, ...), custom_call_target="tpu_custom_call" | custom-call | flops 48318382080 | bytes 16777216 | tf_op jit(solution)/shard_map/scan_forward/pallas_call | solution.py:470
  134.9 20.6 %all-gather.2.cloned.1.call-done = bf16[1024,2048]{1,0:T(8,128)(2,1)} async-done(((bf16[64,2048]{1,0:T(8,128)(2,1)}), bf16[1024,2048]{1,0:T(8,128)(2,1)}) %all-gather.2.cloned.1.call-update) | async-done | bytes 4194320 | tf_op jit(solution)/shard_map/all_gather | solution.py:568
  155.5 2.7 pad_maximum_fusion.5
  160.1 6.7 %copy.100 = bf16[1024,2048]{0,1:T(8,128)(2,1)} copy(bf16[1024,2048]{1,0:T(8,128)(2,1)} %all-gather.2.cloned.1.call-done) | data formatting | bytes 8388608 | tf_op jit(solution)/shard_map/optimization_barrier | solution.py:66
  166.8 10.8 %fusion.52 = f32[1024,4,2,256]{3,0,2,1:T(8,128)} fusion(bf16[1024,2048]{0,1:T(8,128)(2,1)} %copy.100, bf16[4,2,256,1024]{3,2,1,0:T(8,128)(2,1)} %maximum_select_fusion, f32[1024]{0:T(1024)S(1)} %reshape.1669, f32[4,2,256]{2,1,0:T(2,128)S(1)} %add_rsqrt_fusion.1), kind=kOutput, calls=%fused_computation.96 | convolution fusion | flops 4303355904 | bytes 14692352 | tf_op jit(solution)/shard_map/ksld,di->ksil/dot_general | solution.py:528
  177.7 15.4 %multiply_reduce_fusion.1 = (f32[4,2,256]{2,1,0:T(2,128)S(1)}, f32[4,2,256]{2,1,0:T(2,128)S(1)}, f32[4,2,1024,256]{3,2,1,0:T(8,128)}, f32[1024,4,2,256]{3,0,2,1:T(8,128)}) fusion(f32[1024]{0:T(1024)S(1)} %copy-done.56, f32[4,2,1024,256]{3,2,1,0:T(8,128)} %get-tuple-element.67.y_in, f32[1024,4,2,256]{3,0,2,1:T(8,128)} %fusion.52, ...), kind=kOutput, calls=%fused_computation.32 | convolution fusion | flops 4359974912 | bytes 39866368 | tf_op jit(solution)/shard_map/ksld,di->ksil/dot_general | solution.py:528
  194.4 14.8 %fusion.16 = (bf16[4,2,1024,256]{3,2,1,0:T(8,128)(2,1)S(1)}, bf16[4,2,1024,256]{3,2,1,0:T(8,128)(2,1)}, f32[1024]{0:T(1024)S(1)}, bf16[4,2,1024,256]{3,2,1,0:T(8,128)(2,1)S(1)}) fusion(f32[1024,4,2,256]{3,0,2,1:T(8,128)} %fusion.52, f32[4,2,1024,256]{3,2,1,0:T(8,128)} %get-tuple-element.67.y_in, f32[4,2,256]{2,1,0:T(2,128)S(1)} %get-tuple-element.215, ...), kind=kLoop, calls=%fused_computation.27 | loop fusion | flops 50330624 | bytes 46170112 | tf_op jit(solution)/shard_map/convert_element_type | solution.py:606
  209.2 4.9 bitcast_convert_fusion.1
  214.1 17.5 %bitcast_convert_fusion.2 = bf16[1024,1024]{0,1:T(8,128)(2,1)S(1)} fusion(bf16[4,2,1024,256]{3,2,1,0:T(8,128)(2,1)S(1)} %get-tuple-element.73, bf16[1,2,128,1024]{3,2,1,0:T(8,128)(2,1)} %bitcast.60, bf16[1,2,128,1024]{3,2,1,0:T(8,128)(2,1)} %bitcast.59, bf16[1,2,128,1024]{3,2,1,0:T(8,128)(2,1)S(1)} %bitcast.298, ...), kind=kOutput, calls=%fused_computation.49 | convolution fusion | flops 4340056064 | bytes 10485761 | tf_op jit(solution)/shard_map/ksld,ksil->di/dot_general | solution.py:536
  231.7 2.6 pad_maximum_fusion
  235.4 3.7 fusion.37
  239.3 6.5 %copy.110 = bf16[1024,2048]{1,0:T(8,128)(2,1)} copy(bf16[1024,2048]{0,1:T(8,128)(2,1)} %pad_maximum_fusion) | data formatting | bytes 8388608 | tf_op jit(solution)/shard_map/optimization_barrier | solution.py:66
  245.9 4.2 dynamic-slice_bitcast_fusion
  252.7 3.7 fusion.43
  256.5 3.7 fusion.40
  260.2 4.2 fusion.17
  266.2 8.4 %collective-permute-done.25 = bf16[4,64,2048]{2,1,0:T(8,128)(2,1)S(1)} collective-permute-done((bf16[4,64,2048]{2,1,0:T(8,128)(2,1)S(1)}, bf16[4,64,2048]{2,1,0:T(8,128)(2,1)S(1)}, u32[]{:S(2)}, u32[]{:S(2)}) %collective-permute-start.25) | collective-permute-done | bytes 1048608 | tf_op jit(solution)/shard_map/ppermute | solution.py:24
  275.8 51.2 %scan_backward.1 = (bf16[4,2,1296,256]{3,2,1,0:T(8,128)(2,1)}, f32[5,1024,128]{2,1,0:T(8,128)}, f32[5,256,128]{2,1,0:T(8,128)S(1)}, f32[3,16,128]{2,1,0:T(8,128)S(1)}) custom-call(s32[1]{0:T(128)} %bitcast.me, f32[4,2,1024,256]{3,2,1,0:T(8,128)} %get-tuple-element.63.z_in, bf16[4,2,1024,256]{3,2,1,0:T(8,128)(2,1)} %convert_bitcast_fusion.raw, ...), custom_call_target="tpu_custom_call" | custom-call | flops 64424509440 | bytes 16777216 | tf_op jit(solution)/shard_map/scan_backward/pallas_call | solution.py:470
  327.1 10.6 %bitcast_convert_fusion = bf16[1024,1296]{0,1:T(8,128)(2,1)} fusion(bf16[4,2,1296,256]{3,2,1,0:T(8,128)(2,1)} %get-tuple-element.88, bf16[4,2,256,1024]{3,2,1,0:T(8,128)(2,1)S(1)} %copy-done.5, f32[1024]{0:T(1024)S(1)} %reshape.1669, f32[4,2,256]{2,1,0:T(2,128)S(1)} %add_rsqrt_fusion.1), kind=kOutput, calls=%fused_computation.36 | convolution fusion | flops 5445533696 | bytes 12169216 | tf_op jit(solution)/shard_map/ksld,ksil->di/dot_general | solution.py:536
  337.7 4.7 add_convert_fusion.1
  342.4 2.1 collective-permute-start.29
  344.5 2.1 fusion.18
  346.6 2.5 reduce_sum.104
  349.6 3.3 copy.111
  359.2 6.3 %add_convert_fusion = bf16[4,2,128,1024]{3,2,1,0:T(8,128)(2,1)S(1)} fusion(bf16[4,2,128,1024]{3,2,1,0:T(8,128)(2,1)} %collective-permute-done.29, bf16[4,2,128,1024]{3,2,1,0:T(8,128)(2,1)S(1)} %copy-done.65, bf16[1024,656]{0,1:T(8,128)(2,1)S(1)} %copy-done.40, bf16[1024,640]{0,1:T(8,128)(2,1)S(1)} %copy-done.43, ...), kind=kOutput, calls=%fused_computation.50 | convolution fusion | flops 2728460288 | bytes 11599876 | tf_op jit(solution)/shard_map/ksil,di->ksld/dot_general | solution.py:532
  365.5 6.3 %collective-permute-done.30 = bf16[4,64,1296]{2,1,0:T(8,128)(2,1)S(1)} collective-permute-done((bf16[4,64,1296]{2,1,0:T(8,128)(2,1)S(1)}, bf16[4,64,1296]{2,1,0:T(8,128)(2,1)S(1)}, u32[]{:S(2)}, u32[]{:S(2)}) %collective-permute-start.30) | collective-permute-done | bytes 663584 | tf_op jit(solution)/shard_map/ppermute | solution.py:24
  372.7 15.5 %collective-permute-done.32 = bf16[4,64,1296]{2,1,0:T(8,128)(2,1)S(1)} collective-permute-done((bf16[4,64,1296]{2,1,0:T(8,128)(2,1)S(1)}, bf16[4,64,1296]{2,1,0:T(8,128)(2,1)S(1)}, u32[]{:S(2)}, u32[]{:S(2)}) %collective-permute-start.32) | collective-permute-done | bytes 663584 | tf_op jit(solution)/shard_map/ppermute | solution.py:24
  391.4 2.8 add_convert_fusion.2
  399.9 3.9 maximum_select_fusion.2
  403.8 16.8 %collective-permute-done.38 = f32[72,128]{1,0:T(8,128)S(1)} collective-permute-done((f32[72,128]{1,0:T(8,128)S(1)}, f32[72,128]{1,0:T(8,128)S(1)}, u32[]{:S(2)}, u32[]{:S(2)}) %collective-permute-start.38) | collective-permute-done | bytes 36896 | tf_op jit(solution)/shard_map/ppermute | solution.py:24
  426.0 2.5 pad_maximum_fusion.1
  432.2 5.9 %collective-permute-start.36 = (bf16[4,2,128,1024]{3,2,1,0:T(8,128)(2,1)}, bf16[4,2,128,1024]{3,2,1,0:T(8,128)(2,1)}, u32[]{:S(2)}, u32[]{:S(2)}) collective-permute-start(bf16[4,2,128,1024]{3,2,1,0:T(8,128)(2,1)} %pad_maximum_fusion.7), channel_id=1, source_target_pairs={{0,1},{1,0},{2,3},{3,2},{4,5},{5,4},{6,7},{7,6},{8,9},{9,8},{10,11... | collective-permute-start | bytes 6291464 | tf_op jit(solution)/shard_map/ppermute | solution.py:24
  444.3 13.7 %collective-permute-done.43 = bf16[64,3344]{1,0:T(8,128)(2,1)S(1)} collective-permute-done((bf16[64,3344]{1,0:T(8,128)(2,1)}, bf16[64,3344]{1,0:T(8,128)(2,1)S(1)}, u32[]{:S(2)}, u32[]{:S(2)}) %collective-permute-start.43) | collective-permute-done | bytes 428064 | tf_op jit(solution)/shard_map/ppermute | solution.py:24
  458.7 10.2 %collective-permute-done.44 = bf16[64,3344]{1,0:T(8,128)(2,1)} collective-permute-done((bf16[64,3344]{1,0:T(8,128)(2,1)}, bf16[64,3344]{1,0:T(8,128)(2,1)}, u32[]{:S(2)}, u32[]{:S(2)}) %collective-permute-start.44) | collective-permute-done | bytes 428064 | tf_op jit(solution)/shard_map/ppermute | solution.py:24
  475.2 3.8 maximum_select_fusion.3
  481.8 2.4 fusion.3
  484.2 5.2 %fusion.5 = f32[8,256,1024]{2,1,0:T(8,128)} fusion(bf16[8,256,1024]{2,1,0:T(8,128)(2,1)S(1)} %copy-done.7, bf16[8,256,1024]{2,1,0:T(8,128)(2,1)S(1)} %copy-done.8, bf16[4,2,256,1024]{3,2,1,0:T(8,128)(2,1)S(1)} %pad_maximum_fusion.2, f32[8,256]{1,0:T(8,128)S(1)} %broadcast_multiply_fusion, f32[8,256]{1,0:T(8,128)S(1)} %get-tuple-element.217, ...), kind=kLoop, calls=%fused_computation.10 | loop fusion | flops 18874368 | bytes 21000192 | tf_op jit(solution)/shard_map/sub | solution.py:673
  (312 shorter events, 93.9 us)
Async XLA Ops:
  7.2 148.4 %all-gather.2.cloned.1.call-start = ((), (), s32[]{:S(2)}) async-start(), calls=%async_computation | async-start | bytes 4456448 | tf_op jit(solution)/shard_map/all_gather | solution.py:568
  10.3 13.0 %collective-permute-start.8 = (bf16[2,128,1024]{2,1,0:T(8,128)(2,1)}, bf16[2,128,1024]{2,1,0:T(8,128)(2,1)S(1)}, u32[]{:S(2)}, u32[]{:S(2)}) collective-permute-start(bf16[2,128,1024]{2,1,0:T(8,128)(2,1)} %get-tuple-element.192), channel_id=1, source_target_pairs={{0,2},{2,0},{4,6},{6,4},{1,3},{3,1},{5,7},{7,5},{8,10},{10,8},{12,... | collective-permute-start | bytes 1572872 | tf_op jit(solution)/shard_map/ppermute | solution.py:24
  11.5 14.1 %collective-permute-start.9 = (bf16[2,128,1024]{2,1,0:T(8,128)(2,1)}, bf16[2,128,1024]{2,1,0:T(8,128)(2,1)S(1)}, u32[]{:S(2)}, u32[]{:S(2)}) collective-permute-start(bf16[2,128,1024]{2,1,0:T(8,128)(2,1)} %get-tuple-element.191), channel_id=1, source_target_pairs={{0,4},{2,6},{4,0},{6,2},{1,5},{3,7},{5,1},{7,3},{8,12},{10,14},{12... | collective-permute-start | bytes 1572872 | tf_op jit(solution)/shard_map/ppermute | solution.py:24
  12.7 22.8 %collective-permute-start.10 = (bf16[2,128,1024]{2,1,0:T(8,128)(2,1)}, bf16[2,128,1024]{2,1,0:T(8,128)(2,1)S(1)}, u32[]{:S(2)}, u32[]{:S(2)}) collective-permute-start(bf16[2,128,1024]{2,1,0:T(8,128)(2,1)} %get-tuple-element.190), channel_id=1, source_target_pairs={{0,6},{2,4},{4,2},{6,0},{1,7},{3,5},{5,3},{7,1},{8,14},{10,12},{12... | collective-permute-start | bytes 1572872 | tf_op jit(solution)/shard_map/ppermute | solution.py:24
  12.9 25.9 %collective-permute-start.12 = (bf16[1,1,1,1,1,64]{5,4,3,2,1,0:T(2,128)(2,1)S(1)}, bf16[1,1,1,1,1,64]{5,4,3,2,1,0:T(2,128)(2,1)S(1)}, u32[]{:S(2)}, u32[]{:S(2)}) collective-permute-start(bf16[1,1,1,1,1,64]{5,4,3,2,1,0:T(2,128)(2,1)S(1)} %bitcast.309), channel_id=1, source_target_pairs={{0,16},{8,24},{16,0},{24,8},{1,17},{9,25},{17,1},{25,9},{2,18},{10... | collective-permute-start | bytes 392 | tf_op jit(solution)/shard_map/ppermute | solution.py:24
  15.8 31.1 %collective-permute-start.4 = (bf16[1,1,1,1,64,656]{5,4,0,1,3,2:T(8,128)(2,1)S(1)}, bf16[1,1,1,1,64,656]{5,4,0,1,3,2:T(8,128)(2,1)S(1)}, u32[]{:S(2)}, u32[]{:S(2)}) collective-permute-start(bf16[1,1,1,1,64,656]{5,4,0,1,3,2:T(8,128)(2,1)S(1)} %get-tuple-element.204), channel_id=1, source_target_pairs={{0,16},{8,24},{16,0},{24,8},{1,17},{9,25},{17,1},{25,9},{2,18},{10... | collective-permute-start | bytes 251912 | tf_op jit(solution)/shard_map/ppermute | solution.py:24
  23.3 23.3 %collective-permute-start = (bf16[1,1,1,1,64,640]{5,4,0,1,3,2:T(8,128)(2,1)S(1)}, bf16[1,1,1,1,64,640]{5,4,0,1,3,2:T(8,128)(2,1)S(1)}, u32[]{:S(2)}, u32[]{:S(2)}) collective-permute-start(bf16[1,1,1,1,64,640]{5,4,0,1,3,2:T(8,128)(2,1)S(1)} %get-tuple-element.208), channel_id=1, source_target_pairs={{0,16},{8,24},{16,0},{24,8},{1,17},{9,25},{17,1},{25,9},{2,18},{10... | collective-permute-start | bytes 245768 | tf_op jit(solution)/shard_map/ppermute | solution.py:24
  37.1 24.4 %collective-permute-start.11 = (bf16[4,2,128,1024]{3,2,1,0:T(8,128)(2,1)}, bf16[4,2,128,1024]{3,2,1,0:T(8,128)(2,1)}, u32[]{:S(2)}, u32[]{:S(2)}) collective-permute-start(bf16[4,2,128,1024]{3,2,1,0:T(8,128)(2,1)} %pad_maximum_fusion.4), channel_id=1, source_target_pairs={{0,1},{1,0},{2,3},{3,2},{4,5},{5,4},{6,7},{7,6},{8,9},{9,8},{10,11... | collective-permute-start | bytes 6291464 | tf_op jit(solution)/shard_map/ppermute | solution.py:24
  38.9 2.5 collective-permute-start.13
  41.4 2.5 collective-permute-start.14
  43.9 2.5 collective-permute-start.15
  46.6 4.2 collective-permute-start.1
  46.9 6.0 %collective-permute-start.5 = (bf16[2,1,1,1,64,656]{5,4,0,1,3,2:T(8,128)(2,1)S(1)}, bf16[2,1,1,1,64,656]{5,4,0,1,3,2:T(8,128)(2,1)S(1)}, u32[]{:S(2)}, u32[]{:S(2)}) collective-permute-start(bf16[2,1,1,1,64,656]{5,4,0,1,3,2:T(8,128)(2,1)S(1)} %maximum_select_fusion.12), channel_id=1, source_target_pairs={{0,8},{8,0},{16,24},{24,16},{1,9},{9,1},{17,25},{25,17},{2,10},{10... | collective-permute-start | bytes 503816 | tf_op jit(solution)/shard_map/ppermute | solution.py:24
  50.9 6.3 %collective-permute-start.2 = (bf16[2,2,1,1,64,640]{5,4,0,1,3,2:T(8,128)(2,1)S(1)}, bf16[2,2,1,1,64,640]{5,4,0,1,3,2:T(8,128)(2,1)S(1)}, u32[]{:S(2)}, u32[]{:S(2)}) collective-permute-start(bf16[2,2,1,1,64,640]{5,4,0,1,3,2:T(8,128)(2,1)S(1)} %maximum_select_fusion.10), channel_id=1, source_target_pairs={{0,4},{2,6},{4,0},{6,2},{1,5},{3,7},{5,1},{7,3},{8,12},{10,14},{12... | collective-permute-start | bytes 983048 | tf_op jit(solution)/shard_map/ppermute | solution.py:24
  53.0 7.0 %collective-permute-start.6 = (bf16[2,2,1,1,64,656]{5,4,0,1,3,2:T(8,128)(2,1)S(1)}, bf16[2,2,1,1,64,656]{5,4,0,1,3,2:T(8,128)(2,1)S(1)}, u32[]{:S(2)}, u32[]{:S(2)}) collective-permute-start(bf16[2,2,1,1,64,656]{5,4,0,1,3,2:T(8,128)(2,1)S(1)} %maximum_select_fusion.8), channel_id=1, source_target_pairs={{0,2},{2,0},{4,6},{6,4},{1,3},{3,1},{5,7},{7,5},{8,10},{10,8},{12,... | collective-permute-start | bytes 1007624 | tf_op jit(solution)/shard_map/ppermute | solution.py:24
  57.3 16.1 %collective-permute-start.3 = (bf16[2,2,2,1,64,640]{5,4,0,1,3,2:T(8,128)(2,1)S(1)}, bf16[2,2,2,1,64,640]{5,4,0,1,3,2:T(8,128)(2,1)}, u32[]{:S(2)}, u32[]{:S(2)}) collective-permute-start(bf16[2,2,2,1,64,640]{5,4,0,1,3,2:T(8,128)(2,1)S(1)} %maximum_select_fusion.7), channel_id=1, source_target_pairs={{0,2},{2,0},{4,6},{6,4},{1,3},{3,1},{5,7},{7,5},{8,10},{10,8},{12,... | collective-permute-start | bytes 1966088 | tf_op jit(solution)/shard_map/ppermute | solution.py:24
  60.2 16.4 %collective-permute-start.7 = (bf16[2,2,1,2,64,656]{5,4,0,1,3,2:T(8,128)(2,1)S(1)}, bf16[2,2,1,2,64,656]{5,4,0,1,3,2:T(8,128)(2,1)}, u32[]{:S(2)}, u32[]{:S(2)}) collective-permute-start(bf16[2,2,1,2,64,656]{5,4,0,1,3,2:T(8,128)(2,1)S(1)} %maximum_select_fusion.6), channel_id=1, source_target_pairs={{0,4},{2,6},{4,0},{6,2},{1,5},{3,7},{5,1},{7,3},{8,12},{10,14},{12... | collective-permute-start | bytes 2015240 | tf_op jit(solution)/shard_map/ppermute | solution.py:24
  82.2 52.8 %collective-permute-start.16 = (bf16[2,128,1024]{2,1,0:T(8,128)(2,1)S(1)}, bf16[2,128,1024]{2,1,0:T(8,128)(2,1)S(1)}, u32[]{:S(2)}, u32[]{:S(2)}) collective-permute-start(bf16[2,128,1024]{2,1,0:T(8,128)(2,1)S(1)} %get-tuple-element.187), channel_id=1, source_target_pairs={{0,2},{2,0},{4,6},{6,4},{1,3},{3,1},{5,7},{7,5},{8,10},{10,8},{12,... | collective-permute-start | bytes 1572872 | tf_op jit(solution)/shard_map/ppermute | solution.py:24
  83.2 51.8 %collective-permute-start.17 = (bf16[2,128,1024]{2,1,0:T(8,128)(2,1)S(1)}, bf16[2,128,1024]{2,1,0:T(8,128)(2,1)}, u32[]{:S(2)}, u32[]{:S(2)}) collective-permute-start(bf16[2,128,1024]{2,1,0:T(8,128)(2,1)S(1)} %get-tuple-element.186), channel_id=1, source_target_pairs={{0,4},{2,6},{4,0},{6,2},{1,5},{3,7},{5,1},{7,3},{8,12},{10,14},{12... | collective-permute-start | bytes 1572872 | tf_op jit(solution)/shard_map/ppermute | solution.py:24
  83.7 51.2 %collective-permute-start.18 = (bf16[2,128,1024]{2,1,0:T(8,128)(2,1)S(1)}, bf16[2,128,1024]{2,1,0:T(8,128)(2,1)}, u32[]{:S(2)}, u32[]{:S(2)}) collective-permute-start(bf16[2,128,1024]{2,1,0:T(8,128)(2,1)S(1)} %get-tuple-element.185), channel_id=1, source_target_pairs={{0,6},{2,4},{4,2},{6,0},{1,7},{3,5},{5,3},{7,1},{8,14},{10,12},{12... | collective-permute-start | bytes 1572872 | tf_op jit(solution)/shard_map/ppermute | solution.py:24
  158.3 19.4 %collective-permute-start.19 = (bf16[4,2,128,1024]{3,2,1,0:T(8,128)(2,1)}, bf16[4,2,128,1024]{3,2,1,0:T(8,128)(2,1)}, u32[]{:S(2)}, u32[]{:S(2)}) collective-permute-start(bf16[4,2,128,1024]{3,2,1,0:T(8,128)(2,1)} %pad_maximum_fusion.5), channel_id=1, source_target_pairs={{0,1},{1,0},{2,3},{3,2},{4,5},{5,4},{6,7},{7,6},{8,9},{9,8},{10,11... | collective-permute-start | bytes 6291464 | tf_op jit(solution)/shard_map/ppermute | solution.py:24
  193.1 1.2 collective-permute-start.20
  239.1 21.1 %collective-permute-start.21 = (bf16[4,2,128,1024]{3,2,1,0:T(8,128)(2,1)}, bf16[4,2,128,1024]{3,2,1,0:T(8,128)(2,1)}, u32[]{:S(2)}, u32[]{:S(2)}) collective-permute-start(bf16[4,2,128,1024]{3,2,1,0:T(8,128)(2,1)} %fusion.37), channel_id=1, source_target_pairs={{0,1},{1,0},{2,3},{3,2},{4,5},{5,4},{6,7},{7,6},{8,9},{9,8},{10,11... | collective-permute-start | bytes 6291464 | tf_op jit(solution)/shard_map/ppermute | solution.py:24
  250.1 24.5 %collective-permute-start.25 = (bf16[4,64,2048]{2,1,0:T(8,128)(2,1)S(1)}, bf16[4,64,2048]{2,1,0:T(8,128)(2,1)S(1)}, u32[]{:S(2)}, u32[]{:S(2)}) collective-permute-start(bf16[4,64,2048]{2,1,0:T(8,128)(2,1)S(1)} %get-tuple-element.171), channel_id=1, source_target_pairs={{0,2},{2,0},{4,6},{6,4},{1,3},{3,1},{5,7},{7,5},{8,10},{10,8},{12,... | collective-permute-start | bytes 3145736 | tf_op jit(solution)/shard_map/ppermute | solution.py:24
  251.3 75.7 %collective-permute-start.26 = (bf16[4,64,2048]{2,1,0:T(8,128)(2,1)}, bf16[4,64,2048]{2,1,0:T(8,128)(2,1)}, u32[]{:S(2)}, u32[]{:S(2)}) collective-permute-start(bf16[4,64,2048]{2,1,0:T(8,128)(2,1)} %get-tuple-element.170), channel_id=1, source_target_pairs={{0,4},{2,6},{4,0},{6,2},{1,5},{3,7},{5,1},{7,3},{8,12},{10,14},{12... | collective-permute-start | bytes 3145736 | tf_op jit(solution)/shard_map/ppermute | solution.py:24
  251.6 75.4 %collective-permute-start.27 = (bf16[4,64,2048]{2,1,0:T(8,128)(2,1)}, bf16[4,64,2048]{2,1,0:T(8,128)(2,1)}, u32[]{:S(2)}, u32[]{:S(2)}) collective-permute-start(bf16[4,64,2048]{2,1,0:T(8,128)(2,1)} %get-tuple-element.169), channel_id=1, source_target_pairs={{0,6},{2,4},{4,2},{6,0},{1,7},{3,5},{5,3},{7,1},{8,14},{10,12},{12... | collective-permute-start | bytes 3145736 | tf_op jit(solution)/shard_map/ppermute | solution.py:24
  264.7 62.3 %collective-permute-start.22 = (bf16[2,128,1024]{2,1,0:T(8,128)(2,1)S(1)}, bf16[2,128,1024]{2,1,0:T(8,128)(2,1)S(1)}, u32[]{:S(2)}, u32[]{:S(2)}) collective-permute-start(bf16[2,128,1024]{2,1,0:T(8,128)(2,1)S(1)} %get-tuple-element.183), channel_id=1, source_target_pairs={{0,2},{2,0},{4,6},{6,4},{1,3},{3,1},{5,7},{7,5},{8,10},{10,8},{12,... | collective-permute-start | bytes 1572872 | tf_op jit(solution)/shard_map/ppermute | solution.py:24
  265.9 61.1 %collective-permute-start.23 = (bf16[2,128,1024]{2,1,0:T(8,128)(2,1)S(1)}, bf16[2,128,1024]{2,1,0:T(8,128)(2,1)S(1)}, u32[]{:S(2)}, u32[]{:S(2)}) collective-permute-start(bf16[2,128,1024]{2,1,0:T(8,128)(2,1)S(1)} %get-tuple-element.182), channel_id=1, source_target_pairs={{0,4},{2,6},{4,0},{6,2},{1,5},{3,7},{5,1},{7,3},{8,12},{10,14},{12... | collective-permute-start | bytes 1572872 | tf_op jit(solution)/shard_map/ppermute | solution.py:24
  274.6 52.4 %collective-permute-start.24 = (bf16[2,128,1024]{2,1,0:T(8,128)(2,1)S(1)}, bf16[2,128,1024]{2,1,0:T(8,128)(2,1)S(1)}, u32[]{:S(2)}, u32[]{:S(2)}) collective-permute-start(bf16[2,128,1024]{2,1,0:T(8,128)(2,1)S(1)} %get-tuple-element.181), channel_id=1, source_target_pairs={{0,6},{2,4},{4,2},{6,0},{1,7},{3,5},{5,3},{7,1},{8,14},{10,12},{12... | collective-permute-start | bytes 1572872 | tf_op jit(solution)/shard_map/ppermute | solution.py:24
  342.4 16.7 %collective-permute-start.29 = (bf16[4,2,128,1024]{3,2,1,0:T(8,128)(2,1)}, bf16[4,2,128,1024]{3,2,1,0:T(8,128)(2,1)}, u32[]{:S(2)}, u32[]{:S(2)}) collective-permute-start(bf16[4,2,128,1024]{3,2,1,0:T(8,128)(2,1)} %add_convert_fusion.1), channel_id=1, source_target_pairs={{0,1},{1,0},{2,3},{3,2},{4,5},{5,4},{6,7},{7,6},{8,9},{9,8},{10,11... | collective-permute-start | bytes 6291464 | tf_op jit(solution)/shard_map/ppermute | solution.py:24
  354.1 17.8 %collective-permute-start.30 = (bf16[4,64,1296]{2,1,0:T(8,128)(2,1)S(1)}, bf16[4,64,1296]{2,1,0:T(8,128)(2,1)S(1)}, u32[]{:S(2)}, u32[]{:S(2)}) collective-permute-start(bf16[4,64,1296]{2,1,0:T(8,128)(2,1)S(1)} %get-tuple-element.175), channel_id=1, source_target_pairs={{0,2},{2,0},{4,6},{6,4},{1,3},{3,1},{5,7},{7,5},{8,10},{10,8},{12,... | collective-permute-start | bytes 1990664 | tf_op jit(solution)/shard_map/ppermute | solution.py:24
  355.2 17.4 %collective-permute-start.31 = (bf16[4,64,1296]{2,1,0:T(8,128)(2,1)S(1)}, bf16[4,64,1296]{2,1,0:T(8,128)(2,1)S(1)}, u32[]{:S(2)}, u32[]{:S(2)}) collective-permute-start(bf16[4,64,1296]{2,1,0:T(8,128)(2,1)S(1)} %get-tuple-element.174), channel_id=1, source_target_pairs={{0,4},{2,6},{4,0},{6,2},{1,5},{3,7},{5,1},{7,3},{8,12},{10,14},{12... | collective-permute-start | bytes 1990664 | tf_op jit(solution)/shard_map/ppermute | solution.py:24
  355.5 32.7 %collective-permute-start.32 = (bf16[4,64,1296]{2,1,0:T(8,128)(2,1)S(1)}, bf16[4,64,1296]{2,1,0:T(8,128)(2,1)S(1)}, u32[]{:S(2)}, u32[]{:S(2)}) collective-permute-start(bf16[4,64,1296]{2,1,0:T(8,128)(2,1)S(1)} %get-tuple-element.173), channel_id=1, source_target_pairs={{0,6},{2,4},{4,2},{6,0},{1,7},{3,5},{5,3},{7,1},{8,14},{10,12},{12... | collective-permute-start | bytes 1990664 | tf_op jit(solution)/shard_map/ppermute | solution.py:24
  358.3 40.3 %collective-permute-start.28 = (bf16[4,2,128,1024]{3,2,1,0:T(8,128)(2,1)}, bf16[4,2,128,1024]{3,2,1,0:T(8,128)(2,1)}, u32[]{:S(2)}, u32[]{:S(2)}) collective-permute-start(bf16[4,2,128,1024]{3,2,1,0:T(8,128)(2,1)} %pad_maximum_fusion.6), channel_id=1, source_target_pairs={{0,1},{1,0},{2,3},{3,2},{4,5},{5,4},{6,7},{7,6},{8,9},{9,8},{10,11... | collective-permute-start | bytes 6291464 | tf_op jit(solution)/shard_map/ppermute | solution.py:24
  389.1 9.2 %collective-permute-start.37 = (f32[72,128]{1,0:T(8,128)S(1)}, f32[72,128]{1,0:T(8,128)S(1)}, u32[]{:S(2)}, u32[]{:S(2)}) collective-permute-start(f32[72,128]{1,0:T(8,128)S(1)} %pad_bitcast_fusion), channel_id=1, source_target_pairs={{0,4},{2,6},{4,0},{6,2},{1,5},{3,7},{5,1},{7,3},{8,12},{10,14},{12... | collective-permute-start | bytes 110600 | tf_op jit(solution)/shard_map/ppermute | solution.py:24
  395.7 48.6 %collective-permute-start.42 = (bf16[64,3344]{1,0:T(8,128)(2,1)}, bf16[64,3344]{1,0:T(8,128)(2,1)S(1)}, u32[]{:S(2)}, u32[]{:S(2)}) collective-permute-start(bf16[64,3344]{1,0:T(8,128)(2,1)} %get-tuple-element.193), channel_id=1, source_target_pairs={{0,8},{8,0},{16,24},{24,16},{1,9},{9,1},{17,25},{25,17},{2,10},{10... | collective-permute-start | bytes 1284104 | tf_op jit(solution)/shard_map/ppermute | solution.py:24
  396.0 33.7 %collective-permute-start.34 = (bf16[2,128,1024]{2,1,0:T(8,128)(2,1)S(1)}, bf16[2,128,1024]{2,1,0:T(8,128)(2,1)S(1)}, u32[]{:S(2)}, u32[]{:S(2)}) collective-permute-start(bf16[2,128,1024]{2,1,0:T(8,128)(2,1)S(1)} %get-tuple-element.179), channel_id=1, source_target_pairs={{0,4},{2,6},{4,0},{6,2},{1,5},{3,7},{5,1},{7,3},{8,12},{10,14},{12... | collective-permute-start | bytes 1572872 | tf_op jit(solution)/shard_map/ppermute | solution.py:24
  397.1 33.4 %collective-permute-start.35 = (bf16[2,128,1024]{2,1,0:T(8,128)(2,1)S(1)}, bf16[2,128,1024]{2,1,0:T(8,128)(2,1)S(1)}, u32[]{:S(2)}, u32[]{:S(2)}) collective-permute-start(bf16[2,128,1024]{2,1,0:T(8,128)(2,1)S(1)} %get-tuple-element.178), channel_id=1, source_target_pairs={{0,6},{2,4},{4,2},{6,0},{1,7},{3,5},{5,3},{7,1},{8,14},{10,12},{12... | collective-permute-start | bytes 1572872 | tf_op jit(solution)/shard_map/ppermute | solution.py:24
  398.3 32.2 %collective-permute-start.33 = (bf16[2,128,1024]{2,1,0:T(8,128)(2,1)S(1)}, bf16[2,128,1024]{2,1,0:T(8,128)(2,1)S(1)}, u32[]{:S(2)}, u32[]{:S(2)}) collective-permute-start(bf16[2,128,1024]{2,1,0:T(8,128)(2,1)S(1)} %get-tuple-element.180), channel_id=1, source_target_pairs={{0,2},{2,0},{4,6},{6,4},{1,3},{3,1},{5,7},{7,5},{8,10},{10,8},{12,... | collective-permute-start | bytes 1572872 | tf_op jit(solution)/shard_map/ppermute | solution.py:24
  398.6 22.0 %collective-permute-start.38 = (f32[72,128]{1,0:T(8,128)S(1)}, f32[72,128]{1,0:T(8,128)S(1)}, u32[]{:S(2)}, u32[]{:S(2)}) collective-permute-start(f32[72,128]{1,0:T(8,128)S(1)} %fusion.95), channel_id=1, source_target_pairs={{0,2},{2,0},{4,6},{6,4},{1,3},{3,1},{5,7},{7,5},{8,10},{10,8},{12,... | collective-permute-start | bytes 110600 | tf_op jit(solution)/shard_map/ppermute | solution.py:24
  420.6 3.8 collective-permute-start.39
  424.4 4.1 collective-permute-start.40
  428.5 29.4 %collective-permute-start.43 = (bf16[64,3344]{1,0:T(8,128)(2,1)}, bf16[64,3344]{1,0:T(8,128)(2,1)S(1)}, u32[]{:S(2)}, u32[]{:S(2)}) collective-permute-start(bf16[64,3344]{1,0:T(8,128)(2,1)} %get-tuple-element.194), channel_id=1, source_target_pairs={{0,16},{8,24},{16,0},{24,8},{1,17},{9,25},{17,1},{25,9},{2,18},{10... | collective-permute-start | bytes 1284104 | tf_op jit(solution)/shard_map/ppermute | solution.py:24
  429.7 39.2 %collective-permute-start.44 = (bf16[64,3344]{1,0:T(8,128)(2,1)}, bf16[64,3344]{1,0:T(8,128)(2,1)}, u32[]{:S(2)}, u32[]{:S(2)}) collective-permute-start(bf16[64,3344]{1,0:T(8,128)(2,1)} %get-tuple-element.195), channel_id=1, source_target_pairs={{0,24},{8,16},{16,8},{24,0},{1,25},{9,17},{17,9},{25,1},{2,26},{10... | collective-permute-start | bytes 1284104 | tf_op jit(solution)/shard_map/ppermute | solution.py:24
  432.2 43.0 %collective-permute-start.36 = (bf16[4,2,128,1024]{3,2,1,0:T(8,128)(2,1)}, bf16[4,2,128,1024]{3,2,1,0:T(8,128)(2,1)}, u32[]{:S(2)}, u32[]{:S(2)}) collective-permute-start(bf16[4,2,128,1024]{3,2,1,0:T(8,128)(2,1)} %pad_maximum_fusion.7), channel_id=1, source_target_pairs={{0,1},{1,0},{2,3},{3,2},{4,5},{5,4},{6,7},{7,6},{8,9},{9,8},{10,11... | collective-permute-start | bytes 6291464 | tf_op jit(solution)/shard_map/ppermute | solution.py:24
  438.8 3.1 collective-permute-start.41
  441.9 1.2 collective-permute-start.46
  470.4 4.1 collective-permute-start.45
  (67 other events, 729.8 us)
Sparse Core Ops, SparseCore 0:
  67.7 87.8 all-gather.1

commit v3 on v2

--- a/solution.py
+++ b/solution.py
@@ -10,7 +10,7 @@
 EPS = 1e-05
 LOG2E = 1.4426950408889634
 LANES = 128
-GROUP = 2
+GROUP = 4
 HIGH = lax.Precision.HIGHEST
 BF = jnp.bfloat16
 F32 = jnp.float32
@@ -50,13 +50,6 @@
     return whole.reshape((-1,) + whole.shape[len(row_bits()) + 1 :])
 
 
-def gather_rows(shard, order):
-    whole = open_gather(shard)
-    for place in order:
-        whole = double(whole, place)
-    return close_gather(whole)
-
-
 def both_ways(array, cut):
     return [array[:, :cut], array[:, cut:]]
 
@@ -76,6 +69,17 @@
 
 def add_up(pieces):
     return sum(x.astype(F32) for x in pieces)
+
+
+def scatter_dp(part):
+    bits = bits_of("dp")
+    left = part.reshape((2,) * len(bits) + part.shape[1:])
+    for dim, bit in reversed(list(enumerate(bits))):
+        up = side("dp", bit)
+        mine = lax.dynamic_index_in_dim(left, up, dim)
+        theirs = lax.dynamic_index_in_dim(left, 1 - up, dim)
+        left = mine + swap(theirs.astype(BF), "dp", bit).astype(F32)
+    return left.reshape(part.shape[1:])
 
 
 def open_scatter(part):
@@ -552,22 +556,6 @@
     ways = [ctx_bits, ctx_bits[::-1]]
     tensor_bits = [("tensor", b) for b in bits_of("tensor")]
 
-    rows = spread_out(tokens, length)
-    scan_weights = jnp.concatenate(
-        [w_zx[:, 1], w_bc, jnp.pad(w_dt, ((0, 0), (0, head_pad - heads)))], 1
-    )
-    scan_weights = both_ways(scan_weights, inner_here // 2 + LANES)
-    full_scan = jnp.concatenate(
-        [gather_rows(x, dp_bits + way) for x, way in zip(scan_weights, ways)], 1
-    )
-    gain = gather_rows(norm_gain[None], dp_bits + ctx_bits).reshape(-1).astype(F32)
-    rows = gather_cuts(jnp.stack(rows))
-    rows, gain, outer, cot_ready = tie(
-        rows, gain, jnp.concatenate([w_out, w_zx[:, 0]], 1), output_gradient
-    )
-    outer = lax.all_gather(outer, ("dp", "ctx"), axis=0, tiled=True)
-    cots = spread_out(cot_ready, length)
-
     def lanes(column):
         return jnp.broadcast_to(column[..., None], column.shape + (LANES,))
 
@@ -575,6 +563,28 @@
     cbw = lanes(jnp.concatenate([conv_bc_w, conv_bc_b[None]], 0))
     hp = jnp.pad(jnp.stack([dt_bias, a_log, d_skip]), ((0, 0), (0, head_pad - heads)))
     hp = jnp.broadcast_to(hp[..., None], hp.shape + (length,))
+
+    rows = spread_out(tokens, length)
+    scan_weights = jnp.concatenate(
+        [w_zx[:, 1], w_bc, jnp.pad(w_dt, ((0, 0), (0, head_pad - heads)))], 1
+    )
+    cut = inner_here // 2 + LANES
+    scan_weights = both_ways(scan_weights, cut)
+    scan_weights[0] = jnp.concatenate([scan_weights[0], norm_gain[:, None]], 1)
+    scan_weights = [open_gather(x) for x in scan_weights]
+    for place in dp_bits:
+        scan_weights = [double(x, place) for x in scan_weights]
+    outer = jnp.concatenate([w_out, w_zx[:, 0]], 1)
+    rows, scan_weights, outer, cw, cbw, hp = tie(rows, scan_weights, outer, cw, cbw, hp)
+    outer = lax.all_gather(outer, ("dp", "ctx"), axis=0, tiled=True)
+    for places in zip(*ways):
+        scan_weights = [double(x, place) for x, place in zip(scan_weights, places)]
+    first, second = [close_gather(x) for x in scan_weights]
+    full_scan = jnp.concatenate([first[:, :cut], second], 1)
+    gain = first[:, cut].astype(F32)
+    rows = gather_cuts(jnp.stack(rows))
+    rows, cot_ready = tie(rows, output_gradient)
+    cots = spread_out(cot_ready, length)
 
     residual = rows.astype(F32)
     normed = (
@@ -623,31 +633,14 @@
     grad_scan, sum_x, sum_bc, sum_h = run_backward(
         z, inner_raw, y, grad_y, zbc, bc_raw, dt_raw, cs, mem, cw, cbw, hp, heads
     )
-    grad_scan, mixed, outer_grad = tie(grad_scan, mixed, outer_grad)
-
-    scan_grad = weight_grad(normed, grad_scan).astype(BF)
-    grad_scan, scan_grad = tie(grad_scan, scan_grad)
-    scan_grad = offer(open_scatter(scan_grad), 1, "ctx")
-    grad_share = [
-        x.astype(F32) + part for x, part in zip(normed_gate, shares(grad_scan, full_scan))
-    ]
-    grad_share = own_share(grad_share).astype(BF)
-    grad_share, scan_grad, outer_grad = tie(grad_share, scan_grad, outer_grad)
-    grad_home = send_home(grad_share)
-    weight_grads = jnp.concatenate([add_up(outer_grad), add_up(scan_grad)], -1).astype(BF)
-    weight_grads = add_up(offer(weight_grads, 0, "dp"))
-    grad_w_out, grad_w_gate = weight_grads[:, :inner_here], weight_grads[:, inner_here : 2 * inner_here]
-    scan_grad = weight_grads[:, 2 * inner_here :]
-    grad_w_inner = scan_grad[:, :inner_here]
-    grad_w_bc = sum_over(scan_grad[:, inner_here:rest], tensor_bits)
-    grad_w_dt = scan_grad[:, rest : rest + heads]
-    r = lax.rsqrt(jnp.mean(share * share, axis=-1, keepdims=True) + EPS)
-    grad_gain = jnp.sum(share * r * grad_share.astype(F32), axis=(0, 1, 2))
+    grad_scan, sum_x, sum_bc, sum_h, mixed, outer_grad = tie(
+        grad_scan, sum_x, sum_bc, sum_h, mixed, outer_grad
+    )
 
     sum_x = jnp.sum(sum_x, -1)
     sum_bc = jnp.sum(sum_bc, -1)
     sum_h = jnp.sum(sum_h, -1)[:, :heads]
-    pieces = [sum_x, grad_norm_w, sum_h, grad_gain, sum_bc]
+    pieces = [sum_x, grad_norm_w, sum_h, sum_bc]
     flat = jnp.concatenate([p.reshape(-1) for p in pieces])
     size = flat.shape[0]
     flat = jnp.pad(flat, (0, -size % 1024)).reshape(-1, LANES)
@@ -656,9 +649,29 @@
     for p in pieces:
         out.append(flat[: p.size].reshape(p.shape))
         flat = flat[p.size :]
-    sum_x, grad_norm_w, sum_h, grad_gain, sum_bc = out
-    sum_bc, grad_gain = jax.tree.map(lambda x: sum_over(x, tensor_bits), (sum_bc, grad_gain))
+    sum_x, grad_norm_w, sum_h, sum_bc = out
+    sum_bc = sum_over(sum_bc, tensor_bits)
     taps = conv_x_w.shape[0]
+
+    scan_grad = weight_grad(normed, grad_scan).astype(BF)
+    grad_scan, scan_grad = tie(grad_scan, scan_grad)
+    scan_grad = offer(open_scatter(scan_grad), 1, "ctx")
+    outer_grad = scatter_dp(add_up(outer_grad))
+    grad_share = [
+        x.astype(F32) + part for x, part in zip(normed_gate, shares(grad_scan, full_scan))
+    ]
+    grad_share = own_share(grad_share).astype(BF)
+    grad_share, scan_grad = tie(grad_share, scan_grad)
+    grad_home = send_home(grad_share)
+    scan_grad = scatter_dp(add_up(scan_grad))
+    grad_w_out, grad_w_gate = outer_grad[:, :inner_here], outer_grad[:, inner_here:]
+    grad_w_inner = scan_grad[:, :inner_here]
+    grad_w_bc = sum_over(scan_grad[:, inner_here:rest], tensor_bits)
+    grad_w_dt = scan_grad[:, rest : rest + heads]
+    r = lax.rsqrt(jnp.mean(share * share, axis=-1, keepdims=True) + EPS)
+    grad_gain = jnp.sum(share * r * grad_share.astype(F32), axis=(0, 1, 2))
+
+    grad_gain = sum_over(grad_gain.reshape(-1, LANES), tensor_bits + dp_bits + ctx_bits).reshape(-1)
     row = lax.axis_index("dp") * lax.axis_size("ctx") + lax.axis_index("ctx")
     grad_gain = lax.dynamic_slice_in_dim(
         grad_gain, row * norm_gain.shape[0], norm_gain.shape[0], 0

time: 501 us -> 459 us (0.916)
  waiting for transfers between devices: 132 us -> 102 us
  Pallas kernels: 86.4 us -> 75.8 us
  starting transfers between devices: 51.3 us -> 43.3 us
  matrix products: 94.6 us -> 88.4 us
  local copies, waits for them, and re-layouts: 47.5 us -> 53.3 us
  other arithmetic: 68.8 us -> 74.1 us
    ppermute x47 -> x48, waiting for transfers between devices: 112 us -> 91.3 us  [swap(): lax.ppermute(block, axis, [(i, i ^ mask) for i in range(lax.axis_size(axi...]
    dot_general x3, matrix products: 33 us -> 22.4 us  [weight_grad(): return jnp.einsum('ksld,ksil->di', rows, grad, preferred_element_type=F32)]
    pallas_call x2, Pallas kernels: 86.4 us -> 75.8 us  [kernel_call(): pl.pallas_call(body, grid_spec=pltpu.PrefetchScalarGridSpec(num_scalar_pr...]
    all_gather x1, waiting for transfers between devices: 20.6 us -> 10.7 us  [per_device(): outer = lax.all_gather(outer, ('dp', 'ctx'), axis=0, tiled=True)]
    ppermute x47 -> x48, starting transfers between devices: 51.3 us -> 43.2 us  [swap(): lax.ppermute(block, axis, [(i, i ^ mask) for i in range(lax.axis_size(axi...]
    select_n x13 -> x8, other arithmetic: 3.79 us -> 9.52 us  [double(): jnp.where(side(*place) == 1, jnp.concatenate([other, whole], dim), jnp.co...]
    unnamed x141 -> x90, local copies, waits for them, and re-layouts: 8.58 us -> 14.1 us
  transfers between devices with their start and end apart: 48 -> 49, of which waited for: 22 -> 19; matrix products, arithmetic and copies ran while one was open for 23% -> 29% of each run, Pallas kernels for 17% -> 17%
where the time goes in v3:
time: 459 us; the launch traced here: 452 us
  waiting for transfers between devices  102 us (22%)
  matrix products  88.4 us (19%)
  Pallas kernels  75.8 us (17%)
  other arithmetic  74.1 us (16%)
  local copies, waits for them, and re-layouts  53.3 us (12%)
  starting transfers between devices  43.3 us (9%)
  between operations  15.2 us (3%)
    ppermute x48, waiting for transfers between devices, swap(): lax.ppermute(block, axis, [(i, i ^ mask) for i in range(lax.axis_size(axi...  91.3 us
    pallas_call x2, Pallas kernels, kernel_call(): pl.pallas_call(body, grid_spec=pltpu.PrefetchScalarGridSpec(num_scalar_pr...  75.8 us
    ppermute x48, starting transfers between devices, swap(): lax.ppermute(block, axis, [(i, i ^ mask) for i in range(lax.axis_size(axi...  43.2 us
    dot_general x5, matrix products, project(): return jnp.einsum('ksld,di->ksil', rows, weight, preferred_element_type=F32)  35.2 us
    dot_general x6, matrix products, project_back(): return jnp.einsum('ksil,di->ksld', grad, weight, preferred_element_type=F32)  30.8 us
    dot_general x3, matrix products, weight_grad(): return jnp.einsum('ksld,ksil->di', rows, grad, preferred_element_type=F32)  22.4 us
    optimization_barrier x3, local copies, waits for them, and re-layouts, tie(): return jax.tree.unflatten(shape, lax.optimization_barrier(tuple(leaves)))  16.7 us
    convert_element_type x1, other arithmetic, per_device(): (grad_gated * y * gate_sig * (1.0 + gate_raw * (1.0 - gate_sig))).astype(BF)  14.9 us
  transfers between devices with their start and end apart: 49, of which 19 were waited for; matrix products, arithmetic and copies ran while one was open for 29% of the time, Pallas kernels for 17%

profile of v3, /device:TPU:9, one launch (start us, length us, event | category | flops | bytes accessed | tf_op | source)
XLA Modules:
  0.0 452.1 jit_solution(16655038568441612709)
XLA Ops:
  10.3 2.4 collective-permute-start.5
  25.4 2.2 collective-permute-done.4
  28.5 2.9 collective-permute-done.6
  31.5 10.4 %collective-permute-done.2 = bf16[2,128,1024]{2,1,0:T(8,128)(2,1)S(1)} collective-permute-done((bf16[2,128,1024]{2,1,0:T(8,128)(2,1)S(1)}, bf16[2,128,1024]{2,1,0:T(8,128)(2,1)S(1)}, u32[]{:S(2)}, u32[]{:S(2)}) %collective-permute-start.2) | collective-permute-done | bytes 524320 | tf_op jit(solution)/shard_map/ppermute | solution.py:24
  41.9 2.1 broadcast_in_dim.14.cw
  45.9 2.4 collective-permute-start.11
  49.8 9.6 %collective-permute-done.7 = bf16[2,2,1,1,64,641]{5,4,0,3,2,1:T(8,128)(2,1)} collective-permute-done((bf16[2,2,1,1,64,641]{5,4,0,3,2,1:T(8,128)(2,1)}, bf16[2,2,1,1,64,641]{5,4,0,3,2,1:T(8,128)(2,1)}, u32[]{:S(2)}, u32[]{:S(2)}) %collective-permute-start.7) | collective-permute-done | bytes 328224 | tf_op jit(solution)/shard_map/ppermute | solution.py:24
  61.9 2.1 maximum_select_fusion.7
  64.6 16.6 %collective-permute-done.8 = bf16[2,2,2,1,64,641]{5,4,0,3,2,1:T(8,128)(2,1)} collective-permute-done((bf16[2,2,2,1,64,641]{5,4,0,3,2,1:T(8,128)(2,1)S(1)}, bf16[2,2,2,1,64,641]{5,4,0,3,2,1:T(8,128)(2,1)}, u32[]{:S(2)}, u32[]{:S(2)}) %collective-permute-start.8) | collective-permute-done | bytes 656416 | tf_op jit(solution)/shard_map/ppermute | solution.py:24
  84.2 2.5 copy.139
  86.8 2.2 maximum_select_fusion.5
  90.6 4.7 %maximum_select_fusion = bf16[4,2,256,1024]{3,2,1,0:T(8,128)(2,1)S(1)} fusion(bf16[1,2,128,1024]{3,2,1,0:T(8,128)(2,1)} %bitcast.262, bf16[1,2,128,1024]{3,2,1,0:T(8,128)(2,1)} %bitcast.260, bf16[1,2,128,1024]{3,2,1,0:T(8,128)(2,1)S(1)} %bitcast.258, bf16[1,2,128,1024]{3,2,1,0:T(8,128)(2,1)S(1)} %bitcast.251, ...), kind=kLoop, calls=%fused_computation.41 | loop fusion | flops 44040192 | bytes 8388609 | tf_op jit(solution)/shard_map/jit(_where)/select_n | solution.py:114
  102.1 6.3 %convert_bitcast_fusion.raw = bf16[4,2,1024,256]{3,2,1,0:T(8,128)(2,1)} fusion(bf16[1024,656]{0,1:T(8,128)(2,1)S(1)} %copy-done.24, bf16[1024,640]{0,1:T(8,128)(2,1)S(1)} %copy-done.25, bf16[4,2,256,1024]{3,2,1,0:T(8,128)(2,1)S(1)} %maximum_select_fusion, f32[1024]{0:T(1024)S(1)} %convert_reduce_fusion, f32[4,2,256]{2,1,0:T(2,128)S(1)} %add_rsqrt_fusion.1), kind=kOutput, calls=%fused_computation.52 | convolution fusion | flops 4309647360 | bytes 11055104 | tf_op jit(solution)/shard_map/ksld,di->ksil/dot_general | solution.py:532
  108.4 30.7 %scan_forward.1 = (f32[4,2,1024,256]{3,2,1,0:T(8,128)}, f32[4,2,1024,256]{3,2,1,0:T(8,128)}, f32[4,2,16,256]{3,2,1,0:T(8,128)S(1)}, bf16[4,2,1024,128]{3,2,1,0:T(8,128)(2,1)S(1)}, f32[4,2,256,256]{3,2,1,0:T(8,128)S(1)}) custom-call(s32[1]{0:T(128)} %bitcast.me, bf16[4,2,1024,256]{3,2,1,0:T(8,128)(2,1)} %convert_bitcast_fusion.raw, ...), custom_call_target="tpu_custom_call" | custom-call | flops 48318382080 | bytes 16777216 | tf_op jit(solution)/shard_map/scan_forward/pallas_call | solution.py:474
  141.8 10.7 %all-gather.2.cloned.1.call-done = bf16[1024,2048]{1,0:T(8,128)(2,1)} async-done(((bf16[64,2048]{1,0:T(8,128)(2,1)}), bf16[1024,2048]{1,0:T(8,128)(2,1)}) %all-gather.2.cloned.1.call-update) | async-done | bytes 4194320 | tf_op jit(solution)/shard_map/all_gather | solution.py:579
  152.5 2.8 pad_maximum_fusion.5
  156.5 6.8 %copy.102 = bf16[1024,2048]{0,1:T(8,128)(2,1)} copy(bf16[1024,2048]{1,0:T(8,128)(2,1)} %all-gather.2.cloned.1.call-done) | data formatting | bytes 8388608 | tf_op jit(solution)/shard_map/optimization_barrier | solution.py:59
  163.2 10.8 %fusion.52 = f32[1024,4,2,256]{3,0,2,1:T(8,128)} fusion(bf16[1024,2048]{0,1:T(8,128)(2,1)} %copy.102, bf16[4,2,256,1024]{3,2,1,0:T(8,128)(2,1)} %copy-done.3, f32[1024]{0:T(1024)S(1)} %convert_reduce_fusion, f32[4,2,256]{2,1,0:T(2,128)S(1)} %add_rsqrt_fusion.1), kind=kOutput, calls=%fused_computation.88 | convolution fusion | flops 4303355904 | bytes 14692352 | tf_op jit(solution)/shard_map/ksld,di->ksil/dot_general | solution.py:532
  174.1 15.4 %multiply_reduce_fusion.1 = (f32[4,2,256]{2,1,0:T(2,128)S(1)}, f32[4,2,256]{2,1,0:T(2,128)S(1)}, f32[4,2,1024,256]{3,2,1,0:T(8,128)}, f32[1024,4,2,256]{3,0,2,1:T(8,128)}) fusion(f32[1024]{0:T(1024)S(1)} %copy-done.35, f32[4,2,1024,256]{3,2,1,0:T(8,128)} %get-tuple-element.82.y_in, f32[1024,4,2,256]{3,0,2,1:T(8,128)} %fusion.52, ...), kind=kOutput, calls=%fused_computation.32 | convolution fusion | flops 4359974912 | bytes 39866368 | tf_op jit(solution)/shard_map/ksld,di->ksil/dot_general | solution.py:532
  190.8 14.9 %fusion.16 = (bf16[4,2,1024,256]{3,2,1,0:T(8,128)(2,1)S(1)}, bf16[4,2,1024,256]{3,2,1,0:T(8,128)(2,1)}, f32[1024]{0:T(1024)S(1)}, bf16[4,2,1024,256]{3,2,1,0:T(8,128)(2,1)S(1)}) fusion(f32[1024,4,2,256]{3,0,2,1:T(8,128)} %fusion.52, f32[4,2,1024,256]{3,2,1,0:T(8,128)} %get-tuple-element.82.y_in, f32[4,2,256]{2,1,0:T(2,128)S(1)} %get-tuple-element.236, ...), kind=kLoop, calls=%fused_computation.27 | loop fusion | flops 50330624 | bytes 46170112 | tf_op jit(solution)/shard_map/convert_element_type | solution.py:616
  205.7 4.9 %bitcast_convert_fusion.1 = bf16[1024,1024]{0,1:T(8,128)(2,1)S(1)} fusion(bf16[4,2,1024,256]{3,2,1,0:T(8,128)(2,1)S(1)} %get-tuple-element.89, bf16[4,2,256,1024]{3,2,1,0:T(8,128)(2,1)S(1)} %copy-done.4, f32[1024]{0:T(1024)S(1)} %convert_reduce_fusion, f32[4,2,256]{2,1,0:T(2,128)S(1)} %add_rsqrt_fusion.1), kind=kOutput, calls=%fused_computation.48 | convolution fusion | flops 4304404480 | bytes 10498048 | tf_op jit(solution)/shard_map/ksld,ksil->di/dot_general | solution.py:540
  210.6 7.0 %bitcast_convert_fusion.2 = bf16[1024,1024]{0,1:T(8,128)(2,1)S(1)} fusion(bf16[4,2,1024,256]{3,2,1,0:T(8,128)(2,1)S(1)} %get-tuple-element.88, bf16[1,2,128,1024]{3,2,1,0:T(8,128)(2,1)} %bitcast.51, bf16[1,2,128,1024]{3,2,1,0:T(8,128)(2,1)} %bitcast.50, bf16[1,2,128,1024]{3,2,1,0:T(8,128)(2,1)S(1)} %bitcast.277, ...), kind=kOutput, calls=%fused_computation.49 | convolution fusion | flops 4340056064 | bytes 10485761 | tf_op jit(solution)/shard_map/ksld,ksil->di/dot_general | solution.py:540
  217.6 2.6 pad_maximum_fusion
  221.3 3.7 fusion.37
  227.3 6.7 %copy.112 = bf16[1024,2048]{1,0:T(8,128)(2,1)} copy(bf16[1024,2048]{0,1:T(8,128)(2,1)} %pad_maximum_fusion) | data formatting | bytes 8388608 | tf_op jit(solution)/shard_map/optimization_barrier | solution.py:59
  234.0 3.9 dynamic-slice_bitcast_fusion
  240.6 3.8 fusion.43
  244.3 3.7 fusion.40
  248.1 4.2 fusion.17
  253.2 9.2 %collective-permute-done.21 = bf16[4,64,2048]{2,1,0:T(8,128)(2,1)S(1)} collective-permute-done((bf16[4,64,2048]{2,1,0:T(8,128)(2,1)S(1)}, bf16[4,64,2048]{2,1,0:T(8,128)(2,1)S(1)}, u32[]{:S(2)}, u32[]{:S(2)}) %collective-permute-start.21) | collective-permute-done | bytes 1048608 | tf_op jit(solution)/shard_map/ppermute | solution.py:24
  263.3 45.1 %scan_backward.1 = (bf16[4,2,1296,256]{3,2,1,0:T(8,128)(2,1)}, f32[5,1024,128]{2,1,0:T(8,128)}, f32[5,256,128]{2,1,0:T(8,128)S(1)}, f32[3,16,128]{2,1,0:T(8,128)S(1)}) custom-call(s32[1]{0:T(128)} %bitcast.me, f32[4,2,1024,256]{3,2,1,0:T(8,128)} %get-tuple-element.78.z_in, bf16[4,2,1024,256]{3,2,1,0:T(8,128)(2,1)} %convert_bitcast_fusion.raw, ...), custom_call_target="tpu_custom_call" | custom-call | flops 64424509440 | bytes 16777216 | tf_op jit(solution)/shard_map/scan_backward/pallas_call | solution.py:474
  310.5 2.5 reduce_sum.106
  314.0 10.5 %bitcast_convert_fusion = bf16[1024,1296]{0,1:T(8,128)(2,1)} fusion(bf16[4,2,1296,256]{3,2,1,0:T(8,128)(2,1)} %get-tuple-element.106, bf16[4,2,256,1024]{3,2,1,0:T(8,128)(2,1)} %copy-done.3, f32[1024]{0:T(1024)S(1)} %convert_reduce_fusion, f32[4,2,256]{2,1,0:T(2,128)S(1)} %add_rsqrt_fusion.1), kind=kOutput, calls=%fused_computation.36 | convolution fusion | flops 5445533696 | bytes 12169216 | tf_op jit(solution)/shard_map/ksld,ksil->di/dot_general | solution.py:540
  324.5 3.3 copy.113
  327.8 8.2 %add_convert_fusion.1 = bf16[4,2,128,1024]{3,2,1,0:T(8,128)(2,1)} fusion(bf16[4,2,128,1024]{3,2,1,0:T(8,128)(2,1)} %fusion.43, bf16[1024,656]{0,1:T(8,128)(2,1)} %copy.99, bf16[1024,640]{0,1:T(8,128)(2,1)} %copy.139, bf16[4,2,1296,256]{3,2,1,0:T(8,128)(2,1)} %get-tuple-element.106, s32[]{:T(128)S(6)} %select_n.357), kind=kOutput, calls=%fused_computation.51 | convolution fusion | flops 2726363136 | bytes 9502724 | tf_op jit(solution)/shard_map/ksil,di->ksld/dot_general | solution.py:536
  336.0 2.5 collective-permute-start.25
  346.0 8.7 %collective-permute-done.45 = f32[64,128]{1,0:T(8,128)S(1)} collective-permute-done((f32[64,128]{1,0:T(8,128)S(1)}, f32[64,128]{1,0:T(8,128)S(1)}, u32[]{:S(2)}, u32[]{:S(2)}) %collective-permute-start.45) | collective-permute-done | bytes 32800 | tf_op jit(solution)/shard_map/ppermute | solution.py:24
  354.8 3.0 pad_maximum_fusion.6
  365.6 5.7 %collective-permute-done.39 = bf16[1,1,64,2048]{3,2,1,0:T(8,128)(2,1)S(1)} collective-permute-done((bf16[1,1,64,2048]{3,2,1,0:T(8,128)(2,1)S(1)}, bf16[1,1,64,2048]{3,2,1,0:T(8,128)(2,1)S(1)}, u32[]{:S(2)}, u32[]{:S(2)}) %collective-permute-start.39) | collective-permute-done | bytes 262176 | tf_op jit(solution)/shard_map/ppermute | solution.py:24
  374.3 7.2 %add_convert_fusion = bf16[4,2,128,1024]{3,2,1,0:T(8,128)(2,1)S(1)} fusion(bf16[4,2,128,1024]{3,2,1,0:T(8,128)(2,1)} %collective-permute-done.25, bf16[4,2,128,1024]{3,2,1,0:T(8,128)(2,1)} %fusion.40, bf16[1024,656]{0,1:T(8,128)(2,1)} %copy.99, bf16[1024,640]{0,1:T(8,128)(2,1)S(1)} %copy-done.26, bf16[4,2,1296,256]{3,2,1,0:T(8,128)(2,1)} %get-tuple-element.106, ...), kind=kOutput, calls=%fused_computation.50 | convolution fusion | flops 2728460288 | bytes 11599876 | tf_op jit(solution)/shard_map/ksil,di->ksld/dot_general | solution.py:536
  390.9 4.1 maximum_select_fusion.2
  397.0 2.3 collective-permute-done.35
  400.0 11.3 %collective-permute-done.31 = bf16[2,128,1024]{2,1,0:T(8,128)(2,1)S(1)} collective-permute-done((bf16[2,128,1024]{2,1,0:T(8,128)(2,1)S(1)}, bf16[2,128,1024]{2,1,0:T(8,128)(2,1)S(1)}, u32[]{:S(2)}, u32[]{:S(2)}) %collective-permute-start.31) | collective-permute-done | bytes 524320 | tf_op jit(solution)/shard_map/ppermute | solution.py:24
  414.8 2.3 pad_maximum_fusion.1
  420.2 7.0 %collective-permute-done.41 = bf16[1,1,64,1296]{3,2,1,0:T(8,128)(2,1)S(1)} collective-permute-done((bf16[1,1,64,1296]{3,2,1,0:T(8,128)(2,1)S(1)}, bf16[1,1,64,1296]{3,2,1,0:T(8,128)(2,1)S(1)}, u32[]{:S(2)}, u32[]{:S(2)}) %collective-permute-start.41) | collective-permute-done | bytes 165920 | tf_op jit(solution)/shard_map/ppermute | solution.py:24
  430.9 3.9 maximum_select_fusion.3
  437.4 2.4 fusion.3
  439.8 5.2 %fusion.5 = f32[8,256,1024]{2,1,0:T(8,128)} fusion(bf16[8,256,1024]{2,1,0:T(8,128)(2,1)S(1)} %copy-done.7, bf16[8,256,1024]{2,1,0:T(8,128)(2,1)S(1)} %copy-done.9, bf16[4,2,256,1024]{3,2,1,0:T(8,128)(2,1)S(1)} %pad_maximum_fusion.2, f32[8,256]{1,0:T(8,128)S(1)} %broadcast_multiply_fusion, f32[8,256]{1,0:T(8,128)S(1)} %get-tuple-element.238, ...), kind=kLoop, calls=%fused_computation.10 | loop fusion | flops 18874368 | bytes 21000192 | tf_op jit(solution)/shard_map/sub | solution.py:686
  (264 shorter events, 93.9 us)
Async XLA Ops:
  7.2 145.3 %all-gather.2.cloned.1.call-start = ((), (), s32[]{:S(2)}) async-start(), calls=%async_computation | async-start | bytes 4456448 | tf_op jit(solution)/shard_map/all_gather | solution.py:579
  10.3 13.6 %collective-permute-start.5 = (bf16[1,1,1,1,64,656]{5,4,0,3,2,1:T(8,128)(2,1)S(1)}, bf16[1,1,1,1,64,656]{5,4,0,3,2,1:T(8,128)(2,1)S(1)}, u32[]{:S(2)}, u32[]{:S(2)}) collective-permute-start(bf16[1,1,1,1,64,656]{5,4,0,3,2,1:T(8,128)(2,1)S(1)} %get-tuple-element.226), channel_id=1, source_target_pairs={{0,16},{8,24},{16,0},{24,8},{1,17},{9,25},{17,1},{25,9},{2,18},{10... | collective-permute-start | bytes 251912 | tf_op jit(solution)/shard_map/ppermute | solution.py:24
  14.2 7.5 %collective-permute-start.3 = (bf16[1,1,1,1,64,641]{5,4,0,3,2,1:T(8,128)(2,1)}, bf16[1,1,1,1,64,641]{5,4,0,3,2,1:T(8,128)(2,1)}, u32[]{:S(2)}, u32[]{:S(2)}) collective-permute-start(bf16[1,1,1,1,64,641]{5,4,0,3,2,1:T(8,128)(2,1)} %get-tuple-element.228), channel_id=1, source_target_pairs={{0,16},{8,24},{16,0},{24,8},{1,17},{9,25},{17,1},{25,9},{2,18},{10... | collective-permute-start | bytes 246152 | tf_op jit(solution)/shard_map/ppermute | solution.py:24
  17.2 14.2 %collective-permute-start = (bf16[2,128,1024]{2,1,0:T(8,128)(2,1)}, bf16[2,128,1024]{2,1,0:T(8,128)(2,1)S(1)}, u32[]{:S(2)}, u32[]{:S(2)}) collective-permute-start(bf16[2,128,1024]{2,1,0:T(8,128)(2,1)} %get-tuple-element.220), channel_id=1, source_target_pairs={{0,2},{2,0},{4,6},{6,4},{1,3},{3,1},{5,7},{7,5},{8,10},{10,8},{12,... | collective-permute-start | bytes 1572872 | tf_op jit(solution)/shard_map/ppermute | solution.py:24
  18.4 13.0 %collective-permute-start.1 = (bf16[2,128,1024]{2,1,0:T(8,128)(2,1)}, bf16[2,128,1024]{2,1,0:T(8,128)(2,1)S(1)}, u32[]{:S(2)}, u32[]{:S(2)}) collective-permute-start(bf16[2,128,1024]{2,1,0:T(8,128)(2,1)} %get-tuple-element.219), channel_id=1, source_target_pairs={{0,4},{2,6},{4,0},{6,2},{1,5},{3,7},{5,1},{7,3},{8,12},{10,14},{12... | collective-permute-start | bytes 1572872 | tf_op jit(solution)/shard_map/ppermute | solution.py:24
  19.7 22.2 %collective-permute-start.2 = (bf16[2,128,1024]{2,1,0:T(8,128)(2,1)S(1)}, bf16[2,128,1024]{2,1,0:T(8,128)(2,1)S(1)}, u32[]{:S(2)}, u32[]{:S(2)}) collective-permute-start(bf16[2,128,1024]{2,1,0:T(8,128)(2,1)S(1)} %get-tuple-element.218), channel_id=1, source_target_pairs={{0,6},{2,4},{4,2},{6,0},{1,7},{3,5},{5,3},{7,1},{8,14},{10,12},{12... | collective-permute-start | bytes 1572872 | tf_op jit(solution)/shard_map/ppermute | solution.py:24
  22.8 4.9 %collective-permute-start.4 = (bf16[2,1,1,1,64,641]{5,4,0,3,2,1:T(8,128)(2,1)S(1)}, bf16[2,1,1,1,64,641]{5,4,0,3,2,1:T(8,128)(2,1)S(1)}, u32[]{:S(2)}, u32[]{:S(2)}) collective-permute-start(bf16[2,1,1,1,64,641]{5,4,0,3,2,1:T(8,128)(2,1)S(1)} %maximum_select_fusion.10), channel_id=1, source_target_pairs={{0,8},{8,0},{16,24},{24,16},{1,9},{9,1},{17,25},{25,17},{2,10},{10... | collective-permute-start | bytes 492296 | tf_op jit(solution)/shard_map/ppermute | solution.py:24
  24.0 7.3 %collective-permute-start.6 = (bf16[2,1,1,1,64,656]{5,4,0,3,2,1:T(8,128)(2,1)S(1)}, bf16[2,1,1,1,64,656]{5,4,0,3,2,1:T(8,128)(2,1)S(1)}, u32[]{:S(2)}, u32[]{:S(2)}) collective-permute-start(bf16[2,1,1,1,64,656]{5,4,0,3,2,1:T(8,128)(2,1)S(1)} %maximum_select_fusion.12), channel_id=1, source_target_pairs={{0,8},{8,0},{16,24},{24,16},{1,9},{9,1},{17,25},{25,17},{2,10},{10... | collective-permute-start | bytes 503816 | tf_op jit(solution)/shard_map/ppermute | solution.py:24
  45.9 44.8 %collective-permute-start.11 = (bf16[4,2,128,1024]{3,2,1,0:T(8,128)(2,1)}, bf16[4,2,128,1024]{3,2,1,0:T(8,128)(2,1)}, u32[]{:S(2)}, u32[]{:S(2)}) collective-permute-start(bf16[4,2,128,1024]{3,2,1,0:T(8,128)(2,1)} %pad_maximum_fusion.4), channel_id=1, source_target_pairs={{0,1},{1,0},{2,3},{3,2},{4,5},{5,4},{6,7},{7,6},{8,9},{9,8},{10,11... | collective-permute-start | bytes 6291464 | tf_op jit(solution)/shard_map/ppermute | solution.py:24
  48.3 11.1 %collective-permute-start.7 = (bf16[2,2,1,1,64,641]{5,4,0,3,2,1:T(8,128)(2,1)}, bf16[2,2,1,1,64,641]{5,4,0,3,2,1:T(8,128)(2,1)}, u32[]{:S(2)}, u32[]{:S(2)}) collective-permute-start(bf16[2,2,1,1,64,641]{5,4,0,3,2,1:T(8,128)(2,1)} %maximum_select_fusion.8), channel_id=1, source_target_pairs={{0,4},{2,6},{4,0},{6,2},{1,5},{3,7},{5,1},{7,3},{8,12},{10,14},{12... | collective-permute-start | bytes 984584 | tf_op jit(solution)/shard_map/ppermute | solution.py:24
  49.5 12.4 %collective-permute-start.9 = (bf16[2,2,1,1,64,656]{5,4,0,3,2,1:T(8,128)(2,1)S(1)}, bf16[2,2,1,1,64,656]{5,4,0,3,2,1:T(8,128)(2,1)}, u32[]{:S(2)}, u32[]{:S(2)}) collective-permute-start(bf16[2,2,1,1,64,656]{5,4,0,3,2,1:T(8,128)(2,1)S(1)} %maximum_select_fusion.9), channel_id=1, source_target_pairs={{0,2},{2,0},{4,6},{6,4},{1,3},{3,1},{5,7},{7,5},{8,10},{10,8},{12,... | collective-permute-start | bytes 1007624 | tf_op jit(solution)/shard_map/ppermute | solution.py:24
  60.9 20.3 %collective-permute-start.8 = (bf16[2,2,2,1,64,641]{5,4,0,3,2,1:T(8,128)(2,1)S(1)}, bf16[2,2,2,1,64,641]{5,4,0,3,2,1:T(8,128)(2,1)}, u32[]{:S(2)}, u32[]{:S(2)}) collective-permute-start(bf16[2,2,2,1,64,641]{5,4,0,3,2,1:T(8,128)(2,1)S(1)} %maximum_select_fusion.6), channel_id=1, source_target_pairs={{0,2},{2,0},{4,6},{6,4},{1,3},{3,1},{5,7},{7,5},{8,10},{10,8},{12,... | collective-permute-start | bytes 1969160 | tf_op jit(solution)/shard_map/ppermute | solution.py:24
  64.0 22.7 %collective-permute-start.10 = (bf16[2,2,1,2,64,656]{5,4,0,3,2,1:T(8,128)(2,1)}, bf16[2,2,1,2,64,656]{5,4,0,3,2,1:T(8,128)(2,1)}, u32[]{:S(2)}, u32[]{:S(2)}) collective-permute-start(bf16[2,2,1,2,64,656]{5,4,0,3,2,1:T(8,128)(2,1)} %maximum_select_fusion.7), channel_id=1, source_target_pairs={{0,4},{2,6},{4,0},{6,2},{1,5},{3,7},{5,1},{7,3},{8,12},{10,14},{12... | collective-permute-start | bytes 2015240 | tf_op jit(solution)/shard_map/ppermute | solution.py:24
  95.7 46.1 %collective-permute-start.12 = (bf16[2,128,1024]{2,1,0:T(8,128)(2,1)S(1)}, bf16[2,128,1024]{2,1,0:T(8,128)(2,1)S(1)}, u32[]{:S(2)}, u32[]{:S(2)}) collective-permute-start(bf16[2,128,1024]{2,1,0:T(8,128)(2,1)S(1)} %get-tuple-element.216), channel_id=1, source_target_pairs={{0,2},{2,0},{4,6},{6,4},{1,3},{3,1},{5,7},{7,5},{8,10},{10,8},{12,... | collective-permute-start | bytes 1572872 | tf_op jit(solution)/shard_map/ppermute | solution.py:24
  96.5 45.2 %collective-permute-start.13 = (bf16[2,128,1024]{2,1,0:T(8,128)(2,1)S(1)}, bf16[2,128,1024]{2,1,0:T(8,128)(2,1)}, u32[]{:S(2)}, u32[]{:S(2)}) collective-permute-start(bf16[2,128,1024]{2,1,0:T(8,128)(2,1)S(1)} %get-tuple-element.215), channel_id=1, source_target_pairs={{0,4},{2,6},{4,0},{6,2},{1,5},{3,7},{5,1},{7,3},{8,12},{10,14},{12... | collective-permute-start | bytes 1572872 | tf_op jit(solution)/shard_map/ppermute | solution.py:24
  97.1 44.6 %collective-permute-start.14 = (bf16[2,128,1024]{2,1,0:T(8,128)(2,1)S(1)}, bf16[2,128,1024]{2,1,0:T(8,128)(2,1)}, u32[]{:S(2)}, u32[]{:S(2)}) collective-permute-start(bf16[2,128,1024]{2,1,0:T(8,128)(2,1)S(1)} %get-tuple-element.214), channel_id=1, source_target_pairs={{0,6},{2,4},{4,2},{6,0},{1,7},{3,5},{5,3},{7,1},{8,14},{10,12},{12... | collective-permute-start | bytes 1572872 | tf_op jit(solution)/shard_map/ppermute | solution.py:24
  155.3 18.8 %collective-permute-start.15 = (bf16[4,2,128,1024]{3,2,1,0:T(8,128)(2,1)}, bf16[4,2,128,1024]{3,2,1,0:T(8,128)(2,1)}, u32[]{:S(2)}, u32[]{:S(2)}) collective-permute-start(bf16[4,2,128,1024]{3,2,1,0:T(8,128)(2,1)} %pad_maximum_fusion.5), channel_id=1, source_target_pairs={{0,1},{1,0},{2,3},{3,2},{4,5},{5,4},{6,7},{7,6},{8,9},{9,8},{10,11... | collective-permute-start | bytes 6291464 | tf_op jit(solution)/shard_map/ppermute | solution.py:24
  225.1 23.0 %collective-permute-start.17 = (bf16[4,2,128,1024]{3,2,1,0:T(8,128)(2,1)}, bf16[4,2,128,1024]{3,2,1,0:T(8,128)(2,1)}, u32[]{:S(2)}, u32[]{:S(2)}) collective-permute-start(bf16[4,2,128,1024]{3,2,1,0:T(8,128)(2,1)} %fusion.37), channel_id=1, source_target_pairs={{0,1},{1,0},{2,3},{3,2},{4,5},{5,4},{6,7},{7,6},{8,9},{9,8},{10,11... | collective-permute-start | bytes 6291464 | tf_op jit(solution)/shard_map/ppermute | solution.py:24
  237.9 24.4 %collective-permute-start.21 = (bf16[4,64,2048]{2,1,0:T(8,128)(2,1)S(1)}, bf16[4,64,2048]{2,1,0:T(8,128)(2,1)S(1)}, u32[]{:S(2)}, u32[]{:S(2)}) collective-permute-start(bf16[4,64,2048]{2,1,0:T(8,128)(2,1)S(1)} %get-tuple-element.200), channel_id=1, source_target_pairs={{0,2},{2,0},{4,6},{6,4},{1,3},{3,1},{5,7},{7,5},{8,10},{10,8},{12,... | collective-permute-start | bytes 3145736 | tf_op jit(solution)/shard_map/ppermute | solution.py:24
  238.2 70.2 %collective-permute-start.22 = (bf16[4,64,2048]{2,1,0:T(8,128)(2,1)S(1)}, bf16[4,64,2048]{2,1,0:T(8,128)(2,1)S(1)}, u32[]{:S(2)}, u32[]{:S(2)}) collective-permute-start(bf16[4,64,2048]{2,1,0:T(8,128)(2,1)S(1)} %get-tuple-element.199), channel_id=1, source_target_pairs={{0,4},{2,6},{4,0},{6,2},{1,5},{3,7},{5,1},{7,3},{8,12},{10,14},{12... | collective-permute-start | bytes 3145736 | tf_op jit(solution)/shard_map/ppermute | solution.py:24
  238.5 69.9 %collective-permute-start.23 = (bf16[4,64,2048]{2,1,0:T(8,128)(2,1)S(1)}, bf16[4,64,2048]{2,1,0:T(8,128)(2,1)S(1)}, u32[]{:S(2)}, u32[]{:S(2)}) collective-permute-start(bf16[4,64,2048]{2,1,0:T(8,128)(2,1)S(1)} %get-tuple-element.198), channel_id=1, source_target_pairs={{0,6},{2,4},{4,2},{6,0},{1,7},{3,5},{5,3},{7,1},{8,14},{10,12},{12... | collective-permute-start | bytes 3145736 | tf_op jit(solution)/shard_map/ppermute | solution.py:24
  252.5 57.0 %collective-permute-start.18 = (bf16[2,128,1024]{2,1,0:T(8,128)(2,1)S(1)}, bf16[2,128,1024]{2,1,0:T(8,128)(2,1)}, u32[]{:S(2)}, u32[]{:S(2)}) collective-permute-start(bf16[2,128,1024]{2,1,0:T(8,128)(2,1)S(1)} %get-tuple-element.212), channel_id=1, source_target_pairs={{0,2},{2,0},{4,6},{6,4},{1,3},{3,1},{5,7},{7,5},{8,10},{10,8},{12,... | collective-permute-start | bytes 1572872 | tf_op jit(solution)/shard_map/ppermute | solution.py:24
  252.9 57.6 %collective-permute-start.19 = (bf16[2,128,1024]{2,1,0:T(8,128)(2,1)S(1)}, bf16[2,128,1024]{2,1,0:T(8,128)(2,1)}, u32[]{:S(2)}, u32[]{:S(2)}) collective-permute-start(bf16[2,128,1024]{2,1,0:T(8,128)(2,1)S(1)} %get-tuple-element.211), channel_id=1, source_target_pairs={{0,4},{2,6},{4,0},{6,2},{1,5},{3,7},{5,1},{7,3},{8,12},{10,14},{12... | collective-permute-start | bytes 1572872 | tf_op jit(solution)/shard_map/ppermute | solution.py:24
  262.4 48.1 %collective-permute-start.20 = (bf16[2,128,1024]{2,1,0:T(8,128)(2,1)S(1)}, bf16[2,128,1024]{2,1,0:T(8,128)(2,1)}, u32[]{:S(2)}, u32[]{:S(2)}) collective-permute-start(bf16[2,128,1024]{2,1,0:T(8,128)(2,1)S(1)} %get-tuple-element.210), channel_id=1, source_target_pairs={{0,6},{2,4},{4,2},{6,0},{1,7},{3,5},{5,3},{7,1},{8,14},{10,12},{12... | collective-permute-start | bytes 1572872 | tf_op jit(solution)/shard_map/ppermute | solution.py:24
  313.5 25.7 %collective-permute-start.43 = (f32[64,128]{1,0:T(8,128)S(1)}, f32[64,128]{1,0:T(8,128)S(1)}, u32[]{:S(2)}, u32[]{:S(2)}) collective-permute-start(f32[64,128]{1,0:T(8,128)S(1)} %pad_bitcast_fusion), channel_id=1, source_target_pairs={{0,4},{2,6},{4,0},{6,2},{1,5},{3,7},{5,1},{7,3},{8,12},{10,14},{12... | collective-permute-start | bytes 98312 | tf_op jit(solution)/shard_map/ppermute | solution.py:24
  336.0 38.3 %collective-permute-start.25 = (bf16[4,2,128,1024]{3,2,1,0:T(8,128)(2,1)}, bf16[4,2,128,1024]{3,2,1,0:T(8,128)(2,1)}, u32[]{:S(2)}, u32[]{:S(2)}) collective-permute-start(bf16[4,2,128,1024]{3,2,1,0:T(8,128)(2,1)} %add_convert_fusion.1), channel_id=1, source_target_pairs={{0,1},{1,0},{2,3},{3,2},{4,5},{5,4},{6,7},{7,6},{8,9},{9,8},{10,11... | collective-permute-start | bytes 6291464 | tf_op jit(solution)/shard_map/ppermute | solution.py:24
  339.2 2.8 collective-permute-start.44
  340.5 17.4 %collective-permute-start.38 = (bf16[2,1,64,2048]{3,2,1,0:T(8,128)(2,1)S(1)}, bf16[2,1,64,2048]{3,2,1,0:T(8,128)(2,1)S(1)}, u32[]{:S(2)}, u32[]{:S(2)}) collective-permute-start(bf16[2,1,64,2048]{3,2,1,0:T(8,128)(2,1)S(1)} %dynamic-slice_convert_fusion), channel_id=1, source_target_pairs={{0,8},{8,0},{16,24},{24,16},{1,9},{9,1},{17,25},{25,17},{2,10},{10... | collective-permute-start | bytes 1572872 | tf_op jit(solution)/shard_map/ppermute | solution.py:24
  342.0 12.7 %collective-permute-start.45 = (f32[64,128]{1,0:T(8,128)S(1)}, f32[64,128]{1,0:T(8,128)S(1)}, u32[]{:S(2)}, u32[]{:S(2)}) collective-permute-start(f32[64,128]{1,0:T(8,128)S(1)} %fusion.97), channel_id=1, source_target_pairs={{0,16},{8,24},{16,0},{24,8},{1,17},{9,25},{17,1},{25,9},{2,18},{10... | collective-permute-start | bytes 98312 | tf_op jit(solution)/shard_map/ppermute | solution.py:24
  344.5 37.0 %collective-permute-start.26 = (bf16[4,64,1296]{2,1,0:T(8,128)(2,1)}, bf16[4,64,1296]{2,1,0:T(8,128)(2,1)}, u32[]{:S(2)}, u32[]{:S(2)}) collective-permute-start(bf16[4,64,1296]{2,1,0:T(8,128)(2,1)} %get-tuple-element.204), channel_id=1, source_target_pairs={{0,2},{2,0},{4,6},{6,4},{1,3},{3,1},{5,7},{7,5},{8,10},{10,8},{12,... | collective-permute-start | bytes 1990664 | tf_op jit(solution)/shard_map/ppermute | solution.py:24
  345.7 35.9 %collective-permute-start.27 = (bf16[4,64,1296]{2,1,0:T(8,128)(2,1)}, bf16[4,64,1296]{2,1,0:T(8,128)(2,1)}, u32[]{:S(2)}, u32[]{:S(2)}) collective-permute-start(bf16[4,64,1296]{2,1,0:T(8,128)(2,1)} %get-tuple-element.203), channel_id=1, source_target_pairs={{0,4},{2,6},{4,0},{6,2},{1,5},{3,7},{5,1},{7,3},{8,12},{10,14},{12... | collective-permute-start | bytes 1990664 | tf_op jit(solution)/shard_map/ppermute | solution.py:24
  354.8 3.2 collective-permute-start.46
  358.1 13.3 %collective-permute-start.39 = (bf16[1,1,64,2048]{3,2,1,0:T(8,128)(2,1)S(1)}, bf16[1,1,64,2048]{3,2,1,0:T(8,128)(2,1)S(1)}, u32[]{:S(2)}, u32[]{:S(2)}) collective-permute-start(bf16[1,1,64,2048]{3,2,1,0:T(8,128)(2,1)S(1)} %dynamic-slice_convert_fusion.2), channel_id=1, source_target_pairs={{0,16},{8,24},{16,0},{24,8},{1,17},{9,25},{17,1},{25,9},{2,18},{10... | collective-permute-start | bytes 786440 | tf_op jit(solution)/shard_map/ppermute | solution.py:24
  360.6 3.2 collective-permute-start.47
  363.8 18.9 %collective-permute-start.28 = (bf16[4,64,1296]{2,1,0:T(8,128)(2,1)}, bf16[4,64,1296]{2,1,0:T(8,128)(2,1)S(1)}, u32[]{:S(2)}, u32[]{:S(2)}) collective-permute-start(bf16[4,64,1296]{2,1,0:T(8,128)(2,1)} %get-tuple-element.202), channel_id=1, source_target_pairs={{0,6},{2,4},{4,2},{6,0},{1,7},{3,5},{5,3},{7,1},{8,14},{10,12},{12... | collective-permute-start | bytes 1990664 | tf_op jit(solution)/shard_map/ppermute | solution.py:24
  372.1 17.8 %collective-permute-start.24 = (bf16[4,2,128,1024]{3,2,1,0:T(8,128)(2,1)}, bf16[4,2,128,1024]{3,2,1,0:T(8,128)(2,1)S(1)}, u32[]{:S(2)}, u32[]{:S(2)}) collective-permute-start(bf16[4,2,128,1024]{3,2,1,0:T(8,128)(2,1)} %pad_maximum_fusion.6), channel_id=1, source_target_pairs={{0,1},{1,0},{2,3},{3,2},{4,5},{5,4},{6,7},{7,6},{8,9},{9,8},{10,11... | collective-permute-start | bytes 6291464 | tf_op jit(solution)/shard_map/ppermute | solution.py:24
  383.4 4.8 %collective-permute-start.33 = (f32[8,128]{1,0:T(8,128)S(1)}, f32[8,128]{1,0:T(8,128)S(1)}, u32[]{:S(2)}, u32[]{:S(2)}) collective-permute-start(f32[8,128]{1,0:T(8,128)S(1)} %bitcast.281), channel_id=1, source_target_pairs={{0,1},{1,0},{2,3},{3,2},{4,5},{5,4},{6,7},{7,6},{8,9},{9,8},{10,11... | collective-permute-start | bytes 12296 | tf_op jit(solution)/shard_map/ppermute | solution.py:24
  386.2 32.2 %collective-permute-start.40 = (bf16[2,1,64,1296]{3,2,1,0:T(8,128)(2,1)S(1)}, bf16[2,1,64,1296]{3,2,1,0:T(8,128)(2,1)S(1)}, u32[]{:S(2)}, u32[]{:S(2)}) collective-permute-start(bf16[2,1,64,1296]{3,2,1,0:T(8,128)(2,1)S(1)} %dynamic-slice_convert_fusion.1), channel_id=1, source_target_pairs={{0,8},{8,0},{16,24},{24,16},{1,9},{9,1},{17,25},{25,17},{2,10},{10... | collective-permute-start | bytes 995336 | tf_op jit(solution)/shard_map/ppermute | solution.py:24
  387.2 12.8 %collective-permute-start.29 = (bf16[2,128,1024]{2,1,0:T(8,128)(2,1)S(1)}, bf16[2,128,1024]{2,1,0:T(8,128)(2,1)S(1)}, u32[]{:S(2)}, u32[]{:S(2)}) collective-permute-start(bf16[2,128,1024]{2,1,0:T(8,128)(2,1)S(1)} %get-tuple-element.209), channel_id=1, source_target_pairs={{0,2},{2,0},{4,6},{6,4},{1,3},{3,1},{5,7},{7,5},{8,10},{10,8},{12,... | collective-permute-start | bytes 1572872 | tf_op jit(solution)/shard_map/ppermute | solution.py:24
  387.5 12.5 %collective-permute-start.30 = (bf16[2,128,1024]{2,1,0:T(8,128)(2,1)S(1)}, bf16[2,128,1024]{2,1,0:T(8,128)(2,1)S(1)}, u32[]{:S(2)}, u32[]{:S(2)}) collective-permute-start(bf16[2,128,1024]{2,1,0:T(8,128)(2,1)S(1)} %get-tuple-element.208), channel_id=1, source_target_pairs={{0,4},{2,6},{4,0},{6,2},{1,5},{3,7},{5,1},{7,3},{8,12},{10,14},{12... | collective-permute-start | bytes 1572872 | tf_op jit(solution)/shard_map/ppermute | solution.py:24
  388.2 23.1 %collective-permute-start.31 = (bf16[2,128,1024]{2,1,0:T(8,128)(2,1)S(1)}, bf16[2,128,1024]{2,1,0:T(8,128)(2,1)S(1)}, u32[]{:S(2)}, u32[]{:S(2)}) collective-permute-start(bf16[2,128,1024]{2,1,0:T(8,128)(2,1)S(1)} %get-tuple-element.207), channel_id=1, source_target_pairs={{0,6},{2,4},{4,2},{6,0},{1,7},{3,5},{5,3},{7,1},{8,14},{10,12},{12... | collective-permute-start | bytes 1572872 | tf_op jit(solution)/shard_map/ppermute | solution.py:24
  389.9 6.7 %collective-permute-start.34 = (f32[8,128]{1,0:T(8,128)S(1)}, f32[8,128]{1,0:T(8,128)S(1)}, u32[]{:S(2)}, u32[]{:S(2)}) collective-permute-start(f32[8,128]{1,0:T(8,128)S(1)} %bitcast_add_fusion), channel_id=1, source_target_pairs={{0,16},{8,24},{16,0},{24,8},{1,17},{9,25},{17,1},{25,9},{2,18},{10... | collective-permute-start | bytes 12296 | tf_op jit(solution)/shard_map/ppermute | solution.py:24
  396.5 2.8 collective-permute-start.35
  399.3 17.8 %collective-permute-start.36 = (f32[8,128]{1,0:T(8,128)S(1)}, f32[8,128]{1,0:T(8,128)S(1)}, u32[]{:S(2)}, u32[]{:S(2)}) collective-permute-start(f32[8,128]{1,0:T(8,128)S(1)} %add.282), channel_id=1, source_target_pairs={{0,4},{2,6},{4,0},{6,2},{1,5},{3,7},{5,1},{7,3},{8,12},{10,14},{12... | collective-permute-start | bytes 12296 | tf_op jit(solution)/shard_map/ppermute | solution.py:24
  412.9 18.0 %collective-permute-start.32 = (bf16[4,2,128,1024]{3,2,1,0:T(8,128)(2,1)}, bf16[4,2,128,1024]{3,2,1,0:T(8,128)(2,1)}, u32[]{:S(2)}, u32[]{:S(2)}) collective-permute-start(bf16[4,2,128,1024]{3,2,1,0:T(8,128)(2,1)} %pad_maximum_fusion.7), channel_id=1, source_target_pairs={{0,1},{1,0},{2,3},{3,2},{4,5},{5,4},{6,7},{7,6},{8,9},{9,8},{10,11... | collective-permute-start | bytes 6291464 | tf_op jit(solution)/shard_map/ppermute | solution.py:24
  417.1 2.5 collective-permute-start.37
  418.5 8.7 %collective-permute-start.41 = (bf16[1,1,64,1296]{3,2,1,0:T(8,128)(2,1)S(1)}, bf16[1,1,64,1296]{3,2,1,0:T(8,128)(2,1)S(1)}, u32[]{:S(2)}, u32[]{:S(2)}) collective-permute-start(bf16[1,1,64,1296]{3,2,1,0:T(8,128)(2,1)S(1)} %dynamic-slice_convert_fusion.3), channel_id=1, source_target_pairs={{0,16},{8,24},{16,0},{24,8},{1,17},{9,25},{17,1},{25,9},{2,18},{10... | collective-permute-start | bytes 497672 | tf_op jit(solution)/shard_map/ppermute | solution.py:24
  427.3 3.0 collective-permute-start.42
  (43 other events, 314.0 us)
Sparse Core Ops, SparseCore 0:
  64.8 87.6 all-gather.1
